TPU v7x, 1024 devices: a whole 8x8x8 slice. The times are simulated.
1024 devices in a mesh: dom: 64 (over x, y), within: 16 (over z, core).
Axes of the slice: x: 8, y: 8, z: 8, core: 2. Of those that a mesh axis runs over, the one named last changes fastest.
Arguments:
- right_side: float32 [64, 4, 32, 64, 128], P('dom', None, 'within'), may hold values from -6 to 6
- initial: float32 [64, 4, 32, 64, 128], P('dom', None, 'within'), may hold values from -6 to 6
- block_inverse: float32 [64, 4, 4, 32, 64, 128], P('dom', None, None, 'within')
- conductivity: float32 [64, 32, 64, 128], P('dom', 'within'), may hold values from 0.5 to 2
- stencil: float32 [64, 6, 4, 4], P('dom'), may hold values from -1.5 to 1.5
- coupling_source: int32 [64, 16, 64], P('dom', 'within'), may hold values from 0 to 63, as said below
- coupling_target: int32 [64, 16, 64], P('dom', 'within'), may hold values from 0 to 3
- coupling_weight: float32 [64, 16, 64, 4, 4], P('dom', 'within'), may hold values from -3 to 3
- live_count: int32 [64, 16], P('dom', 'within'), may hold values from 1 to 64, as said below
- send_faces: int32 [64, 16, 64, 2], P('dom', 'within'), may hold values from 0 to 3, as said below
Outputs:
- smoothed: float32 [64, 4, 32, 64, 128], P('dom', None, 'within')
Inputs may be any that keep to these rules, and one draw needn't show every extreme that they name: `coupling_source`: entry e of group g at slab w comes from group (g + h + e // 2) mod 64, where 1 <= h <= 32 is fixed for each group and slab. `live_count`: for each group and slab the entries at or beyond the count are ignored; in every slab some group has all 64 entries live. `send_faces`: slots that no entry reads hold 0.
All inputs are finite; a program needn't handle non-finite values.
Results may differ from a plain program's by a relative error of at most 0.0001.
Values sent between devices are 32-bit elements; how exact they have to be, the bound alone decides.
No kernel may reach another device: no remote copies, remote signals or barrier semaphores. Data moves between devices by JAX's collectives and lax.ppermute only.
A program may use at most 32 MiB of HBM per device.

v0:
```python
import jax
import jax.numpy as jnp
from jax import lax
from jax.sharding import PartitionSpec as P

SWEEPS = 3
SLOT = 2


relax_weight = 0.8


def with_halo(block, sides, width):
    for axis, dim in sides:
        count = lax.axis_size(axis)
        forward = [(i, i + 1) for i in range(count - 1)]
        backward = [(target, source) for source, target in forward]
        low = lax.ppermute(
            lax.slice_in_dim(block, block.shape[dim] - width, None, axis=dim), axis, forward
        )
        high = lax.ppermute(lax.slice_in_dim(block, 0, width, axis=dim), axis, backward)
        block = jnp.concatenate([low, block, high], axis=dim)
    return block


def apply_block(matrix, values):
    total = jnp.zeros(values.shape, jnp.float32)
    for column in range(values.shape[1]):
        total = total + matrix[:, :, column][:, :, None, None, None] * values[:, column][:, None]
    return total


def apply_cells(matrix, values):
    total = jnp.zeros(values.shape, jnp.float32)
    for column in range(values.shape[1]):
        total = total + matrix[:, :, column] * values[:, column][:, None]
    return total


def neighbour_sum(padded, stencil):
    shifted = [
        padded[:, :, :-2, 1:-1, 1:-1],
        padded[:, :, 2:, 1:-1, 1:-1],
        padded[:, :, 1:-1, :-2, 1:-1],
        padded[:, :, 1:-1, 2:, 1:-1],
        padded[:, :, 1:-1, 1:-1, :-2],
        padded[:, :, 1:-1, 1:-1, 2:],
    ]
    total = apply_block(stencil[:, 0], shifted[0])
    for direction in range(1, 6):
        total = total + apply_block(stencil[:, direction], shifted[direction])
    return total


def per_device(
    right_side,
    initial,
    block_inverse,
    conductivity,
    stencil,
    coupling_source,
    coupling_target,
    coupling_weight,
    live_count,
    send_faces,
):
    part_count, variables, slab_cells, rows_y, rows_z = initial.shape
    face_count = 2 * part_count * slab_cells
    source_group = coupling_source[0, 0]
    target_face = coupling_target[0, 0]
    weights = coupling_weight[0, 0]
    offered = send_faces[0, 0]
    groups = offered.shape[0]
    entry_count = source_group.shape[0]
    entry_ids = jnp.arange(entry_count, dtype=jnp.int32)
    slot_ids = entry_ids % SLOT
    live = (entry_ids < live_count[0, 0]).astype(jnp.float32)
    scatter_table = (
        target_face[None, :] == jnp.arange(face_count, dtype=jnp.int32)[:, None]
    ).astype(jnp.float32) * live[None, :]
    every_table = lax.all_gather(offered, "dom", axis=0, tiled=True)
    own_group = lax.axis_index("dom")
    source_face = every_table[source_group * groups + own_group, slot_ids]
    picked = source_group * face_count + source_face
    field = initial
    for sweep_index in range(SWEEPS):
        with_planes = with_halo(field, (("within", 2),), 1)
        padded = jnp.pad(with_planes, ((0, 0), (0, 0), (0, 0), (1, 1), (1, 1)))
        load = right_side + conductivity[:, None] * neighbour_sum(padded, stencil)
        edges = jnp.stack([field[:, :, :, 0], field[:, :, :, rows_y - 1]], axis=3)
        strips = jnp.transpose(edges, (0, 2, 3, 1, 4)).reshape(face_count, variables, rows_z)
        every_strip = lax.all_gather(strips, "dom", axis=0, tiled=True)
        incoming = every_strip[picked]
        added = jnp.einsum("rab,rbz->raz", weights, incoming, precision=lax.Precision.HIGHEST)
        per_face = jnp.einsum("fr,raz->faz", scatter_table, added, precision=lax.Precision.HIGHEST)
        per_face = jnp.transpose(
            per_face.reshape(part_count, slab_cells, 2, variables, rows_z), (0, 3, 1, 2, 4)
        )
        middle = jnp.zeros((part_count, variables, slab_cells, rows_y - 2, rows_z), jnp.float32)
        interface = jnp.concatenate(
            [per_face[:, :, :, 0:1], middle, per_face[:, :, :, 1:2]], axis=3
        )
        load = load + interface
        field = (1.0 - relax_weight) * field + relax_weight * apply_cells(block_inverse, load)
    return field


def solution(mesh):
    in_specs = (
        P("dom", None, "within", None, None),
        P("dom", None, "within", None, None),
        P("dom", None, None, "within", None, None),
        P("dom", "within", None, None),
        P("dom", None, None, None),
        P("dom", "within", None),
        P("dom", "within", None),
        P("dom", "within", None, None, None),
        P("dom", "within"),
        P("dom", "within", None, None),
    )
    out_specs = P("dom", None, "within", None, None)
    return jax.shard_map(
        per_device, mesh=mesh, in_specs=in_specs, out_specs=out_specs, check_vma=False
    )
```

profile of v0, /device:TPU:1, one launch (start us, length us, event | category | flops | bytes accessed | tf_op | source)
XLA Modules:
  0.0 243.7 jit_solution(3434418202638530373)
XLA Ops:
  0.0 1.0 fusion.57
  1.0 16.1 %collective-permute-start.1 = (f32[1,4,1,64,128]{4,3,2,1,0:T(8,128)S(1)}, f32[1,4,1,64,128]{4,3,2,1,0:T(8,128)S(1)}, u32[]{:S(2)}, u32[]{:S(2)}) collective-permute-start(f32[1,4,1,64,128]{4,3,2,1,0:T(8,128)S(1)} %get-tuple-element.138), channel_id=1, source_target_pairs={{1,0},{2,1},{3,2},{4,3},{5,4},{6,5},{7,6},{8,7},{9,8},{10,9},{11,1... | collective-permute-start | bytes 393224 | tf_op jit(solution)/shard_map/ppermute | solution.py:21
  17.1 1.9 collective-permute-start
  19.0 0.8 fusion.58
  19.8 33.9 %all_gather.12 = f32[256,4,128]{2,1,0:T(4,128)S(1)} all-gather(f32[4,4,128]{2,1,0:T(4,128)S(1)} %bitcast.313), channel_id=1, replica_groups=mesh['dom'=64,'within'=16] {'dom'}, dimensions={0}, use_global_device_ids=true | all-gather | bytes 532480 | tf_op jit(solution)/shard_map/all_gather | solution.py:92
  53.7 0.8 copy.24
  54.5 39.0 %all-gather = s32[1,1,4096,2]{3,1,0,2:T(1,128)S(1)} all-gather(s32[1,1,64,2]{3,1,0,2:T(1,128)S(1)} %copy.24), channel_id=2, replica_groups=mesh['dom'=64,'within'=16] {'dom'}, dimensions={2}, use_global_device_ids=true | all-gather | bytes 33280 | tf_op jit(solution)/shard_map/all_gather | solution.py:81
  93.5 1.9 copy.25
  95.5 0.9 gather_fusion
  97.2 0.7 gather_fusion.1
  97.9 0.6 convolution_bitcast_fusion.2
  99.9 0.4 select_maximum_fusion.4
  100.7 0.8 copy-done.2
  101.5 0.7 maximum_add_fusion
  102.2 0.5 copy-done
  102.9 34.5 %all_gather.14 = f32[256,4,128]{2,1,0:T(4,128)S(1)} all-gather(f32[4,4,128]{2,1,0:T(4,128)S(1)} %bitcast.314), channel_id=1, replica_groups=mesh['dom'=64,'within'=16] {'dom'}, dimensions={0}, use_global_device_ids=true | all-gather | bytes 532480 | tf_op jit(solution)/shard_map/all_gather | solution.py:92
  137.4 0.7 gather_fusion.2
  138.0 0.6 convolution_bitcast_fusion.1
  138.8 38.1 %collective-permute-start.3 = (f32[1,4,1,64,128]{4,3,2,1,0:T(8,128)S(1)}, f32[1,4,1,64,128]{4,3,2,1,0:T(8,128)S(1)}, u32[]{:S(2)}, u32[]{:S(2)}) collective-permute-start(f32[1,4,1,64,128]{4,3,2,1,0:T(8,128)S(1)} %get-tuple-element.128), channel_id=1, source_target_pairs={{1,0},{2,1},{3,2},{4,3},{5,4},{6,5},{7,6},{8,7},{9,8},{10,9},{11,1... | collective-permute-start | bytes 393224 | tf_op jit(solution)/shard_map/ppermute | solution.py:21
  176.9 1.9 collective-permute-start.2
  178.8 1.9 collective-permute-done.2
  180.7 0.4 select_maximum_fusion.2
  181.4 0.7 maximum_add_fusion.1
  182.4 37.3 %all_gather.15 = f32[256,4,128]{2,1,0:T(4,128)S(1)} all-gather(f32[4,4,128]{2,1,0:T(4,128)S(1)} %bitcast.315), channel_id=1, replica_groups=mesh['dom'=64,'within'=16] {'dom'}, dimensions={0}, use_global_device_ids=true | all-gather | bytes 532480 | tf_op jit(solution)/shard_map/all_gather | solution.py:92
  219.7 0.7 gather_fusion.3
  220.3 0.6 convolution_bitcast_fusion
  221.1 13.5 %collective-permute-start.5 = (f32[1,4,1,64,128]{4,3,2,1,0:T(8,128)S(1)}, f32[1,4,1,64,128]{4,3,2,1,0:T(8,128)S(1)}, u32[]{:S(2)}, u32[]{:S(2)}) collective-permute-start(f32[1,4,1,64,128]{4,3,2,1,0:T(8,128)S(1)} %get-tuple-element.116), channel_id=1, source_target_pairs={{1,0},{2,1},{3,2},{4,3},{5,4},{6,5},{7,6},{8,7},{9,8},{10,9},{11,1... | collective-permute-start | bytes 393224 | tf_op jit(solution)/shard_map/ppermute | solution.py:21
  234.6 4.9 %collective-permute-start.4 = (f32[1,4,1,64,128]{4,3,2,1,0:T(8,128)S(1)}, f32[1,4,1,64,128]{4,3,2,1,0:T(8,128)S(1)}, u32[]{:S(2)}, u32[]{:S(2)}) collective-permute-start(f32[1,4,1,64,128]{4,3,2,1,0:T(8,128)S(1)} %get-tuple-element.115), channel_id=1, source_target_pairs={{0,1},{1,2},{2,3},{3,4},{4,5},{5,6},{6,7},{7,8},{8,9},{9,10},{10,1... | collective-permute-start | bytes 393224 | tf_op jit(solution)/shard_map/ppermute | solution.py:18
  239.5 0.7 collective-permute-done.5
  240.2 1.2 collective-permute-done.4
  242.1 0.7 maximum_add_fusion.2
  242.8 0.8 fusion.11
  (60 shorter events, 3.7 us)
Async XLA Ops:
  1.0 98.8 %collective-permute-start.1 = (f32[1,4,1,64,128]{4,3,2,1,0:T(8,128)S(1)}, f32[1,4,1,64,128]{4,3,2,1,0:T(8,128)S(1)}, u32[]{:S(2)}, u32[]{:S(2)}) collective-permute-start(f32[1,4,1,64,128]{4,3,2,1,0:T(8,128)S(1)} %get-tuple-element.138), channel_id=1, source_target_pairs={{1,0},{2,1},{3,2},{4,3},{5,4},{6,5},{7,6},{8,7},{9,8},{10,9},{11,1... | collective-permute-start | bytes 393224 | tf_op jit(solution)/shard_map/ppermute | solution.py:21
  17.1 82.8 %collective-permute-start = (f32[1,4,1,64,128]{4,3,2,1,0:T(8,128)S(1)}, f32[1,4,1,64,128]{4,3,2,1,0:T(8,128)S(1)}, u32[]{:S(2)}, u32[]{:S(2)}) collective-permute-start(f32[1,4,1,64,128]{4,3,2,1,0:T(8,128)S(1)} %get-tuple-element.137), channel_id=1, source_target_pairs={{0,1},{1,2},{2,3},{3,4},{4,5},{5,6},{6,7},{7,8},{8,9},{9,10},{10,1... | collective-permute-start | bytes 393224 | tf_op jit(solution)/shard_map/ppermute | solution.py:18
  93.5 2.0 copy-start.7
  93.5 2.9 %copy-start.5 = (f32[1,1,64,4,4]{2,4,3,1,0:T(4,128)S(1)}, f32[1,1,64,4,4]{2,4,3,1,0:T(4,128)}, u32[]{:S(2)}) copy-start(f32[1,1,64,4,4]{2,4,3,1,0:T(4,128)} %param.17) | copy-start | bytes 12292
  95.4 3.0 %copy-start.6 = (s32[1,1,64]{2,1,0:T(1,128)S(1)}, s32[1,1,64]{2,1,0:T(1,128)}, u32[]{:S(2)}) copy-start(s32[1,1,64]{2,1,0:T(1,128)} %param.16) | copy-start | bytes 772
  95.5 3.2 %copy-start.4 = (f32[1,6,4,4]{1,3,2,0:T(4,128)S(1)}, f32[1,6,4,4]{1,3,2,0:T(4,128)}, u32[]{:S(2)}) copy-start(f32[1,6,4,4]{1,3,2,0:T(4,128)} %param.14) | copy-start | bytes 1156
  95.5 4.4 %copy-start.1 = (f32[1,4,2,64,128]{4,3,2,1,0:T(8,128)S(1)}, f32[1,4,2,64,128]{4,3,2,1,0:T(8,128)}, u32[]{:S(2)}) copy-start(f32[1,4,2,64,128]{4,3,2,1,0:T(8,128)} %param.11) | copy-start | bytes 786436
  100.5 1.0 copy-start.2
  100.5 0.9 copy-start.3
  101.5 1.2 copy-start
  138.8 40.1 %collective-permute-start.3 = (f32[1,4,1,64,128]{4,3,2,1,0:T(8,128)S(1)}, f32[1,4,1,64,128]{4,3,2,1,0:T(8,128)S(1)}, u32[]{:S(2)}, u32[]{:S(2)}) collective-permute-start(f32[1,4,1,64,128]{4,3,2,1,0:T(8,128)S(1)} %get-tuple-element.128), channel_id=1, source_target_pairs={{1,0},{2,1},{3,2},{4,3},{5,4},{6,5},{7,6},{8,7},{9,8},{10,9},{11,1... | collective-permute-start | bytes 393224 | tf_op jit(solution)/shard_map/ppermute | solution.py:21
  176.9 3.9 %collective-permute-start.2 = (f32[1,4,1,64,128]{4,3,2,1,0:T(8,128)S(1)}, f32[1,4,1,64,128]{4,3,2,1,0:T(8,128)S(1)}, u32[]{:S(2)}, u32[]{:S(2)}) collective-permute-start(f32[1,4,1,64,128]{4,3,2,1,0:T(8,128)S(1)} %get-tuple-element.127), channel_id=1, source_target_pairs={{0,1},{1,2},{2,3},{3,4},{4,5},{5,6},{6,7},{7,8},{8,9},{9,10},{10,1... | collective-permute-start | bytes 393224 | tf_op jit(solution)/shard_map/ppermute | solution.py:18
  221.1 19.1 %collective-permute-start.5 = (f32[1,4,1,64,128]{4,3,2,1,0:T(8,128)S(1)}, f32[1,4,1,64,128]{4,3,2,1,0:T(8,128)S(1)}, u32[]{:S(2)}, u32[]{:S(2)}) collective-permute-start(f32[1,4,1,64,128]{4,3,2,1,0:T(8,128)S(1)} %get-tuple-element.116), channel_id=1, source_target_pairs={{1,0},{2,1},{3,2},{4,3},{5,4},{6,5},{7,6},{8,7},{9,8},{10,9},{11,1... | collective-permute-start | bytes 393224 | tf_op jit(solution)/shard_map/ppermute | solution.py:21
  234.6 6.8 %collective-permute-start.4 = (f32[1,4,1,64,128]{4,3,2,1,0:T(8,128)S(1)}, f32[1,4,1,64,128]{4,3,2,1,0:T(8,128)S(1)}, u32[]{:S(2)}, u32[]{:S(2)}) collective-permute-start(f32[1,4,1,64,128]{4,3,2,1,0:T(8,128)S(1)} %get-tuple-element.115), channel_id=1, source_target_pairs={{0,1},{1,2},{2,3},{3,4},{4,5},{5,6},{6,7},{7,8},{8,9},{9,10},{10,1... | collective-permute-start | bytes 393224 | tf_op jit(solution)/shard_map/ppermute | solution.py:18
where the time goes:
time: 244 us
  blocking collectives  145 us (59%)
  starting transfers between devices  76.3 us (31%)
  local copies, waits for them, and re-layouts  11 us (5%)
  other arithmetic  4.43 us (2%)
  waiting for transfers between devices  3.82 us (2%)
    all_gather x3, blocking collectives, per_device(): every_strip = lax.all_gather(strips, 'dom', axis=0, tiled=True)  106 us
    ppermute x3, starting transfers between devices, with_halo(): lax.ppermute(lax.slice_in_dim(block, 0, width, axis=dim), axis, backward)  67.6 us
    all_gather x1, blocking collectives, per_device(): every_table = lax.all_gather(offered, 'dom', axis=0, tiled=True)  39 us
    ppermute x3, starting transfers between devices, with_halo(): lax.ppermute(lax.slice_in_dim(block, block.shape[dim] - width, None, axis...  8.74 us
  transfers between devices with their start and end apart: 6, of which 3 were waited for; matrix products, arithmetic and copies ran while one was open for 3% of the time, Pallas kernels for 0%

commit v1 on v0

v1 whole, which is shorter than its diff:
```python
import functools

import jax
import jax.numpy as jnp
from jax import lax
from jax.experimental import pallas as pl
from jax.experimental.pallas import tpu as pltpu
from jax.sharding import PartitionSpec as P

SWEEPS = 3
V = 4
CX = 2
FACES = 4
SLOT = 2

relax_weight = 0.8

VMEM = pl.BlockSpec(memory_space=pltpu.VMEM)
SMEM = pl.BlockSpec(memory_space=pltpu.SMEM)
PARAMS = pltpu.CompilerParams(vmem_limit_bytes=24 * 1024 * 1024)


def face_place(face, rows):
    return face // 2, (rows - 1) * (face % 2)


def fill_send(faces_ref, strips_ref, send_ref):
    for group in range(send_ref.shape[0]):
        for slot in range(SLOT):
            face = faces_ref[group * SLOT + slot]
            send_ref[group, slot * V : (slot + 1) * V, :] = strips_ref[face]


def first_kernel(faces_ref, field_ref, send_ref, strips):
    rows = field_ref.shape[2]
    for face in range(FACES):
        plane, row = face_place(face, rows)
        for var in range(V):
            strips[face, var : var + 1, :] = field_ref[var, plane, row : row + 1, :]
    fill_send(faces_ref, strips, send_ref)


def first_send(faces, field):
    groups = faces.shape[0] // SLOT
    z = field.shape[-1]
    return pl.pallas_call(
        first_kernel,
        out_shape=jax.ShapeDtypeStruct((groups, SLOT * V, z), jnp.float32),
        in_specs=[SMEM, VMEM],
        out_specs=VMEM,
        scratch_shapes=[pltpu.VMEM((FACES, V, z), jnp.float32)],
        compiler_params=PARAMS,
        cost_estimate=pl.CostEstimate(flops=0, bytes_accessed=512 * 1024, transcendentals=0),
    )(faces, field)


def local_kernel(
    first,
    stencil_ref,
    plane0_ref,
    plane1_ref,
    low_ref,
    high_ref,
    right_ref,
    conductivity_ref,
    inverse_ref,
    next0_ref,
    next1_ref,
    strips_ref,
    *maybe_edge,
):
    rows, lanes = plane0_ref.shape[1:]
    row_ids = lax.broadcasted_iota(jnp.int32, (rows, lanes), 0)
    lane_ids = lax.broadcasted_iota(jnp.int32, (rows, lanes), 1)
    around = (low_ref, plane0_ref, plane1_ref, high_ref)
    outs = (next0_ref, next1_ref)
    for plane in range(CX):
        below, here, above = around[plane : plane + 3]
        sums = [jnp.zeros((rows, lanes), jnp.float32) for _ in range(V)]
        for col in range(V):
            value = here[col]
            shifted = (
                below[col],
                above[col],
                jnp.where(row_ids == 0, 0.0, pltpu.roll(value, 1, 0)),
                jnp.where(row_ids == rows - 1, 0.0, pltpu.roll(value, rows - 1, 0)),
                jnp.where(lane_ids == 0, 0.0, pltpu.roll(value, 1, 1)),
                jnp.where(lane_ids == lanes - 1, 0.0, pltpu.roll(value, lanes - 1, 1)),
            )
            for direction in range(6):
                for var in range(V):
                    coef = stencil_ref[(direction * V + var) * V + col]
                    sums[var] = sums[var] + coef * shifted[direction]
        cond = conductivity_ref[plane]
        loads = [right_ref[var, plane] + cond * sums[var] for var in range(V)]
        for var in range(V):
            total = inverse_ref[var, 0, plane] * loads[0]
            for col in range(1, V):
                total = total + inverse_ref[var, col, plane] * loads[col]
            outs[plane][var] = (1.0 - relax_weight) * here[var] + relax_weight * total
    for face in range(FACES):
        plane, row = face_place(face, rows)
        for var in range(V):
            at = face * V + var
            strips_ref[at : at + 1, :] = outs[plane][var, row : row + 1, :]
            if first:
                for col in range(V):
                    maybe_edge[0][col, at : at + 1, :] = (
                        relax_weight * inverse_ref[var, col, plane, row : row + 1, :]
                    )


def local_part(first, stencil, plane0, plane1, low, high, right, conductivity, inverse):
    shape = jax.ShapeDtypeStruct(plane0.shape, jnp.float32)
    z = plane0.shape[-1]
    out_shape = [shape, shape, jax.ShapeDtypeStruct((FACES * V, z), jnp.float32)]
    if first:
        out_shape.append(jax.ShapeDtypeStruct((V, FACES * V, z), jnp.float32))
    return pl.pallas_call(
        functools.partial(local_kernel, first),
        out_shape=out_shape,
        in_specs=[SMEM] + [VMEM] * 7,
        out_specs=[VMEM] * len(out_shape),
        compiler_params=PARAMS,
        cost_estimate=pl.CostEstimate(
            flops=4_000_000, bytes_accessed=2 * 1024 * 1024, transcendentals=0
        ),
    )(stencil, plane0, plane1, low, high, right, conductivity, inverse)


def new_strips(start_ref, matrix_ref, edge_ref, strips_ref, got_ref):
    groups = got_ref.shape[0]
    hops = matrix_ref.shape[1] // (SLOT * V)
    start = start_ref[0]
    values = jnp.concatenate(
        [got_ref[lax.rem(start + hop, groups)] for hop in range(hops)], axis=0
    )
    added = jnp.dot(
        matrix_ref[...],
        values,
        precision=lax.Precision.HIGHEST,
        preferred_element_type=jnp.float32,
    )
    total = strips_ref[...]
    count = FACES * V
    for col in range(V):
        total = total + edge_ref[col] * added[col * count : (col + 1) * count]
    return total


def strip_kernel(
    start_ref, faces_ref, matrix_ref, edge_ref, strips_ref, got_ref, send_ref, new_ref, scratch
):
    total = new_strips(start_ref, matrix_ref, edge_ref, strips_ref, got_ref)
    new_ref[...] = total
    for face in range(FACES):
        scratch[face] = total[face * V : (face + 1) * V]
    fill_send(faces_ref, scratch, send_ref)


def strip_part(start, faces, matrix, edge, strips, got):
    return pl.pallas_call(
        strip_kernel,
        out_shape=[
            jax.ShapeDtypeStruct(got.shape, jnp.float32),
            jax.ShapeDtypeStruct(strips.shape, jnp.float32),
        ],
        in_specs=[SMEM, SMEM, VMEM, VMEM, VMEM, VMEM],
        out_specs=[VMEM, VMEM],
        scratch_shapes=[pltpu.VMEM((FACES, V, strips.shape[-1]), jnp.float32)],
        compiler_params=PARAMS,
        cost_estimate=pl.CostEstimate(flops=0, bytes_accessed=512 * 1024, transcendentals=0),
    )(start, faces, matrix, edge, strips, got)


def patch_kernel(new_ref, old0_ref, old1_ref, plane0_ref, plane1_ref):
    rows = plane0_ref.shape[1]
    plane0_ref[...] = old0_ref[...]
    plane1_ref[...] = old1_ref[...]
    outs = (plane0_ref, plane1_ref)
    for face in range(FACES):
        plane, row = face_place(face, rows)
        for var in range(V):
            at = face * V + var
            outs[plane][var, row : row + 1, :] = new_ref[at : at + 1, :]


def patch_part(new, plane0, plane1):
    shape = jax.ShapeDtypeStruct(plane0.shape, jnp.float32)
    return pl.pallas_call(
        patch_kernel,
        out_shape=[shape, shape],
        in_specs=[VMEM] * 3,
        out_specs=[VMEM] * 2,
        compiler_params=PARAMS,
        cost_estimate=pl.CostEstimate(flops=0, bytes_accessed=512 * 1024, transcendentals=0),
    )(new, plane0, plane1)


def last_kernel(
    start_ref, matrix_ref, edge_ref, strips_ref, got_ref, plane0_ref, plane1_ref, out_ref
):
    rows = plane0_ref.shape[1]
    for var in range(V):
        out_ref[var, 0] = plane0_ref[var]
        out_ref[var, 1] = plane1_ref[var]
    total = new_strips(start_ref, matrix_ref, edge_ref, strips_ref, got_ref)
    for face in range(FACES):
        plane, row = face_place(face, rows)
        for var in range(V):
            at = face * V + var
            out_ref[var, plane, row : row + 1, :] = total[at : at + 1]


def last_part(start, matrix, edge, strips, got, plane0, plane1):
    return pl.pallas_call(
        last_kernel,
        out_shape=jax.ShapeDtypeStruct((V, CX) + plane0.shape[1:], jnp.float32),
        in_specs=[SMEM] + [VMEM] * 6,
        out_specs=VMEM,
        compiler_params=PARAMS,
        cost_estimate=pl.CostEstimate(flops=0, bytes_accessed=512 * 1024, transcendentals=0),
    )(start, matrix, edge, strips, got, plane0, plane1)


def per_device(
    right_side,
    initial,
    block_inverse,
    conductivity,
    stencil,
    coupling_source,
    coupling_target,
    coupling_weight,
    live_count,
    send_faces,
):
    field = initial[0]
    right = right_side[0]
    inverse = block_inverse[0]
    cond = conductivity[0]
    coefs = stencil[0].reshape(-1)
    start = coupling_source[0, 0, 0:1]
    targets = coupling_target[0, 0]
    weights = coupling_weight[0, 0]
    faces = send_faces[0, 0].reshape(-1)
    entries = targets.shape[0]

    send = first_send(faces, field)

    live = jnp.arange(entries, dtype=jnp.int32) < live_count[0, 0]
    face_ids = jnp.arange(FACES, dtype=jnp.int32)
    chosen = (targets[None, :] == face_ids[:, None]) & live[None, :]
    by_col = jnp.transpose(weights, (1, 0, 2))
    matrix = jnp.where(chosen[None, :, None, :, None], by_col[:, None, None], 0.0)
    matrix = jnp.broadcast_to(matrix, (V, FACES, V, entries, V))
    matrix = matrix.reshape(V * FACES * V, entries * V)

    count = lax.axis_size("within")
    forward = [(i, i + 1) for i in range(count - 1)]
    backward = [(i + 1, i) for i in range(count - 1)]

    plane0, plane1 = field[:, 0], field[:, 1]
    edge = None
    for sweep in range(SWEEPS):
        got = lax.all_to_all(send, "dom", 0, 0, tiled=True)
        high = lax.ppermute(plane0, "within", backward)
        low = lax.ppermute(plane1, "within", forward)
        results = local_part(
            sweep == 0, coefs, plane0, plane1, low, high, right, cond, inverse
        )
        next0, next1, strips = results[:3]
        if sweep == 0:
            edge = results[3]
        if sweep < SWEEPS - 1:
            send, new = strip_part(start, faces, matrix, edge, strips, got)
            plane0, plane1 = patch_part(new, next0, next1)
        else:
            out = last_part(start, matrix, edge, strips, got, next0, next1)
    return out[None]


def solution(mesh):
    in_specs = (
        P("dom", None, "within", None, None),
        P("dom", None, "within", None, None),
        P("dom", None, None, "within", None, None),
        P("dom", "within", None, None),
        P("dom", None, None, None),
        P("dom", "within", None),
        P("dom", "within", None),
        P("dom", "within", None, None, None),
        P("dom", "within"),
        P("dom", "within", None, None),
    )
    out_specs = P("dom", None, "within", None, None)
    return jax.shard_map(
        per_device, mesh=mesh, in_specs=in_specs, out_specs=out_specs, check_vma=False
    )
```

time: 244 us -> 91 us (0.37)
  the two profiles are of different devices: /device:TPU:1 before, /device:TPU:385 now
where the time goes in v1:
time: 91 us; the launch traced here: 90.4 us
  starting transfers between devices  53.4 us (59%)
  waiting for transfers between devices  17.3 us (19%)
  Pallas kernels  9.28 us (10%)
  local copies, waits for them, and re-layouts  8.76 us (10%)
    all_to_all x3, starting transfers between devices, per_device(): got = lax.all_to_all(send, 'dom', 0, 0, tiled=True)  32.8 us
    ppermute x3, starting transfers between devices, per_device(): low = lax.ppermute(plane1, 'within', forward)  14.4 us
    ppermute x3, waiting for transfers between devices, per_device(): high = lax.ppermute(plane0, 'within', backward)  10.8 us
    all_to_all x3, waiting for transfers between devices, per_device(): got = lax.all_to_all(send, 'dom', 0, 0, tiled=True)  6.55 us
    ppermute x3, starting transfers between devices, per_device(): high = lax.ppermute(plane0, 'within', backward)  6.11 us
    pallas_call x3, Pallas kernels, local_part(): pl.pallas_call(functools.partial(local_kernel, first), out_shape=out_shap...  3.59 us
    pallas_call x2, Pallas kernels, strip_part(): pl.pallas_call(strip_kernel, out_shape=[jax.ShapeDtypeStruct(got.shape, j...  3.28 us
    reshape x1, local copies, waits for them, and re-layouts, per_device(): matrix = matrix.reshape(V * FACES * V, entries * V)  3.27 us
  transfers between devices with their start and end apart: 9, of which 4 were waited for; matrix products, arithmetic and copies ran while one was open for 8% of the time, Pallas kernels for 6%

profile of v1, /device:TPU:385, one launch (start us, length us, event | category | flops | bytes accessed | tf_op | source)
XLA Modules:
  0.0 90.4 jit_solution(16959063646312932202)
XLA Ops:
  0.0 1.0 %slice_bitcast_fusion = (f32[4,64,128]{2,1,0:T(8,128)S(1)}, f32[4,64,128]{2,1,0:T(8,128)S(1)}) fusion(f32[4,2,64,128]{3,2,1,0:T(8,128)} %bitcast.27), kind=kLoop, calls=%fused_computation.1 | loop fusion | bytes 524288 | tf_op jit(solution)/shard_map/squeeze | solution.py:263
  1.0 6.7 %collective-permute-start = (f32[4,64,128]{2,1,0:T(8,128)S(1)}, f32[4,64,128]{2,1,0:T(8,128)S(1)}, u32[]{:S(2)}, u32[]{:S(2)}) collective-permute-start(f32[4,64,128]{2,1,0:T(8,128)S(1)} %get-tuple-element.41.plane1_ref), channel_id=1, source_target_pairs={{0,1},{1,2},{2,3},{3,4},{4,5},{5,6},{6,7},{7,8},{8,9},{9,10},{10,1... | collective-permute-start | bytes 393224 | tf_op jit(solution)/shard_map/ppermute | solution.py:268
  7.7 1.9 %collective-permute-start.1 = (f32[4,64,128]{2,1,0:T(8,128)S(1)}, f32[4,64,128]{2,1,0:T(8,128)S(1)}, u32[]{:S(2)}, u32[]{:S(2)}) collective-permute-start(f32[4,64,128]{2,1,0:T(8,128)S(1)} %get-tuple-element.42.plane0_ref), channel_id=1, source_target_pairs={{1,0},{2,1},{3,2},{4,3},{5,4},{6,5},{7,6},{8,7},{9,8},{10,9},{11,1... | collective-permute-start | bytes 393224 | tf_op jit(solution)/shard_map/ppermute | solution.py:267
  9.6 0.8 copy.16
  10.4 0.1 reshape_squeeze.7.faces_ref
  10.5 0.9 %copy-done.2 = f32[1,4,2,64,128]{4,3,2,1,0:T(8,128)S(1)} copy-done((f32[1,4,2,64,128]{4,3,2,1,0:T(8,128)S(1)}, f32[1,4,2,64,128]{4,3,2,1,0:T(8,128)}, u32[]{:S(2)}) %copy-start.2) | copy-done | bytes 262168
  11.5 1.3 %shard_map.101 = f32[64,8,128]{2,1,0:T(8,128)} custom-call(s32[128]{0:T(128)S(1)} %reshape_squeeze.7.faces_ref, f32[4,2,64,128]{3,2,1,0:T(8,128)S(1)} %bitcast.28), custom_call_target="tpu_custom_call" | custom-call | bytes 524288 | tf_op jit(solution)/shard_map/pallas_call | solution.py:46
  12.8 13.2 %all-to-all-start = ((f32[64,8,128]{2,1,0:T(8,128)}), f32[64,8,128]{2,1,0:T(8,128)S(1)}, u32[]{:S(2)}, u32[]{:S(2)}) async-start(f32[64,8,128]{2,1,0:T(8,128)} %shard_map.101), calls=%async_computation | async-start | bytes 524288 | tf_op jit(solution)/shard_map/all_to_all | solution.py:266
  26.7 0.8 copy.14
  27.5 0.7 fusion
  28.2 0.1 broadcast_select_fusion
  28.3 0.0 copy-start.1
  28.3 1.6 %broadcast_in_dim.35 = f32[4,4,4,64,4]{4,3,2,1,0:T(8,128)} broadcast(f32[4,4,64,4]{3,2,1,0:T(8,128)S(1)} %broadcast_select_fusion), dimensions={0,1,3,4} | broadcast | bytes 81920 | tf_op jit(solution)/shard_map/broadcast_in_dim | solution.py:256
  30.0 3.3 %reshape.54.matrix_ref = f32[64,256]{1,0:T(8,128)S(1)} reshape(f32[4,4,4,64,4]{4,3,2,1,0:T(8,128)} %broadcast_in_dim.35) | data formatting | bytes 131072 | tf_op jit(solution)/shard_map/reshape | solution.py:257
  33.2 0.1 copy.15
  33.3 0.1 reshape_squeeze.6.stencil_ref
  33.5 1.2 %shard_map.100 = (f32[4,64,128]{2,1,0:T(8,128)S(1)}, f32[4,64,128]{2,1,0:T(8,128)S(1)}, f32[16,128]{1,0:T(8,128)S(1)}, f32[4,16,128]{2,1,0:T(8,128)S(1)}) custom-call(f32[96]{0:T(128)S(1)} %reshape_squeeze.6.stencil_ref, f32[4,64,128]{2,1,0:T(8,128)S(1)} %get-tuple-element.42.plane0_ref, f32[4,64,128]{2,1,0:T(8,128)S(1)} %get-tuple-element.41.plane1_ref, ...), custom_call_target="tpu_custom_call" | custom-call | flops 4000000 | bytes 2097152 | tf_op jit(solution)/shard_map/pallas_call | solution.py:119
  34.7 5.0 %all-to-all-done.got_ref = f32[64,8,128]{2,1,0:T(8,128)S(1)} async-done(((f32[64,8,128]{2,1,0:T(8,128)}), f32[64,8,128]{2,1,0:T(8,128)S(1)}, u32[]{:S(2)}, u32[]{:S(2)}) %all-to-all-start) | async-done | bytes 262176 | tf_op jit(solution)/shard_map/all_to_all | solution.py:266
  39.7 1.6 %shard_map.102 = (f32[64,8,128]{2,1,0:T(8,128)}, f32[16,128]{1,0:T(8,128)S(1)}) custom-call(s32[1]{0:T(128)S(1)} %bitcast.32, s32[128]{0:T(128)S(1)} %reshape_squeeze.7.faces_ref, f32[64,256]{1,0:T(8,128)S(1)} %reshape.54.matrix_ref, f32[4,16,128]{2,1,0:T(8,128)S(1)} %get-tuple-element.23.edge_ref, f32[16,128]{1,0:T(8,128)S(1)} %get-tuple-element.24.strips_ref, ...), custom_call_target="tpu_custom_call" | custom-call | bytes 524288 | tf_op jit(solution)/shard_map/pallas_call | solution.py:162
  41.3 7.2 %all-to-all-start.1 = ((f32[64,8,128]{2,1,0:T(8,128)}), f32[64,8,128]{2,1,0:T(8,128)S(1)}, u32[]{:S(2)}, u32[]{:S(2)}) async-start(f32[64,8,128]{2,1,0:T(8,128)} %get-tuple-element.31), calls=%async_computation.1 | async-start | bytes 524288 | tf_op jit(solution)/shard_map/all_to_all | solution.py:266
  48.6 5.7 %collective-permute-start.2 = (f32[4,64,128]{2,1,0:T(8,128)S(1)}, f32[4,64,128]{2,1,0:T(8,128)S(1)}, u32[]{:S(2)}, u32[]{:S(2)}) collective-permute-start(f32[4,64,128]{2,1,0:T(8,128)S(1)} %get-tuple-element.29.plane1_ref), channel_id=1, source_target_pairs={{0,1},{1,2},{2,3},{3,4},{4,5},{5,6},{6,7},{7,8},{8,9},{9,10},{10,1... | collective-permute-start | bytes 393224 | tf_op jit(solution)/shard_map/ppermute | solution.py:268
  54.3 1.9 %collective-permute-start.3 = (f32[4,64,128]{2,1,0:T(8,128)S(1)}, f32[4,64,128]{2,1,0:T(8,128)S(1)}, u32[]{:S(2)}, u32[]{:S(2)}) collective-permute-start(f32[4,64,128]{2,1,0:T(8,128)S(1)} %get-tuple-element.28.plane0_ref), channel_id=1, source_target_pairs={{1,0},{2,1},{3,2},{4,3},{5,4},{6,5},{7,6},{8,7},{9,8},{10,9},{11,1... | collective-permute-start | bytes 393224 | tf_op jit(solution)/shard_map/ppermute | solution.py:267
  56.2 5.6 %collective-permute-done.3.high_ref = f32[4,64,128]{2,1,0:T(8,128)S(1)} collective-permute-done((f32[4,64,128]{2,1,0:T(8,128)S(1)}, f32[4,64,128]{2,1,0:T(8,128)S(1)}, u32[]{:S(2)}, u32[]{:S(2)}) %collective-permute-start.3) | collective-permute-done | bytes 131104 | tf_op jit(solution)/shard_map/ppermute | solution.py:267
  61.8 1.2 %shard_map.104 = (f32[4,64,128]{2,1,0:T(8,128)S(1)}, f32[4,64,128]{2,1,0:T(8,128)S(1)}, f32[16,128]{1,0:T(8,128)S(1)}) custom-call(f32[96]{0:T(128)S(1)} %reshape_squeeze.6.stencil_ref, f32[4,64,128]{2,1,0:T(8,128)S(1)} %get-tuple-element.28.plane0_ref, f32[4,64,128]{2,1,0:T(8,128)S(1)} %get-tuple-element.29.plane1_ref, ...), custom_call_target="tpu_custom_call" | custom-call | flops 4000000 | bytes 2097152 | tf_op jit(solution)/shard_map/pallas_call | solution.py:119
  63.0 1.6 %shard_map.105 = (f32[64,8,128]{2,1,0:T(8,128)}, f32[16,128]{1,0:T(8,128)S(1)}) custom-call(s32[1]{0:T(128)S(1)} %bitcast.33, s32[128]{0:T(128)S(1)} %reshape_squeeze.7.faces_ref, f32[64,256]{1,0:T(8,128)S(1)} %reshape.54.matrix_ref, f32[4,16,128]{2,1,0:T(8,128)S(1)} %get-tuple-element.23.edge_ref, f32[16,128]{1,0:T(8,128)S(1)} %get-tuple-element.30.strips_ref, ...), custom_call_target="tpu_custom_call" | custom-call | bytes 524288 | tf_op jit(solution)/shard_map/pallas_call | solution.py:162
  64.6 12.4 %all-to-all-start.2 = ((f32[64,8,128]{2,1,0:T(8,128)}), f32[64,8,128]{2,1,0:T(8,128)S(1)}, u32[]{:S(2)}, u32[]{:S(2)}) async-start(f32[64,8,128]{2,1,0:T(8,128)} %get-tuple-element.38), calls=%async_computation.2 | async-start | bytes 524288 | tf_op jit(solution)/shard_map/all_to_all | solution.py:266
  77.1 2.1 %collective-permute-start.4 = (f32[4,64,128]{2,1,0:T(8,128)S(1)}, f32[4,64,128]{2,1,0:T(8,128)S(1)}, u32[]{:S(2)}, u32[]{:S(2)}) collective-permute-start(f32[4,64,128]{2,1,0:T(8,128)S(1)} %get-tuple-element.36.plane1_ref), channel_id=1, source_target_pairs={{0,1},{1,2},{2,3},{3,4},{4,5},{5,6},{6,7},{7,8},{8,9},{9,10},{10,1... | collective-permute-start | bytes 393224 | tf_op jit(solution)/shard_map/ppermute | solution.py:268
  79.1 2.3 %collective-permute-start.5 = (f32[4,64,128]{2,1,0:T(8,128)S(1)}, f32[4,64,128]{2,1,0:T(8,128)S(1)}, u32[]{:S(2)}, u32[]{:S(2)}) collective-permute-start(f32[4,64,128]{2,1,0:T(8,128)S(1)} %get-tuple-element.35.plane0_ref), channel_id=1, source_target_pairs={{1,0},{2,1},{3,2},{4,3},{5,4},{6,5},{7,6},{8,7},{9,8},{10,9},{11,1... | collective-permute-start | bytes 393224 | tf_op jit(solution)/shard_map/ppermute | solution.py:267
  81.4 5.2 %collective-permute-done.5.high_ref = f32[4,64,128]{2,1,0:T(8,128)S(1)} collective-permute-done((f32[4,64,128]{2,1,0:T(8,128)S(1)}, f32[4,64,128]{2,1,0:T(8,128)S(1)}, u32[]{:S(2)}, u32[]{:S(2)}) %collective-permute-start.5) | collective-permute-done | bytes 131104 | tf_op jit(solution)/shard_map/ppermute | solution.py:267
  86.6 1.2 %shard_map.107 = (f32[4,64,128]{2,1,0:T(8,128)S(1)}, f32[4,64,128]{2,1,0:T(8,128)S(1)}, f32[16,128]{1,0:T(8,128)S(1)}) custom-call(f32[96]{0:T(128)S(1)} %reshape_squeeze.6.stencil_ref, f32[4,64,128]{2,1,0:T(8,128)S(1)} %get-tuple-element.35.plane0_ref, f32[4,64,128]{2,1,0:T(8,128)S(1)} %get-tuple-element.36.plane1_ref, ...), custom_call_target="tpu_custom_call" | custom-call | flops 4000000 | bytes 2097152 | tf_op jit(solution)/shard_map/pallas_call | solution.py:119
  87.8 1.6 %all-to-all-done.2.got_ref = f32[64,8,128]{2,1,0:T(8,128)S(1)} async-done(((f32[64,8,128]{2,1,0:T(8,128)}), f32[64,8,128]{2,1,0:T(8,128)S(1)}, u32[]{:S(2)}, u32[]{:S(2)}) %all-to-all-start.2) | async-done | bytes 262176 | tf_op jit(solution)/shard_map/all_to_all | solution.py:266
  89.4 1.0 %shard_map.108 = f32[4,2,64,128]{3,2,1,0:T(8,128)} custom-call(s32[1]{0:T(128)S(1)} %bitcast.34, f32[64,256]{1,0:T(8,128)S(1)} %reshape.54.matrix_ref, f32[4,16,128]{2,1,0:T(8,128)S(1)} %get-tuple-element.23.edge_ref, f32[16,128]{1,0:T(8,128)S(1)} %get-tuple-element.37.strips_ref, f32[64,8,128]{2,1,0:T(8,128)S(1)} %all-to-all-done.2.got_ref, ...), custom_call_target="tpu_custom_call" | custom-call | bytes 524288 | tf_op jit(solution)/shard_map/pallas_call | solution.py:216
  (18 shorter events, 0.1 us)
Async XLA Ops:
  1.0 32.5 %collective-permute-start = (f32[4,64,128]{2,1,0:T(8,128)S(1)}, f32[4,64,128]{2,1,0:T(8,128)S(1)}, u32[]{:S(2)}, u32[]{:S(2)}) collective-permute-start(f32[4,64,128]{2,1,0:T(8,128)S(1)} %get-tuple-element.41.plane1_ref), channel_id=1, source_target_pairs={{0,1},{1,2},{2,3},{3,4},{4,5},{5,6},{6,7},{7,8},{8,9},{9,10},{10,1... | collective-permute-start | bytes 393224 | tf_op jit(solution)/shard_map/ppermute | solution.py:268
  7.7 25.8 %collective-permute-start.1 = (f32[4,64,128]{2,1,0:T(8,128)S(1)}, f32[4,64,128]{2,1,0:T(8,128)S(1)}, u32[]{:S(2)}, u32[]{:S(2)}) collective-permute-start(f32[4,64,128]{2,1,0:T(8,128)S(1)} %get-tuple-element.42.plane0_ref), channel_id=1, source_target_pairs={{1,0},{2,1},{3,2},{4,3},{5,4},{6,5},{7,6},{8,7},{9,8},{10,9},{11,1... | collective-permute-start | bytes 393224 | tf_op jit(solution)/shard_map/ppermute | solution.py:267
  10.5 1.0 %copy-start.2 = (f32[1,4,2,64,128]{4,3,2,1,0:T(8,128)S(1)}, f32[1,4,2,64,128]{4,3,2,1,0:T(8,128)}, u32[]{:S(2)}) copy-start(f32[1,4,2,64,128]{4,3,2,1,0:T(8,128)} %param.11) | copy-start | bytes 786436
  12.8 26.9 %all-to-all-start = ((f32[64,8,128]{2,1,0:T(8,128)}), f32[64,8,128]{2,1,0:T(8,128)S(1)}, u32[]{:S(2)}, u32[]{:S(2)}) async-start(f32[64,8,128]{2,1,0:T(8,128)} %shard_map.101), calls=%async_computation | async-start | bytes 524288 | tf_op jit(solution)/shard_map/all_to_all | solution.py:266
  28.3 4.9 %copy-start.5 = (f32[1,6,4,4]{1,3,2,0:T(4,128)S(1)}, f32[1,6,4,4]{1,3,2,0:T(4,128)}, u32[]{:S(2)}) copy-start(f32[1,6,4,4]{1,3,2,0:T(4,128)} %param.14) | copy-start | bytes 1156
  28.3 5.2 %copy-start = (f32[1,4,4,2,64,128]{5,4,3,2,1,0:T(8,128)S(1)}, f32[1,4,4,2,64,128]{5,4,3,2,1,0:T(8,128)}, u32[]{:S(2)}) copy-start(f32[1,4,4,2,64,128]{5,4,3,2,1,0:T(8,128)} %param.12) | copy-start | bytes 3145732
  28.3 5.2 %copy-start.1 = (f32[1,4,2,64,128]{4,3,2,1,0:T(8,128)S(1)}, f32[1,4,2,64,128]{4,3,2,1,0:T(8,128)}, u32[]{:S(2)}) copy-start(f32[1,4,2,64,128]{4,3,2,1,0:T(8,128)} %param.10) | copy-start | bytes 786436
  28.3 5.2 %copy-start.3 = (f32[1,2,64,128]{3,2,1,0:T(8,128)S(1)}, f32[1,2,64,128]{3,2,1,0:T(8,128)}, u32[]{:S(2)}) copy-start(f32[1,2,64,128]{3,2,1,0:T(8,128)} %param.13) | copy-start | bytes 196612
  30.0 9.7 %copy-start.4 = (s32[1,1,64]{2,1,0:T(1,128)S(1)}, s32[1,1,64]{2,1,0:T(1,128)}, u32[]{:S(2)}) copy-start(s32[1,1,64]{2,1,0:T(1,128)} %param.15) | copy-start | bytes 772
  41.3 21.6 %all-to-all-start.1 = ((f32[64,8,128]{2,1,0:T(8,128)}), f32[64,8,128]{2,1,0:T(8,128)S(1)}, u32[]{:S(2)}, u32[]{:S(2)}) async-start(f32[64,8,128]{2,1,0:T(8,128)} %get-tuple-element.31), calls=%async_computation.1 | async-start | bytes 524288 | tf_op jit(solution)/shard_map/all_to_all | solution.py:266
  48.6 7.6 %collective-permute-start.2 = (f32[4,64,128]{2,1,0:T(8,128)S(1)}, f32[4,64,128]{2,1,0:T(8,128)S(1)}, u32[]{:S(2)}, u32[]{:S(2)}) collective-permute-start(f32[4,64,128]{2,1,0:T(8,128)S(1)} %get-tuple-element.29.plane1_ref), channel_id=1, source_target_pairs={{0,1},{1,2},{2,3},{3,4},{4,5},{5,6},{6,7},{7,8},{8,9},{9,10},{10,1... | collective-permute-start | bytes 393224 | tf_op jit(solution)/shard_map/ppermute | solution.py:268
  54.3 7.5 %collective-permute-start.3 = (f32[4,64,128]{2,1,0:T(8,128)S(1)}, f32[4,64,128]{2,1,0:T(8,128)S(1)}, u32[]{:S(2)}, u32[]{:S(2)}) collective-permute-start(f32[4,64,128]{2,1,0:T(8,128)S(1)} %get-tuple-element.28.plane0_ref), channel_id=1, source_target_pairs={{1,0},{2,1},{3,2},{4,3},{5,4},{6,5},{7,6},{8,7},{9,8},{10,9},{11,1... | collective-permute-start | bytes 393224 | tf_op jit(solution)/shard_map/ppermute | solution.py:267
  64.6 24.8 %all-to-all-start.2 = ((f32[64,8,128]{2,1,0:T(8,128)}), f32[64,8,128]{2,1,0:T(8,128)S(1)}, u32[]{:S(2)}, u32[]{:S(2)}) async-start(f32[64,8,128]{2,1,0:T(8,128)} %get-tuple-element.38), calls=%async_computation.2 | async-start | bytes 524288 | tf_op jit(solution)/shard_map/all_to_all | solution.py:266
  77.1 4.3 %collective-permute-start.4 = (f32[4,64,128]{2,1,0:T(8,128)S(1)}, f32[4,64,128]{2,1,0:T(8,128)S(1)}, u32[]{:S(2)}, u32[]{:S(2)}) collective-permute-start(f32[4,64,128]{2,1,0:T(8,128)S(1)} %get-tuple-element.36.plane1_ref), channel_id=1, source_target_pairs={{0,1},{1,2},{2,3},{3,4},{4,5},{5,6},{6,7},{7,8},{8,9},{9,10},{10,1... | collective-permute-start | bytes 393224 | tf_op jit(solution)/shard_map/ppermute | solution.py:268
  79.1 7.5 %collective-permute-start.5 = (f32[4,64,128]{2,1,0:T(8,128)S(1)}, f32[4,64,128]{2,1,0:T(8,128)S(1)}, u32[]{:S(2)}, u32[]{:S(2)}) collective-permute-start(f32[4,64,128]{2,1,0:T(8,128)S(1)} %get-tuple-element.35.plane0_ref), channel_id=1, source_target_pairs={{1,0},{2,1},{3,2},{4,3},{5,4},{6,5},{7,6},{8,7},{9,8},{10,9},{11,1... | collective-permute-start | bytes 393224 | tf_op jit(solution)/shard_map/ppermute | solution.py:267

commit v2 on v0

v2 whole, which is shorter than its diff:
```python
import functools

import jax
import jax.numpy as jnp
from jax import lax
from jax.experimental import pallas as pl
from jax.experimental.pallas import tpu as pltpu
from jax.sharding import PartitionSpec as P

SWEEPS = 3
V = 4
CX = 2
FACES = 4
SLOT = 2
ROWS = FACES * V

relax_weight = 0.8

VMEM = pl.BlockSpec(memory_space=pltpu.VMEM)
SMEM = pl.BlockSpec(memory_space=pltpu.SMEM)
PARAMS = pltpu.CompilerParams(vmem_limit_bytes=24 * 1024 * 1024)


def call(kernel, out_shape, in_specs, args, scratch=(), flops=0, moved=512 * 1024):
    single = not isinstance(out_shape, list)
    return pl.pallas_call(
        kernel,
        out_shape=out_shape,
        in_specs=in_specs,
        out_specs=VMEM if single else [VMEM] * len(out_shape),
        scratch_shapes=list(scratch),
        compiler_params=PARAMS,
        cost_estimate=pl.CostEstimate(flops=flops, bytes_accessed=moved, transcendentals=0),
    )(*args)


def f32(*shape):
    return jax.ShapeDtypeStruct(shape, jnp.float32)


def inner_plane():
    return 1 - lax.rem(lax.axis_index("within"), 2)


def edge_rows(rows):
    return (0, rows - 1)


def first_kernel(faces_ref, field_ref, send_ref, strips_ref, scratch):
    rows = field_ref.shape[2]
    for plane in range(CX):
        for side, row in enumerate(edge_rows(rows)):
            for var in range(V):
                value = field_ref[var, plane, row : row + 1, :]
                scratch[plane * 2 + side, var : var + 1, :] = value
                at = side * V + var
                strips_ref[plane, at : at + 1, :] = value
    for group in range(send_ref.shape[0]):
        for slot in range(SLOT):
            send_ref[group, slot * V : (slot + 1) * V, :] = scratch[faces_ref[slot, group]]


def first_part(faces, field):
    groups, z = faces.shape[1], field.shape[-1]
    return call(
        first_kernel,
        [f32(groups, SLOT * V, z), f32(CX, 2 * V, z)],
        [SMEM, VMEM],
        (faces, field),
        scratch=[pltpu.VMEM((FACES, V, z), jnp.float32)],
    )


def split_kernel(strips_ref, field_ref, inner_ref, outer_ref):
    rows = inner_ref.shape[1]
    at = inner_plane()
    for ref, plane in ((inner_ref, at), (outer_ref, 1 - at)):
        for var in range(V):
            ref[var] = field_ref[var, plane]
        for side, row in enumerate(edge_rows(rows)):
            for var in range(V):
                here = side * V + var
                ref[var, row : row + 1, :] = strips_ref[plane, here : here + 1, :]


def split_part(strips, field):
    shape = f32(V, field.shape[2], field.shape[3])
    return call(split_kernel, [shape, shape], [VMEM] * 2, (strips, field))


def patch_kernel(strips_ref, old_inner_ref, old_outer_ref, inner_ref, outer_ref):
    rows = inner_ref.shape[1]
    at = inner_plane()
    for ref, old, plane in (
        (inner_ref, old_inner_ref, at),
        (outer_ref, old_outer_ref, 1 - at),
    ):
        ref[...] = old[...]
        for side, row in enumerate(edge_rows(rows)):
            for var in range(V):
                here = side * V + var
                ref[var, row : row + 1, :] = strips_ref[plane, here : here + 1, :]


def patch_part(strips, inner, outer):
    shape = f32(*inner.shape)
    return call(patch_kernel, [shape, shape], [VMEM] * 3, (strips, inner, outer))


def setup_kernel(
    source_ref, live_ref, faces_ref, target_ref, weight_ref, matrix_ref, mask_ref
):
    entries = target_ref.shape[1]
    groups = mask_ref.shape[0]
    columns = matrix_ref.shape[1]
    row_ids = lax.broadcasted_iota(jnp.int32, (ROWS, entries), 0)
    entry_ids = lax.broadcasted_iota(jnp.int32, (ROWS, entries), 1)
    chosen = (row_ids // V == target_ref[...]) & (entry_ids < live_ref[0, 0])
    place = lax.broadcasted_iota(jnp.int32, (entries, columns), 0) + SLOT * source_ref[0, 0]
    place = jnp.where(place >= SLOT * groups, place - SLOT * groups, place)
    column_ids = lax.broadcasted_iota(jnp.int32, (entries, columns), 1)
    matrix = jnp.zeros((V * ROWS, columns), jnp.float32)
    for col in range(V):
        spread = jnp.concatenate(
            [jnp.where(chosen, weight_ref[var, col : col + 1, :], 0.0) for var in range(V)],
            axis=0,
        )
        order = (column_ids == place * V + col).astype(jnp.float32)
        matrix = matrix + jnp.dot(
            spread,
            order,
            precision=lax.Precision.HIGHEST,
            preferred_element_type=jnp.float32,
        )
    high = matrix.astype(jnp.bfloat16)
    matrix_ref[: V * ROWS, :] = high
    matrix_ref[V * ROWS :, :] = (matrix - high.astype(jnp.float32)).astype(jnp.bfloat16)
    tile_rows = lax.broadcasted_iota(jnp.int32, mask_ref.shape[1:], 0)
    for group in range(groups):
        mask_ref[group] = jnp.where(tile_rows < V, faces_ref[0, group], faces_ref[1, group])


def setup_part(source, live, faces, target, weight, z):
    groups = faces.shape[1]
    return call(
        setup_kernel,
        [
            jax.ShapeDtypeStruct((2 * V * ROWS, groups * SLOT * V), jnp.bfloat16),
            jax.ShapeDtypeStruct((groups, SLOT * V, z), jnp.int32),
        ],
        [SMEM, SMEM, SMEM, VMEM, VMEM],
        (source, live, faces, target, weight),
    )


def local_kernel(
    first,
    stencil_ref,
    inner_ref,
    outer_ref,
    from_core_ref,
    from_chip_ref,
    right_ref,
    conductivity_ref,
    inverse_ref,
    next_inner_ref,
    next_outer_ref,
    strips_ref,
    *maybe_edge,
):
    rows, lanes = inner_ref.shape[1:]
    row_ids = lax.broadcasted_iota(jnp.int32, (rows, lanes), 0)
    lane_ids = lax.broadcasted_iota(jnp.int32, (rows, lanes), 1)
    at = inner_plane()
    for here, beside, outside, plane, out_ref in (
        (inner_ref, outer_ref, from_core_ref, at, next_inner_ref),
        (outer_ref, inner_ref, from_chip_ref, 1 - at, next_outer_ref),
    ):
        directions = (plane, 1 - plane, 2, 3, 4, 5)
        sums = [jnp.zeros((rows, lanes), jnp.float32) for _ in range(V)]
        for col in range(V):
            value = here[col]
            shifted = (
                outside[col],
                beside[col],
                jnp.where(row_ids == 0, 0.0, pltpu.roll(value, 1, 0)),
                jnp.where(row_ids == rows - 1, 0.0, pltpu.roll(value, rows - 1, 0)),
                jnp.where(lane_ids == 0, 0.0, pltpu.roll(value, 1, 1)),
                jnp.where(lane_ids == lanes - 1, 0.0, pltpu.roll(value, lanes - 1, 1)),
            )
            for direction, moved in zip(directions, shifted):
                for var in range(V):
                    sums[var] = sums[var] + stencil_ref[var, col, direction] * moved
        cond = conductivity_ref[plane]
        loads = [right_ref[var, plane] + cond * sums[var] for var in range(V)]
        for var in range(V):
            total = inverse_ref[var, 0, plane] * loads[0]
            for col in range(1, V):
                total = total + inverse_ref[var, col, plane] * loads[col]
            out_ref[var] = (1.0 - relax_weight) * here[var] + relax_weight * total
        for side, row in enumerate(edge_rows(rows)):
            for var in range(V):
                to = side * V + var
                strips_ref[plane, to : to + 1, :] = out_ref[var, row : row + 1, :]
                if first:
                    for col in range(V):
                        maybe_edge[0][col, plane, to : to + 1, :] = (
                            relax_weight * inverse_ref[var, col, plane, row : row + 1, :]
                        )


def local_part(first, stencil, inner, outer, from_core, from_chip, right, cond, inverse):
    z = inner.shape[-1]
    out_shape = [f32(*inner.shape), f32(*inner.shape), f32(CX, 2 * V, z)]
    if first:
        out_shape.append(f32(V, CX, 2 * V, z))
    return call(
        functools.partial(local_kernel, first),
        out_shape,
        [SMEM] + [VMEM] * 7,
        (stencil, inner, outer, from_core, from_chip, right, cond, inverse),
        flops=4_000_000,
        moved=2 * 1024 * 1024,
    )


def new_strips(matrix_ref, edge_ref, strips_ref, got_ref):
    groups, block, z = got_ref.shape
    values = got_ref[...].reshape(groups * block, z)
    high = values.astype(jnp.bfloat16)
    low = (values - high.astype(jnp.float32)).astype(jnp.bfloat16)
    count = V * ROWS
    both = jnp.dot(matrix_ref[...], high, preferred_element_type=jnp.float32)
    rest = jnp.dot(matrix_ref[:count, :], low, preferred_element_type=jnp.float32)
    added = both[:count] + (both[count:] + rest)
    tiles = []
    for plane in range(CX):
        total = strips_ref[plane]
        for col in range(V):
            begin = col * ROWS + plane * 2 * V
            total = total + edge_ref[col, plane] * added[begin : begin + 2 * V]
        tiles.append(total)
    return tiles


def strip_kernel(matrix_ref, edge_ref, strips_ref, got_ref, mask_ref, send_ref, new_ref):
    tiles = new_strips(matrix_ref, edge_ref, strips_ref, got_ref)
    upper = lax.broadcasted_iota(jnp.int32, tiles[0].shape, 0) < V
    faces = []
    for plane, tile in enumerate(tiles):
        new_ref[plane] = tile
        other = pltpu.roll(tile, V, 0)
        faces += [jnp.where(upper, tile, other), jnp.where(upper, other, tile)]
    for group in range(send_ref.shape[0]):
        mask = mask_ref[group]
        value = faces[FACES - 1]
        for face in range(FACES - 1):
            value = jnp.where(mask == face, faces[face], value)
        send_ref[group] = value


def strip_part(matrix, edge, strips, got, mask):
    return call(
        strip_kernel,
        [f32(*got.shape), f32(*strips.shape)],
        [VMEM] * 5,
        (matrix, edge, strips, got, mask),
    )


def last_kernel(matrix_ref, edge_ref, strips_ref, got_ref, inner_ref, outer_ref, out_ref):
    rows = inner_ref.shape[1]
    at = inner_plane()
    for ref, plane in ((inner_ref, at), (outer_ref, 1 - at)):
        for var in range(V):
            out_ref[var, plane] = ref[var]
    tiles = new_strips(matrix_ref, edge_ref, strips_ref, got_ref)
    for plane, tile in enumerate(tiles):
        for side, row in enumerate(edge_rows(rows)):
            for var in range(V):
                here = side * V + var
                out_ref[var, plane, row : row + 1, :] = tile[here : here + 1]


def last_part(matrix, edge, strips, got, inner, outer):
    return call(
        last_kernel,
        f32(V, CX, *inner.shape[1:]),
        [VMEM] * 6,
        (matrix, edge, strips, got, inner, outer),
    )


def per_device(
    right_side,
    initial,
    block_inverse,
    conductivity,
    stencil,
    coupling_source,
    coupling_target,
    coupling_weight,
    live_count,
    send_faces,
):
    field = initial[0]
    right = right_side[0]
    inverse = block_inverse[0]
    cond = conductivity[0]
    coefs = jnp.transpose(stencil[0], (1, 2, 0))
    weight = jnp.transpose(coupling_weight[0, 0], (1, 2, 0))
    faces = jnp.transpose(send_faces[0, 0], (1, 0))

    count = lax.axis_size("within")
    core_swap = [(i, i ^ 1) for i in range(count)]
    chip_swap = [(i, i + 1) for i in range(1, count - 1, 2)]
    chip_swap += [(j, i) for i, j in chip_swap]

    send, strips = first_part(faces, field)
    inner, outer = split_part(strips, field)
    matrix, mask = setup_part(
        coupling_source[0], live_count, faces, coupling_target[0], weight, field.shape[-1]
    )
    edge = None
    for sweep in range(SWEEPS):
        got = lax.all_to_all(send, "dom", 0, 0, tiled=True)
        from_chip = lax.ppermute(outer, "within", chip_swap)
        from_core = lax.ppermute(inner, "within", core_swap)
        results = local_part(
            sweep == 0, coefs, inner, outer, from_core, from_chip, right, cond, inverse
        )
        inner, outer, strips = results[:3]
        if sweep == 0:
            edge = results[3]
        if sweep < SWEEPS - 1:
            send, new = strip_part(matrix, edge, strips, got, mask)
            inner, outer = patch_part(new, inner, outer)
        else:
            out = last_part(matrix, edge, strips, got, inner, outer)
    return out[None]


def solution(mesh):
    in_specs = (
        P("dom", None, "within", None, None),
        P("dom", None, "within", None, None),
        P("dom", None, None, "within", None, None),
        P("dom", "within", None, None),
        P("dom", None, None, None),
        P("dom", "within", None),
        P("dom", "within", None),
        P("dom", "within", None, None, None),
        P("dom", "within"),
        P("dom", "within", None, None),
    )
    out_specs = P("dom", None, "within", None, None)
    return jax.shard_map(
        per_device, mesh=mesh, in_specs=in_specs, out_specs=out_specs, check_vma=False
    )
```

time: 244 us -> 85.9 us (0.35)
  the two profiles are of different devices: /device:TPU:1 before, /device:TPU:385 now
where the time goes in v2:
time: 85.9 us; the launch traced here: 85.2 us
  starting transfers between devices  58.5 us (68%)
  waiting for transfers between devices  11.3 us (13%)
  Pallas kernels  9.38 us (11%)
  local copies, waits for them, and re-layouts  5.13 us (6%)
  between operations  0.86 us (1%)
    all_to_all x3, starting transfers between devices, per_device(): got = lax.all_to_all(send, 'dom', 0, 0, tiled=True)  35.4 us
    ppermute x3, starting transfers between devices, per_device(): from_chip = lax.ppermute(outer, 'within', chip_swap)  16.3 us
    pallas_call x11, Pallas kernels, call(): pl.pallas_call(kernel, out_shape=out_shape, in_specs=in_specs, out_specs=...  9.38 us
    ppermute x3, starting transfers between devices, per_device(): from_core = lax.ppermute(inner, 'within', core_swap)  6.84 us
    ppermute x3, waiting for transfers between devices, per_device(): from_chip = lax.ppermute(outer, 'within', chip_swap)  6.25 us
    unnamed x26, local copies, waits for them, and re-layouts  5.13 us
    all_to_all x3, waiting for transfers between devices, per_device(): got = lax.all_to_all(send, 'dom', 0, 0, tiled=True)  5.06 us
  transfers between devices with their start and end apart: 9, of which 5 were waited for; matrix products, arithmetic and copies ran while one was open for 0% of the time, Pallas kernels for 6%

profile of v2, /device:TPU:385, one launch (start us, length us, event | category | flops | bytes accessed | tf_op | source)
XLA Modules:
  0.0 85.2 jit_solution(13274599301728053654)
XLA Ops:
  0.0 1.0 %copy-done.3 = f32[1,4,2,64,128]{4,3,2,1,0:T(8,128)S(1)} copy-done((f32[1,4,2,64,128]{4,3,2,1,0:T(8,128)S(1)}, f32[1,4,2,64,128]{4,3,2,1,0:T(8,128)}, u32[]{:S(2)}) %copy-start.3) | copy-done | bytes 262168
  1.0 0.7 copy-done.9
  1.7 1.4 %shard_map.101 = (f32[64,8,128]{2,1,0:T(8,128)}, f32[2,8,128]{2,1,0:T(8,128)S(1)}) custom-call(s32[2,64]{1,0:T(2,128)S(1)} %bitcast.31, f32[4,2,64,128]{3,2,1,0:T(8,128)S(1)} %bitcast.22), custom_call_target="tpu_custom_call" | custom-call | bytes 524288 | tf_op jit(solution)/shard_map/pallas_call | solution.py:26
  3.1 13.2 %all-to-all-start = ((f32[64,8,128]{2,1,0:T(8,128)}), f32[64,8,128]{2,1,0:T(8,128)S(1)}, u32[]{:S(2)}, u32[]{:S(2)}) async-start(f32[64,8,128]{2,1,0:T(8,128)} %get-tuple-element.35), calls=%async_computation | async-start | bytes 524288 | tf_op jit(solution)/shard_map/all_to_all | solution.py:326
  16.3 0.0 copy-start.4
  16.3 0.9 %copy-done.4 = f32[1,4,2,64,128]{4,3,2,1,0:T(8,128)S(1)} copy-done((f32[1,4,2,64,128]{4,3,2,1,0:T(8,128)S(1)}, f32[1,4,2,64,128]{4,3,2,1,0:T(8,128)}, u32[]{:S(2)}) %copy-start.4) | copy-done | bytes 262168
  17.3 0.0 copy-start.8
  17.3 2.9 %collective-permute-start = (f32[4,64,128]{2,1,0:T(8,128)S(1)}, f32[4,64,128]{2,1,0:T(8,128)S(1)}, u32[]{:S(2)}, u32[]{:S(2)}) collective-permute-start(f32[4,64,128]{2,1,0:T(8,128)S(1)} %get-tuple-element.31.inner_ref), channel_id=1, source_target_pairs={{0,1},{1,0},{2,3},{3,2},{4,5},{5,4},{6,7},{7,6},{8,9},{9,8},{10,11... | collective-permute-start | bytes 393224 | tf_op jit(solution)/shard_map/ppermute | solution.py:328
  20.2 6.0 %collective-permute-start.1 = (f32[4,64,128]{2,1,0:T(8,128)S(1)}, f32[4,64,128]{2,1,0:T(8,128)S(1)}, u32[]{:S(2)}, u32[]{:S(2)}) collective-permute-start(f32[4,64,128]{2,1,0:T(8,128)S(1)} %get-tuple-element.32.outer_ref), channel_id=1, source_target_pairs={{1,2},{3,4},{5,6},{7,8},{9,10},{11,12},{13,14},{2,1},{4,3},{6,5},{... | collective-permute-start | bytes 393224 | tf_op jit(solution)/shard_map/ppermute | solution.py:327
  26.8 0.0 copy-start.10
  26.8 0.0 copy-start.11
  26.9 0.6 copy-done.10
  27.5 1.2 %shard_map.100 = (bf16[128,512]{1,0:T(8,128)(2,1)S(1)}, s32[64,8,128]{2,1,0:T(8,128)S(1)}) custom-call(s32[1,64]{1,0:T(1,128)S(1)} %bitcast.33, s32[1,1]{1,0:T(1,128)S(6)} %copy.11.live_ref, s32[2,64]{1,0:T(2,128)S(1)} %bitcast.32, s32[1,64]{1,0:T(1,128)S(1)} %bitcast.34, f32[4,4,64]{2,1,0:T(4,128)S(1)} %bitcast.30), custom_call_target="tpu_custom_call" | custom-call | bytes 524288 | tf_op jit(solution)/shard_map/pallas_call | solution.py:26
  28.7 0.4 collective-permute-done.1.from_chip_ref
  29.1 0.9 %copy-done.1 = f32[1,4,2,64,128]{4,3,2,1,0:T(8,128)S(1)} copy-done((f32[1,4,2,64,128]{4,3,2,1,0:T(8,128)S(1)}, f32[1,4,2,64,128]{4,3,2,1,0:T(8,128)}, u32[]{:S(2)}) %copy-start.1) | copy-done | bytes 262168
  30.1 0.8 copy-done.5
  30.9 1.3 %shard_map.103 = (f32[4,64,128]{2,1,0:T(8,128)S(1)}, f32[4,64,128]{2,1,0:T(8,128)S(1)}, f32[2,8,128]{2,1,0:T(8,128)S(1)}, f32[4,2,8,128]{3,2,1,0:T(8,128)S(1)}) custom-call(f32[4,4,6]{2,1,0:T(4,128)S(1)} %bitcast.27, f32[4,64,128]{2,1,0:T(8,128)S(1)} %get-tuple-element.31.inner_ref, f32[4,64,128]{2,1,0:T(8,128)S(1)} %get-tuple-element.32.outer_ref, ...), custom_call_target="tpu_custom_call" | custom-call | flops 4000000 | bytes 2097152 | tf_op jit(solution)/shard_map/pallas_call | solution.py:26
  32.3 1.0 %shard_map.104 = (f32[64,8,128]{2,1,0:T(8,128)}, f32[2,8,128]{2,1,0:T(8,128)S(1)}) custom-call(bf16[128,512]{1,0:T(8,128)(2,1)S(1)} %get-tuple-element.29.matrix_ref, f32[4,2,8,128]{3,2,1,0:T(8,128)S(1)} %get-tuple-element.33.edge_ref, f32[2,8,128]{2,1,0:T(8,128)S(1)} %get-tuple-element.34.strips_ref, f32[64,8,128]{2,1,0:T(8,128)S(1)} %all-to-all-done.got_ref, ...), custom_call_target="tpu_custom_call" | custom-call | bytes 524288 | tf_op jit(solution)/shard_map/pallas_call | solution.py:26
  33.2 12.3 %all-to-all-start.1 = ((f32[64,8,128]{2,1,0:T(8,128)}), f32[64,8,128]{2,1,0:T(8,128)S(1)}, u32[]{:S(2)}, u32[]{:S(2)}) async-start(f32[64,8,128]{2,1,0:T(8,128)} %get-tuple-element.43), calls=%async_computation.1 | async-start | bytes 524288 | tf_op jit(solution)/shard_map/all_to_all | solution.py:326
  45.5 2.1 %collective-permute-start.2 = (f32[4,64,128]{2,1,0:T(8,128)S(1)}, f32[4,64,128]{2,1,0:T(8,128)S(1)}, u32[]{:S(2)}, u32[]{:S(2)}) collective-permute-start(f32[4,64,128]{2,1,0:T(8,128)S(1)} %get-tuple-element.40.inner_ref), channel_id=1, source_target_pairs={{0,1},{1,0},{2,3},{3,2},{4,5},{5,4},{6,7},{7,6},{8,9},{9,8},{10,11... | collective-permute-start | bytes 393224 | tf_op jit(solution)/shard_map/ppermute | solution.py:328
  47.6 5.1 %collective-permute-start.3 = (f32[4,64,128]{2,1,0:T(8,128)S(1)}, f32[4,64,128]{2,1,0:T(8,128)S(1)}, u32[]{:S(2)}, u32[]{:S(2)}) collective-permute-start(f32[4,64,128]{2,1,0:T(8,128)S(1)} %get-tuple-element.41.outer_ref), channel_id=1, source_target_pairs={{1,2},{3,4},{5,6},{7,8},{9,10},{11,12},{13,14},{2,1},{4,3},{6,5},{... | collective-permute-start | bytes 393224 | tf_op jit(solution)/shard_map/ppermute | solution.py:327
  52.7 2.9 %collective-permute-done.3.from_chip_ref = f32[4,64,128]{2,1,0:T(8,128)S(1)} collective-permute-done((f32[4,64,128]{2,1,0:T(8,128)S(1)}, f32[4,64,128]{2,1,0:T(8,128)S(1)}, u32[]{:S(2)}, u32[]{:S(2)}) %collective-permute-start.3) | collective-permute-done | bytes 131104 | tf_op jit(solution)/shard_map/ppermute | solution.py:327
  55.7 1.3 %shard_map.106 = (f32[4,64,128]{2,1,0:T(8,128)S(1)}, f32[4,64,128]{2,1,0:T(8,128)S(1)}, f32[2,8,128]{2,1,0:T(8,128)S(1)}) custom-call(f32[4,4,6]{2,1,0:T(4,128)S(1)} %bitcast.28, f32[4,64,128]{2,1,0:T(8,128)S(1)} %get-tuple-element.40.inner_ref, f32[4,64,128]{2,1,0:T(8,128)S(1)} %get-tuple-element.41.outer_ref, ...), custom_call_target="tpu_custom_call" | custom-call | flops 4000000 | bytes 2097152 | tf_op jit(solution)/shard_map/pallas_call | solution.py:26
  57.0 2.2 %all-to-all-done.1.got_ref = f32[64,8,128]{2,1,0:T(8,128)S(1)} async-done(((f32[64,8,128]{2,1,0:T(8,128)}), f32[64,8,128]{2,1,0:T(8,128)S(1)}, u32[]{:S(2)}, u32[]{:S(2)}) %all-to-all-start.1) | async-done | bytes 262176 | tf_op jit(solution)/shard_map/all_to_all | solution.py:326
  59.1 1.0 %shard_map.107 = (f32[64,8,128]{2,1,0:T(8,128)}, f32[2,8,128]{2,1,0:T(8,128)S(1)}) custom-call(bf16[128,512]{1,0:T(8,128)(2,1)S(1)} %get-tuple-element.29.matrix_ref, f32[4,2,8,128]{3,2,1,0:T(8,128)S(1)} %get-tuple-element.33.edge_ref, f32[2,8,128]{2,1,0:T(8,128)S(1)} %get-tuple-element.42.strips_ref, f32[64,8,128]{2,1,0:T(8,128)S(1)} %all-to-all-done.1.got_ref, ...), custom_call_target="tpu_custom_call" | custom-call | bytes 524288 | tf_op jit(solution)/shard_map/pallas_call | solution.py:26
  60.1 10.0 %all-to-all-start.2 = ((f32[64,8,128]{2,1,0:T(8,128)}), f32[64,8,128]{2,1,0:T(8,128)S(1)}, u32[]{:S(2)}, u32[]{:S(2)}) async-start(f32[64,8,128]{2,1,0:T(8,128)} %get-tuple-element.50), calls=%async_computation.2 | async-start | bytes 524288 | tf_op jit(solution)/shard_map/all_to_all | solution.py:326
  70.1 1.9 %collective-permute-start.4 = (f32[4,64,128]{2,1,0:T(8,128)S(1)}, f32[4,64,128]{2,1,0:T(8,128)S(1)}, u32[]{:S(2)}, u32[]{:S(2)}) collective-permute-start(f32[4,64,128]{2,1,0:T(8,128)S(1)} %get-tuple-element.47.inner_ref), channel_id=1, source_target_pairs={{0,1},{1,0},{2,3},{3,2},{4,5},{5,4},{6,7},{7,6},{8,9},{9,8},{10,11... | collective-permute-start | bytes 393224 | tf_op jit(solution)/shard_map/ppermute | solution.py:328
  72.0 5.1 %collective-permute-start.5 = (f32[4,64,128]{2,1,0:T(8,128)S(1)}, f32[4,64,128]{2,1,0:T(8,128)S(1)}, u32[]{:S(2)}, u32[]{:S(2)}) collective-permute-start(f32[4,64,128]{2,1,0:T(8,128)S(1)} %get-tuple-element.48.outer_ref), channel_id=1, source_target_pairs={{1,2},{3,4},{5,6},{7,8},{9,10},{11,12},{13,14},{2,1},{4,3},{6,5},{... | collective-permute-start | bytes 393224 | tf_op jit(solution)/shard_map/ppermute | solution.py:327
  77.2 2.9 %collective-permute-done.5.from_chip_ref = f32[4,64,128]{2,1,0:T(8,128)S(1)} collective-permute-done((f32[4,64,128]{2,1,0:T(8,128)S(1)}, f32[4,64,128]{2,1,0:T(8,128)S(1)}, u32[]{:S(2)}, u32[]{:S(2)}) %collective-permute-start.5) | collective-permute-done | bytes 131104 | tf_op jit(solution)/shard_map/ppermute | solution.py:327
  80.1 1.3 %shard_map.109 = (f32[4,64,128]{2,1,0:T(8,128)S(1)}, f32[4,64,128]{2,1,0:T(8,128)S(1)}, f32[2,8,128]{2,1,0:T(8,128)S(1)}) custom-call(f32[4,4,6]{2,1,0:T(4,128)S(1)} %bitcast.29, f32[4,64,128]{2,1,0:T(8,128)S(1)} %get-tuple-element.47.inner_ref, f32[4,64,128]{2,1,0:T(8,128)S(1)} %get-tuple-element.48.outer_ref, ...), custom_call_target="tpu_custom_call" | custom-call | flops 4000000 | bytes 2097152 | tf_op jit(solution)/shard_map/pallas_call | solution.py:26
  81.4 2.9 %all-to-all-done.2.got_ref = f32[64,8,128]{2,1,0:T(8,128)S(1)} async-done(((f32[64,8,128]{2,1,0:T(8,128)}), f32[64,8,128]{2,1,0:T(8,128)S(1)}, u32[]{:S(2)}, u32[]{:S(2)}) %all-to-all-start.2) | async-done | bytes 262176 | tf_op jit(solution)/shard_map/all_to_all | solution.py:326
  84.3 0.9 %shard_map.110 = f32[4,2,64,128]{3,2,1,0:T(8,128)} custom-call(bf16[128,512]{1,0:T(8,128)(2,1)S(1)} %get-tuple-element.29.matrix_ref, f32[4,2,8,128]{3,2,1,0:T(8,128)S(1)} %get-tuple-element.33.edge_ref, f32[2,8,128]{2,1,0:T(8,128)S(1)} %get-tuple-element.49.strips_ref, f32[64,8,128]{2,1,0:T(8,128)S(1)} %all-to-all-done.2.got_ref, ...), custom_call_target="tpu_custom_call" | custom-call | bytes 524288 | tf_op jit(solution)/shard_map/pallas_call | solution.py:26
  (23 shorter events, 0.1 us)
Async XLA Ops:
  0.0 29.1 %copy-start = (f32[1,4,4,2,64,128]{5,4,3,2,1,0:T(8,128)S(1)}, f32[1,4,4,2,64,128]{5,4,3,2,1,0:T(8,128)}, u32[]{:S(2)}) copy-start(f32[1,4,4,2,64,128]{5,4,3,2,1,0:T(8,128)} %param.12) | copy-start | bytes 3145732
  0.0 1.0 %copy-start.3 = (f32[1,4,2,64,128]{4,3,2,1,0:T(8,128)S(1)}, f32[1,4,2,64,128]{4,3,2,1,0:T(8,128)}, u32[]{:S(2)}) copy-start(f32[1,4,2,64,128]{4,3,2,1,0:T(8,128)} %param.11) | copy-start | bytes 786436
  1.0 0.7 copy-start.9
  3.1 29.2 %all-to-all-start = ((f32[64,8,128]{2,1,0:T(8,128)}), f32[64,8,128]{2,1,0:T(8,128)S(1)}, u32[]{:S(2)}, u32[]{:S(2)}) async-start(f32[64,8,128]{2,1,0:T(8,128)} %get-tuple-element.35), calls=%async_computation | async-start | bytes 524288 | tf_op jit(solution)/shard_map/all_to_all | solution.py:326
  16.3 1.0 %copy-start.4 = (f32[1,4,2,64,128]{4,3,2,1,0:T(8,128)S(1)}, f32[1,4,2,64,128]{4,3,2,1,0:T(8,128)}, u32[]{:S(2)}) copy-start(f32[1,4,2,64,128]{4,3,2,1,0:T(8,128)} %param.11) | copy-start | bytes 786436
  17.3 9.6 %copy-start.12 = (s32[1,1,64]{2,1,0:T(1,128)S(1)}, s32[1,1,64]{2,1,0:T(1,128)}, u32[]{:S(2)}) copy-start(s32[1,1,64]{2,1,0:T(1,128)} %param.16) | copy-start | bytes 772
  17.3 9.6 %copy-start.8 = (f32[1,1,64,4,4]{2,4,3,1,0:T(4,128)S(1)}, f32[1,1,64,4,4]{2,4,3,1,0:T(4,128)}, u32[]{:S(2)}) copy-start(f32[1,1,64,4,4]{2,4,3,1,0:T(4,128)} %param.17) | copy-start | bytes 12292
  17.3 11.4 %collective-permute-start = (f32[4,64,128]{2,1,0:T(8,128)S(1)}, f32[4,64,128]{2,1,0:T(8,128)S(1)}, u32[]{:S(2)}, u32[]{:S(2)}) collective-permute-start(f32[4,64,128]{2,1,0:T(8,128)S(1)} %get-tuple-element.31.inner_ref), channel_id=1, source_target_pairs={{0,1},{1,0},{2,3},{3,2},{4,5},{5,4},{6,7},{7,6},{8,9},{9,8},{10,11... | collective-permute-start | bytes 393224 | tf_op jit(solution)/shard_map/ppermute | solution.py:328
  20.2 9.0 %collective-permute-start.1 = (f32[4,64,128]{2,1,0:T(8,128)S(1)}, f32[4,64,128]{2,1,0:T(8,128)S(1)}, u32[]{:S(2)}, u32[]{:S(2)}) collective-permute-start(f32[4,64,128]{2,1,0:T(8,128)S(1)} %get-tuple-element.32.outer_ref), channel_id=1, source_target_pairs={{1,2},{3,4},{5,6},{7,8},{9,10},{11,12},{13,14},{2,1},{4,3},{6,5},{... | collective-permute-start | bytes 393224 | tf_op jit(solution)/shard_map/ppermute | solution.py:327
  26.8 0.7 copy-start.10
  26.8 0.7 copy-start.11
  27.5 1.6 %copy-start.7 = (f32[1,6,4,4]{1,3,2,0:T(4,128)S(1)}, f32[1,6,4,4]{1,3,2,0:T(4,128)}, u32[]{:S(2)}) copy-start(f32[1,6,4,4]{1,3,2,0:T(4,128)} %param.14) | copy-start | bytes 1156
  29.1 1.0 %copy-start.1 = (f32[1,4,2,64,128]{4,3,2,1,0:T(8,128)S(1)}, f32[1,4,2,64,128]{4,3,2,1,0:T(8,128)}, u32[]{:S(2)}) copy-start(f32[1,4,2,64,128]{4,3,2,1,0:T(8,128)} %param.10) | copy-start | bytes 786436
  30.1 0.8 copy-start.5
  33.2 22.4 %copy-start.6 = (f32[1,2,64,128]{3,2,1,0:T(8,128)S(1)}, f32[1,2,64,128]{3,2,1,0:T(8,128)}, u32[]{:S(2)}) copy-start(f32[1,2,64,128]{3,2,1,0:T(8,128)} %param.13) | copy-start | bytes 196612
  33.2 25.9 %all-to-all-start.1 = ((f32[64,8,128]{2,1,0:T(8,128)}), f32[64,8,128]{2,1,0:T(8,128)S(1)}, u32[]{:S(2)}, u32[]{:S(2)}) async-start(f32[64,8,128]{2,1,0:T(8,128)} %get-tuple-element.43), calls=%async_computation.1 | async-start | bytes 524288 | tf_op jit(solution)/shard_map/all_to_all | solution.py:326
  45.5 10.2 %copy-start.2 = (f32[1,4,2,64,128]{4,3,2,1,0:T(8,128)S(1)}, f32[1,4,2,64,128]{4,3,2,1,0:T(8,128)}, u32[]{:S(2)}) copy-start(f32[1,4,2,64,128]{4,3,2,1,0:T(8,128)} %param.10) | copy-start | bytes 786436
  45.5 7.2 %collective-permute-start.2 = (f32[4,64,128]{2,1,0:T(8,128)S(1)}, f32[4,64,128]{2,1,0:T(8,128)S(1)}, u32[]{:S(2)}, u32[]{:S(2)}) collective-permute-start(f32[4,64,128]{2,1,0:T(8,128)S(1)} %get-tuple-element.40.inner_ref), channel_id=1, source_target_pairs={{0,1},{1,0},{2,3},{3,2},{4,5},{5,4},{6,7},{7,6},{8,9},{9,8},{10,11... | collective-permute-start | bytes 393224 | tf_op jit(solution)/shard_map/ppermute | solution.py:328
  47.6 8.1 %collective-permute-start.3 = (f32[4,64,128]{2,1,0:T(8,128)S(1)}, f32[4,64,128]{2,1,0:T(8,128)S(1)}, u32[]{:S(2)}, u32[]{:S(2)}) collective-permute-start(f32[4,64,128]{2,1,0:T(8,128)S(1)} %get-tuple-element.41.outer_ref), channel_id=1, source_target_pairs={{1,2},{3,4},{5,6},{7,8},{9,10},{11,12},{13,14},{2,1},{4,3},{6,5},{... | collective-permute-start | bytes 393224 | tf_op jit(solution)/shard_map/ppermute | solution.py:327
  60.1 24.2 %all-to-all-start.2 = ((f32[64,8,128]{2,1,0:T(8,128)}), f32[64,8,128]{2,1,0:T(8,128)S(1)}, u32[]{:S(2)}, u32[]{:S(2)}) async-start(f32[64,8,128]{2,1,0:T(8,128)} %get-tuple-element.50), calls=%async_computation.2 | async-start | bytes 524288 | tf_op jit(solution)/shard_map/all_to_all | solution.py:326
  70.1 7.1 %collective-permute-start.4 = (f32[4,64,128]{2,1,0:T(8,128)S(1)}, f32[4,64,128]{2,1,0:T(8,128)S(1)}, u32[]{:S(2)}, u32[]{:S(2)}) collective-permute-start(f32[4,64,128]{2,1,0:T(8,128)S(1)} %get-tuple-element.47.inner_ref), channel_id=1, source_target_pairs={{0,1},{1,0},{2,3},{3,2},{4,5},{5,4},{6,7},{7,6},{8,9},{9,8},{10,11... | collective-permute-start | bytes 393224 | tf_op jit(solution)/shard_map/ppermute | solution.py:328
  72.0 8.1 %collective-permute-start.5 = (f32[4,64,128]{2,1,0:T(8,128)S(1)}, f32[4,64,128]{2,1,0:T(8,128)S(1)}, u32[]{:S(2)}, u32[]{:S(2)}) collective-permute-start(f32[4,64,128]{2,1,0:T(8,128)S(1)} %get-tuple-element.48.outer_ref), channel_id=1, source_target_pairs={{1,2},{3,4},{5,6},{7,8},{9,10},{11,12},{13,14},{2,1},{4,3},{6,5},{... | collective-permute-start | bytes 393224 | tf_op jit(solution)/shard_map/ppermute | solution.py:327

commit v3 on v2

--- a/solution.py
+++ b/solution.py
@@ -18,6 +18,7 @@
 
 VMEM = pl.BlockSpec(memory_space=pltpu.VMEM)
 SMEM = pl.BlockSpec(memory_space=pltpu.SMEM)
+HBM = pl.BlockSpec(memory_space=pltpu.HBM)
 PARAMS = pltpu.CompilerParams(vmem_limit_bytes=24 * 1024 * 1024)
 
 
@@ -34,6 +35,10 @@
     )(*args)
 
 
+def in_hbm(*arrays):
+    return tuple(pltpu.with_memory_space_constraint(array, pltpu.HBM) for array in arrays)
+
+
 def f32(*shape):
     return jax.ShapeDtypeStruct(shape, jnp.float32)
 
@@ -46,46 +51,53 @@
     return (0, rows - 1)
 
 
-def first_kernel(faces_ref, field_ref, send_ref, strips_ref, scratch):
-    rows = field_ref.shape[2]
+def first_kernel(
+    faces_hbm, field_hbm, send_ref, strips_ref, inner_ref, outer_ref, faces, edges, scratch, sems
+):
+    rows = field_hbm.shape[2]
+    tile = edges.shape[3]
+    at = inner_plane()
+    copies = [
+        pltpu.make_async_copy(faces_hbm, faces, sems.at[0]),
+        pltpu.make_async_copy(field_hbm.at[:, :, pl.ds(0, tile)], edges.at[0], sems.at[1]),
+        pltpu.make_async_copy(
+            field_hbm.at[:, :, pl.ds(rows - tile, tile)], edges.at[1], sems.at[2]
+        ),
+        pltpu.make_async_copy(field_hbm.at[:, at], inner_ref, sems.at[3]),
+        pltpu.make_async_copy(field_hbm.at[:, 1 - at], outer_ref, sems.at[4]),
+    ]
+    for copy in copies:
+        copy.start()
+    for copy in copies[:3]:
+        copy.wait()
     for plane in range(CX):
-        for side, row in enumerate(edge_rows(rows)):
+        for side, row in enumerate((0, tile - 1)):
             for var in range(V):
-                value = field_ref[var, plane, row : row + 1, :]
+                value = edges[side, var, plane, row : row + 1, :]
                 scratch[plane * 2 + side, var : var + 1, :] = value
-                at = side * V + var
-                strips_ref[plane, at : at + 1, :] = value
+                to = side * V + var
+                strips_ref[plane, to : to + 1, :] = value
     for group in range(send_ref.shape[0]):
         for slot in range(SLOT):
-            send_ref[group, slot * V : (slot + 1) * V, :] = scratch[faces_ref[slot, group]]
+            send_ref[group, slot * V : (slot + 1) * V, :] = scratch[faces[slot, group]]
+    for copy in copies[3:]:
+        copy.wait()
 
 
 def first_part(faces, field):
-    groups, z = faces.shape[1], field.shape[-1]
+    groups, (rows, z) = faces.shape[1], field.shape[2:]
     return call(
         first_kernel,
-        [f32(groups, SLOT * V, z), f32(CX, 2 * V, z)],
-        [SMEM, VMEM],
-        (faces, field),
-        scratch=[pltpu.VMEM((FACES, V, z), jnp.float32)],
-    )
-
-
-def split_kernel(strips_ref, field_ref, inner_ref, outer_ref):
-    rows = inner_ref.shape[1]
-    at = inner_plane()
-    for ref, plane in ((inner_ref, at), (outer_ref, 1 - at)):
-        for var in range(V):
-            ref[var] = field_ref[var, plane]
-        for side, row in enumerate(edge_rows(rows)):
-            for var in range(V):
-                here = side * V + var
-                ref[var, row : row + 1, :] = strips_ref[plane, here : here + 1, :]
-
-
-def split_part(strips, field):
-    shape = f32(V, field.shape[2], field.shape[3])
-    return call(split_kernel, [shape, shape], [VMEM] * 2, (strips, field))
+        [f32(groups, SLOT * V, z), f32(CX, 2 * V, z), f32(V, rows, z), f32(V, rows, z)],
+        [HBM, HBM],
+        in_hbm(faces, field),
+        scratch=[
+            pltpu.SMEM(faces.shape, jnp.int32),
+            pltpu.VMEM((2, V, CX, 8, z), jnp.float32),
+            pltpu.VMEM((FACES, V, z), jnp.float32),
+            pltpu.SemaphoreType.DMA((5,)),
+        ],
+    )
 
 
 def patch_kernel(strips_ref, old_inner_ref, old_outer_ref, inner_ref, outer_ref):
@@ -108,8 +120,33 @@
 
 
 def setup_kernel(
-    source_ref, live_ref, faces_ref, target_ref, weight_ref, matrix_ref, mask_ref
-):
+    source_ref,
+    live_ref,
+    target_ref,
+    stencil_ref,
+    weight_ref,
+    faces_hbm,
+    right_hbm,
+    conductivity_hbm,
+    inverse_hbm,
+    matrix_ref,
+    mask_ref,
+    coefs_ref,
+    right_ref,
+    conductivity_ref,
+    inverse_ref,
+    edge_ref,
+    faces_ref,
+    sems,
+):
+    copies = [
+        pltpu.make_async_copy(faces_hbm, faces_ref, sems.at[0]),
+        pltpu.make_async_copy(right_hbm, right_ref, sems.at[1]),
+        pltpu.make_async_copy(conductivity_hbm, conductivity_ref, sems.at[2]),
+        pltpu.make_async_copy(inverse_hbm, inverse_ref, sems.at[3]),
+    ]
+    for copy in copies:
+        copy.start()
     entries = target_ref.shape[1]
     groups = mask_ref.shape[0]
     columns = matrix_ref.shape[1]
@@ -135,53 +172,68 @@
     high = matrix.astype(jnp.bfloat16)
     matrix_ref[: V * ROWS, :] = high
     matrix_ref[V * ROWS :, :] = (matrix - high.astype(jnp.float32)).astype(jnp.bfloat16)
+    for direction in range(6):
+        for var in range(V):
+            for col in range(V):
+                coefs_ref[direction, var, col] = jnp.full(
+                    coefs_ref.shape[3:], stencil_ref[var, col, direction], jnp.float32
+                )
+    copies[0].wait()
     tile_rows = lax.broadcasted_iota(jnp.int32, mask_ref.shape[1:], 0)
     for group in range(groups):
         mask_ref[group] = jnp.where(tile_rows < V, faces_ref[0, group], faces_ref[1, group])
-
-
-def setup_part(source, live, faces, target, weight, z):
-    groups = faces.shape[1]
+    for copy in copies[1:]:
+        copy.wait()
+    for plane in range(CX):
+        for side, row in enumerate(edge_rows(inverse_ref.shape[3])):
+            for var in range(V):
+                to = side * V + var
+                for col in range(V):
+                    edge_ref[col, plane, to : to + 1, :] = (
+                        relax_weight * inverse_ref[var, col, plane, row : row + 1, :]
+                    )
+
+
+def setup_part(source, live, target, stencil, weight, faces, right, cond, inverse):
+    groups, z = faces.shape[1], right.shape[-1]
     return call(
         setup_kernel,
         [
             jax.ShapeDtypeStruct((2 * V * ROWS, groups * SLOT * V), jnp.bfloat16),
             jax.ShapeDtypeStruct((groups, SLOT * V, z), jnp.int32),
+            f32(6, V, V, 8, z),
+            f32(*right.shape),
+            f32(*cond.shape),
+            f32(*inverse.shape),
+            f32(V, CX, 2 * V, z),
         ],
-        [SMEM, SMEM, SMEM, VMEM, VMEM],
-        (source, live, faces, target, weight),
-    )
-
-
-def local_kernel(
-    first,
-    stencil_ref,
-    inner_ref,
-    outer_ref,
-    from_core_ref,
-    from_chip_ref,
-    right_ref,
-    conductivity_ref,
-    inverse_ref,
-    next_inner_ref,
-    next_outer_ref,
-    strips_ref,
-    *maybe_edge,
+        [SMEM, SMEM, VMEM, SMEM, VMEM, HBM, HBM, HBM, HBM],
+        (source, live, target, stencil, weight, *in_hbm(faces, right, cond, inverse)),
+        scratch=[pltpu.SMEM(faces.shape, jnp.int32), pltpu.SemaphoreType.DMA((4,))],
+    )
+
+
+def times(coef, value):
+    rows, lanes = value.shape
+    return (value.reshape(rows // 8, 8, lanes) * coef).reshape(rows, lanes)
+
+
+def near_kernel(
+    coefs_ref, inner_ref, outer_ref, right_ref, conductivity_ref, inner_load_ref, outer_load_ref
 ):
     rows, lanes = inner_ref.shape[1:]
     row_ids = lax.broadcasted_iota(jnp.int32, (rows, lanes), 0)
     lane_ids = lax.broadcasted_iota(jnp.int32, (rows, lanes), 1)
     at = inner_plane()
-    for here, beside, outside, plane, out_ref in (
-        (inner_ref, outer_ref, from_core_ref, at, next_inner_ref),
-        (outer_ref, inner_ref, from_chip_ref, 1 - at, next_outer_ref),
+    for here, beside, plane, out_ref in (
+        (inner_ref, outer_ref, at, inner_load_ref),
+        (outer_ref, inner_ref, 1 - at, outer_load_ref),
     ):
-        directions = (plane, 1 - plane, 2, 3, 4, 5)
+        directions = (1 - plane, 2, 3, 4, 5)
         sums = [jnp.zeros((rows, lanes), jnp.float32) for _ in range(V)]
         for col in range(V):
             value = here[col]
             shifted = (
-                outside[col],
                 beside[col],
                 jnp.where(row_ids == 0, 0.0, pltpu.roll(value, 1, 0)),
                 jnp.where(row_ids == rows - 1, 0.0, pltpu.roll(value, rows - 1, 0)),
@@ -190,37 +242,103 @@
             )
             for direction, moved in zip(directions, shifted):
                 for var in range(V):
-                    sums[var] = sums[var] + stencil_ref[var, col, direction] * moved
+                    sums[var] = sums[var] + times(coefs_ref[direction, var, col], moved)
         cond = conductivity_ref[plane]
-        loads = [right_ref[var, plane] + cond * sums[var] for var in range(V)]
         for var in range(V):
-            total = inverse_ref[var, 0, plane] * loads[0]
-            for col in range(1, V):
-                total = total + inverse_ref[var, col, plane] * loads[col]
-            out_ref[var] = (1.0 - relax_weight) * here[var] + relax_weight * total
-        for side, row in enumerate(edge_rows(rows)):
-            for var in range(V):
-                to = side * V + var
-                strips_ref[plane, to : to + 1, :] = out_ref[var, row : row + 1, :]
-                if first:
-                    for col in range(V):
-                        maybe_edge[0][col, plane, to : to + 1, :] = (
-                            relax_weight * inverse_ref[var, col, plane, row : row + 1, :]
-                        )
-
-
-def local_part(first, stencil, inner, outer, from_core, from_chip, right, cond, inverse):
-    z = inner.shape[-1]
-    out_shape = [f32(*inner.shape), f32(*inner.shape), f32(CX, 2 * V, z)]
-    if first:
-        out_shape.append(f32(V, CX, 2 * V, z))
-    return call(
-        functools.partial(local_kernel, first),
-        out_shape,
-        [SMEM] + [VMEM] * 7,
-        (stencil, inner, outer, from_core, from_chip, right, cond, inverse),
-        flops=4_000_000,
-        moved=2 * 1024 * 1024,
+            out_ref[var] = right_ref[var, plane] + cond * sums[var]
+
+
+def near_part(coefs, inner, outer, right, cond):
+    return call(
+        near_kernel,
+        [f32(*inner.shape), f32(*inner.shape)],
+        [VMEM] * 5,
+        (coefs, inner, outer, right, cond),
+        flops=3_000_000,
+        moved=1024 * 1024,
+    )
+
+
+def finish(plane, coefs_ref, here_ref, load_ref, outside_ref, conductivity_ref, inverse_ref):
+    cond = conductivity_ref[plane]
+    loads = []
+    for var in range(V):
+        total = times(coefs_ref[plane, var, 0], outside_ref[0])
+        for col in range(1, V):
+            total = total + times(coefs_ref[plane, var, col], outside_ref[col])
+        loads.append(load_ref[var] + cond * total)
+    values = []
+    for var in range(V):
+        total = inverse_ref[var, 0, plane] * loads[0]
+        for col in range(1, V):
+            total = total + inverse_ref[var, col, plane] * loads[col]
+        values.append((1.0 - relax_weight) * here_ref[var] + relax_weight * total)
+    return values
+
+
+def outer_kernel(
+    coefs_ref,
+    here_ref,
+    load_ref,
+    outside_ref,
+    conductivity_ref,
+    inverse_ref,
+    next_ref,
+    strips_ref,
+):
+    plane = 1 - inner_plane()
+    values = finish(
+        plane, coefs_ref, here_ref, load_ref, outside_ref, conductivity_ref, inverse_ref
+    )
+    for var, value in enumerate(values):
+        next_ref[var] = value
+        for side, row in enumerate(edge_rows(value.shape[0])):
+            to = side * V + var
+            strips_ref[to : to + 1, :] = value[row : row + 1]
+
+
+def outer_part(coefs, here, load, outside, cond, inverse):
+    return call(
+        outer_kernel,
+        [f32(*here.shape), f32(2 * V, here.shape[-1])],
+        [VMEM] * 6,
+        (coefs, here, load, outside, cond, inverse),
+        flops=1_000_000,
+        moved=1024 * 1024,
+    )
+
+
+def inner_kernel(
+    coefs_ref,
+    here_ref,
+    load_ref,
+    outside_ref,
+    conductivity_ref,
+    inverse_ref,
+    other_ref,
+    next_ref,
+    strips_ref,
+):
+    plane = inner_plane()
+    strips_ref[1 - plane] = other_ref[...]
+    values = finish(
+        plane, coefs_ref, here_ref, load_ref, outside_ref, conductivity_ref, inverse_ref
+    )
+    for var, value in enumerate(values):
+        next_ref[var] = value
+        for side, row in enumerate(edge_rows(value.shape[0])):
+            to = side * V + var
+            strips_ref[plane, to : to + 1, :] = value[row : row + 1]
+
+
+def inner_part(coefs, here, load, outside, cond, inverse, other):
+    return call(
+        inner_kernel,
+        [f32(*here.shape), f32(CX, *other.shape)],
+        [VMEM] * 7,
+        (coefs, here, load, outside, cond, inverse, other),
+        flops=1_000_000,
+        moved=1024 * 1024,
     )
 
 
@@ -243,7 +361,9 @@
     return tiles
 
 
-def strip_kernel(matrix_ref, edge_ref, strips_ref, got_ref, mask_ref, send_ref, new_ref):
+def strip_kernel(
+    matrix_ref, edge_ref, strips_ref, got_ref, mask_ref, send_ref, new_ref
+):
     tiles = new_strips(matrix_ref, edge_ref, strips_ref, got_ref)
     upper = lax.broadcasted_iota(jnp.int32, tiles[0].shape, 0) < V
     faces = []
@@ -268,7 +388,9 @@
     )
 
 
-def last_kernel(matrix_ref, edge_ref, strips_ref, got_ref, inner_ref, outer_ref, out_ref):
+def last_kernel(
+    matrix_ref, edge_ref, strips_ref, got_ref, inner_ref, outer_ref, out_ref
+):
     rows = inner_ref.shape[1]
     at = inner_plane()
     for ref, plane in ((inner_ref, at), (outer_ref, 1 - at)):
@@ -316,25 +438,28 @@
     chip_swap = [(i, i + 1) for i in range(1, count - 1, 2)]
     chip_swap += [(j, i) for i, j in chip_swap]
 
-    send, strips = first_part(faces, field)
-    inner, outer = split_part(strips, field)
-    matrix, mask = setup_part(
-        coupling_source[0], live_count, faces, coupling_target[0], weight, field.shape[-1]
-    )
-    edge = None
+    send, new, inner, outer = first_part(faces, field)
+    matrix, mask, coefs, right, cond, inverse, edge = setup_part(
+        coupling_source[0],
+        live_count,
+        coupling_target[0],
+        coefs,
+        weight,
+        faces,
+        right,
+        cond,
+        inverse,
+    )
     for sweep in range(SWEEPS):
         got = lax.all_to_all(send, "dom", 0, 0, tiled=True)
+        inner, outer = patch_part(new, inner, outer)
         from_chip = lax.ppermute(outer, "within", chip_swap)
         from_core = lax.ppermute(inner, "within", core_swap)
-        results = local_part(
-            sweep == 0, coefs, inner, outer, from_core, from_chip, right, cond, inverse
-        )
-        inner, outer, strips = results[:3]
-        if sweep == 0:
-            edge = results[3]
+        inner_load, outer_load = near_part(coefs, inner, outer, right, cond)
+        outer, rows = outer_part(coefs, outer, outer_load, from_chip, cond, inverse)
+        inner, strips = inner_part(coefs, inner, inner_load, from_core, cond, inverse, rows)
         if sweep < SWEEPS - 1:
             send, new = strip_part(matrix, edge, strips, got, mask)
-            inner, outer = patch_part(new, inner, outer)
         else:
             out = last_part(matrix, edge, strips, got, inner, outer)
     return out[None]

time: 85.9 us -> 80.3 us (0.935)
  the two profiles are of different devices: /device:TPU:385 before, /device:TPU:256 now
where the time goes in v3:
time: 80.3 us; the launch traced here: 79.8 us
  starting transfers between devices  51.7 us (64%)
  waiting for transfers between devices  17.9 us (22%)
  Pallas kernels  8.68 us (11%)
  between operations  0.88 us (1%)
    all_to_all x3, starting transfers between devices, per_device(): got = lax.all_to_all(send, 'dom', 0, 0, tiled=True)  29.8 us
    all_to_all x3, waiting for transfers between devices, per_device(): got = lax.all_to_all(send, 'dom', 0, 0, tiled=True)  17.1 us
    ppermute x3, starting transfers between devices, per_device(): from_core = lax.ppermute(inner, 'within', core_swap)  16.2 us
    pallas_call x17, Pallas kernels, call(): pl.pallas_call(kernel, out_shape=out_shape, in_specs=in_specs, out_specs=...  8.68 us
    ppermute x3, starting transfers between devices, per_device(): from_chip = lax.ppermute(outer, 'within', chip_swap)  5.76 us
  transfers between devices with their start and end apart: 9, of which 5 were waited for; matrix products, arithmetic and copies ran while one was open for 0% of the time, Pallas kernels for 5%

profile of v3, /device:TPU:256, one launch (start us, length us, event | category | flops | bytes accessed | tf_op | source)
XLA Modules:
  0.0 79.8 jit_solution(50489957608681401)
XLA Ops:
  0.0 1.8 %shard_map.101 = (f32[64,8,128]{2,1,0:T(8,128)}, f32[2,8,128]{2,1,0:T(8,128)S(1)}, f32[4,64,128]{2,1,0:T(8,128)S(1)}, f32[4,64,128]{2,1,0:T(8,128)S(1)}) custom-call(s32[2,64]{1,0:T(2,128)} %bitcast.24, f32[4,2,64,128]{3,2,1,0:T(8,128)} %bitcast.22), custom_call_target="tpu_custom_call" | custom-call | bytes 524288 | tf_op jit(solution)/shard_map/pallas_call | solution.py:27
  1.8 13.5 %all-to-all-start = ((f32[64,8,128]{2,1,0:T(8,128)}), f32[64,8,128]{2,1,0:T(8,128)S(1)}, u32[]{:S(2)}, u32[]{:S(2)}) async-start(f32[64,8,128]{2,1,0:T(8,128)} %get-tuple-element.59), calls=%async_computation | async-start | bytes 524288 | tf_op jit(solution)/shard_map/all_to_all | solution.py:454
  15.3 1.9 %collective-permute-start.1 = (f32[4,64,128]{2,1,0:T(8,128)S(1)}, f32[4,64,128]{2,1,0:T(8,128)S(1)}, u32[]{:S(2)}, u32[]{:S(2)}) collective-permute-start(f32[4,64,128]{2,1,0:T(8,128)S(1)} %get-tuple-element.51.outer_ref.here_ref), channel_id=1, source_target_pairs={{1,2},{3,4},{5,6},{7,8},{9,10},{11,12},{13,14},{2,1},{4,3},{6,5},{... | collective-permute-start | bytes 393224 | tf_op jit(solution)/shard_map/ppermute | solution.py:456
  17.2 0.0 copy-start.1
  17.3 5.3 %collective-permute-start = (f32[4,64,128]{2,1,0:T(8,128)S(1)}, f32[4,64,128]{2,1,0:T(8,128)S(1)}, u32[]{:S(2)}, u32[]{:S(2)}) collective-permute-start(f32[4,64,128]{2,1,0:T(8,128)S(1)} %get-tuple-element.50.inner_ref.here_ref), channel_id=1, source_target_pairs={{0,1},{1,0},{2,3},{3,2},{4,5},{5,4},{6,7},{7,6},{8,9},{9,8},{10,11... | collective-permute-start | bytes 393224 | tf_op jit(solution)/shard_map/ppermute | solution.py:457
  23.2 0.0 copy-start.3
  23.2 0.6 copy-done.2
  23.9 0.0 copy-done.3
  23.9 2.1 %shard_map.100 = (bf16[128,512]{1,0:T(8,128)(2,1)S(1)}, s32[64,8,128]{2,1,0:T(8,128)S(1)}, f32[6,4,4,8,128]{4,3,2,1,0:T(8,128)S(1)}, f32[4,2,64,128]{3,2,1,0:T(8...) custom-call(s32[1,64]{1,0:T(1,128)S(1)} %bitcast.18, ...), custom_call_target="tpu_custom_call" | custom-call | bytes 524288 | tf_op jit(solution)/shard_map/pallas_call | solution.py:27
  26.0 0.4 shard_map.103
  26.4 0.1 shard_map.104
  26.6 0.1 shard_map.105
  26.7 3.6 %all-to-all-done.got_ref = f32[64,8,128]{2,1,0:T(8,128)S(1)} async-done(((f32[64,8,128]{2,1,0:T(8,128)}), f32[64,8,128]{2,1,0:T(8,128)S(1)}, u32[]{:S(2)}, u32[]{:S(2)}) %all-to-all-start) | async-done | bytes 262176 | tf_op jit(solution)/shard_map/all_to_all | solution.py:454
  30.3 1.0 %shard_map.106 = (f32[64,8,128]{2,1,0:T(8,128)}, f32[2,8,128]{2,1,0:T(8,128)S(1)}) custom-call(bf16[128,512]{1,0:T(8,128)(2,1)S(1)} %get-tuple-element.44.matrix_ref, f32[4,2,8,128]{3,2,1,0:T(8,128)S(1)} %get-tuple-element.45.edge_ref, f32[2,8,128]{2,1,0:T(8,128)S(1)} %get-tuple-element.58.strips_ref, f32[64,8,128]{2,1,0:T(8,128)S(1)} %all-to-all-done.got_ref, ...), custom_call_target="tpu_custom_call" | custom-call | bytes 524288 | tf_op jit(solution)/shard_map/pallas_call | solution.py:27
  31.2 9.1 %all-to-all-start.1 = ((f32[64,8,128]{2,1,0:T(8,128)}), f32[64,8,128]{2,1,0:T(8,128)S(1)}, u32[]{:S(2)}, u32[]{:S(2)}) async-start(f32[64,8,128]{2,1,0:T(8,128)} %get-tuple-element.70), calls=%async_computation.1 | async-start | bytes 524288 | tf_op jit(solution)/shard_map/all_to_all | solution.py:454
  40.4 1.9 %collective-permute-start.3 = (f32[4,64,128]{2,1,0:T(8,128)S(1)}, f32[4,64,128]{2,1,0:T(8,128)S(1)}, u32[]{:S(2)}, u32[]{:S(2)}) collective-permute-start(f32[4,64,128]{2,1,0:T(8,128)S(1)} %get-tuple-element.65.outer_ref.here_ref), channel_id=1, source_target_pairs={{1,2},{3,4},{5,6},{7,8},{9,10},{11,12},{13,14},{2,1},{4,3},{6,5},{... | collective-permute-start | bytes 393224 | tf_op jit(solution)/shard_map/ppermute | solution.py:456
  42.3 6.5 %collective-permute-start.2 = (f32[4,64,128]{2,1,0:T(8,128)S(1)}, f32[4,64,128]{2,1,0:T(8,128)S(1)}, u32[]{:S(2)}, u32[]{:S(2)}) collective-permute-start(f32[4,64,128]{2,1,0:T(8,128)S(1)} %get-tuple-element.64.inner_ref.here_ref), channel_id=1, source_target_pairs={{0,1},{1,0},{2,3},{3,2},{4,5},{5,4},{6,7},{7,6},{8,9},{9,8},{10,11... | collective-permute-start | bytes 393224 | tf_op jit(solution)/shard_map/ppermute | solution.py:457
  48.8 0.4 shard_map.108
  49.3 0.1 shard_map.109
  49.4 0.4 collective-permute-done.2.outside_ref
  49.8 0.1 shard_map.110
  49.9 5.6 %all-to-all-done.1.got_ref = f32[64,8,128]{2,1,0:T(8,128)S(1)} async-done(((f32[64,8,128]{2,1,0:T(8,128)}), f32[64,8,128]{2,1,0:T(8,128)S(1)}, u32[]{:S(2)}, u32[]{:S(2)}) %all-to-all-start.1) | async-done | bytes 262176 | tf_op jit(solution)/shard_map/all_to_all | solution.py:454
  55.5 1.0 %shard_map.111 = (f32[64,8,128]{2,1,0:T(8,128)}, f32[2,8,128]{2,1,0:T(8,128)S(1)}) custom-call(bf16[128,512]{1,0:T(8,128)(2,1)S(1)} %get-tuple-element.44.matrix_ref, f32[4,2,8,128]{3,2,1,0:T(8,128)S(1)} %get-tuple-element.45.edge_ref, f32[2,8,128]{2,1,0:T(8,128)S(1)} %get-tuple-element.69.strips_ref, f32[64,8,128]{2,1,0:T(8,128)S(1)} %all-to-all-done.1.got_ref, ...), custom_call_target="tpu_custom_call" | custom-call | bytes 524288 | tf_op jit(solution)/shard_map/pallas_call | solution.py:27
  56.4 7.1 %all-to-all-start.2 = ((f32[64,8,128]{2,1,0:T(8,128)}), f32[64,8,128]{2,1,0:T(8,128)S(1)}, u32[]{:S(2)}, u32[]{:S(2)}) async-start(f32[64,8,128]{2,1,0:T(8,128)} %get-tuple-element.80), calls=%async_computation.2 | async-start | bytes 524288 | tf_op jit(solution)/shard_map/all_to_all | solution.py:454
  63.6 1.9 %collective-permute-start.5 = (f32[4,64,128]{2,1,0:T(8,128)S(1)}, f32[4,64,128]{2,1,0:T(8,128)S(1)}, u32[]{:S(2)}, u32[]{:S(2)}) collective-permute-start(f32[4,64,128]{2,1,0:T(8,128)S(1)} %get-tuple-element.75.outer_ref.here_ref), channel_id=1, source_target_pairs={{1,2},{3,4},{5,6},{7,8},{9,10},{11,12},{13,14},{2,1},{4,3},{6,5},{... | collective-permute-start | bytes 393224 | tf_op jit(solution)/shard_map/ppermute | solution.py:456
  65.5 4.4 %collective-permute-start.4 = (f32[4,64,128]{2,1,0:T(8,128)S(1)}, f32[4,64,128]{2,1,0:T(8,128)S(1)}, u32[]{:S(2)}, u32[]{:S(2)}) collective-permute-start(f32[4,64,128]{2,1,0:T(8,128)S(1)} %get-tuple-element.74.inner_ref.here_ref), channel_id=1, source_target_pairs={{0,1},{1,0},{2,3},{3,2},{4,5},{5,4},{6,7},{7,6},{8,9},{9,8},{10,11... | collective-permute-start | bytes 393224 | tf_op jit(solution)/shard_map/ppermute | solution.py:457
  69.9 0.4 shard_map.113
  70.4 0.1 shard_map.114
  70.5 0.4 collective-permute-done.4.outside_ref
  70.9 0.1 shard_map.115
  71.0 7.9 %all-to-all-done.2.got_ref = f32[64,8,128]{2,1,0:T(8,128)S(1)} async-done(((f32[64,8,128]{2,1,0:T(8,128)}), f32[64,8,128]{2,1,0:T(8,128)S(1)}, u32[]{:S(2)}, u32[]{:S(2)}) %all-to-all-start.2) | async-done | bytes 262176 | tf_op jit(solution)/shard_map/all_to_all | solution.py:454
  78.9 0.9 %shard_map.116 = f32[4,2,64,128]{3,2,1,0:T(8,128)} custom-call(bf16[128,512]{1,0:T(8,128)(2,1)S(1)} %get-tuple-element.44.matrix_ref, f32[4,2,8,128]{3,2,1,0:T(8,128)S(1)} %get-tuple-element.45.edge_ref, f32[2,8,128]{2,1,0:T(8,128)S(1)} %get-tuple-element.79.strips_ref, f32[64,8,128]{2,1,0:T(8,128)S(1)} %all-to-all-done.2.got_ref, ...), custom_call_target="tpu_custom_call" | custom-call | bytes 524288 | tf_op jit(solution)/shard_map/pallas_call | solution.py:27
  (11 shorter events, 0.1 us)
Async XLA Ops:
  1.8 28.5 %all-to-all-start = ((f32[64,8,128]{2,1,0:T(8,128)}), f32[64,8,128]{2,1,0:T(8,128)S(1)}, u32[]{:S(2)}, u32[]{:S(2)}) async-start(f32[64,8,128]{2,1,0:T(8,128)} %get-tuple-element.59), calls=%async_computation | async-start | bytes 524288 | tf_op jit(solution)/shard_map/all_to_all | solution.py:454
  15.3 11.1 %collective-permute-start.1 = (f32[4,64,128]{2,1,0:T(8,128)S(1)}, f32[4,64,128]{2,1,0:T(8,128)S(1)}, u32[]{:S(2)}, u32[]{:S(2)}) collective-permute-start(f32[4,64,128]{2,1,0:T(8,128)S(1)} %get-tuple-element.51.outer_ref.here_ref), channel_id=1, source_target_pairs={{1,2},{3,4},{5,6},{7,8},{9,10},{11,12},{13,14},{2,1},{4,3},{6,5},{... | collective-permute-start | bytes 393224 | tf_op jit(solution)/shard_map/ppermute | solution.py:456
  17.2 6.0 %copy-start.1 = (f32[1,1,64,4,4]{2,4,3,1,0:T(4,128)S(1)}, f32[1,1,64,4,4]{2,4,3,1,0:T(4,128)}, u32[]{:S(2)}) copy-start(f32[1,1,64,4,4]{2,4,3,1,0:T(4,128)} %param.17) | copy-start | bytes 12292
  17.2 6.0 %copy-start = (f32[1,6,4,4]{1,3,2,0:T(4,128)S(1)}, f32[1,6,4,4]{1,3,2,0:T(4,128)}, u32[]{:S(2)}) copy-start(f32[1,6,4,4]{1,3,2,0:T(4,128)} %param.14) | copy-start | bytes 1156
  17.3 9.3 %collective-permute-start = (f32[4,64,128]{2,1,0:T(8,128)S(1)}, f32[4,64,128]{2,1,0:T(8,128)S(1)}, u32[]{:S(2)}, u32[]{:S(2)}) collective-permute-start(f32[4,64,128]{2,1,0:T(8,128)S(1)} %get-tuple-element.50.inner_ref.here_ref), channel_id=1, source_target_pairs={{0,1},{1,0},{2,3},{3,2},{4,5},{5,4},{6,7},{7,6},{8,9},{9,8},{10,11... | collective-permute-start | bytes 393224 | tf_op jit(solution)/shard_map/ppermute | solution.py:457
  23.2 0.7 copy-start.2
  23.2 0.7 copy-start.3
  31.2 24.2 %all-to-all-start.1 = ((f32[64,8,128]{2,1,0:T(8,128)}), f32[64,8,128]{2,1,0:T(8,128)S(1)}, u32[]{:S(2)}, u32[]{:S(2)}) async-start(f32[64,8,128]{2,1,0:T(8,128)} %get-tuple-element.70), calls=%async_computation.1 | async-start | bytes 524288 | tf_op jit(solution)/shard_map/all_to_all | solution.py:454
  40.4 8.9 %collective-permute-start.3 = (f32[4,64,128]{2,1,0:T(8,128)S(1)}, f32[4,64,128]{2,1,0:T(8,128)S(1)}, u32[]{:S(2)}, u32[]{:S(2)}) collective-permute-start(f32[4,64,128]{2,1,0:T(8,128)S(1)} %get-tuple-element.65.outer_ref.here_ref), channel_id=1, source_target_pairs={{1,2},{3,4},{5,6},{7,8},{9,10},{11,12},{13,14},{2,1},{4,3},{6,5},{... | collective-permute-start | bytes 393224 | tf_op jit(solution)/shard_map/ppermute | solution.py:456
  42.3 7.5 %collective-permute-start.2 = (f32[4,64,128]{2,1,0:T(8,128)S(1)}, f32[4,64,128]{2,1,0:T(8,128)S(1)}, u32[]{:S(2)}, u32[]{:S(2)}) collective-permute-start(f32[4,64,128]{2,1,0:T(8,128)S(1)} %get-tuple-element.64.inner_ref.here_ref), channel_id=1, source_target_pairs={{0,1},{1,0},{2,3},{3,2},{4,5},{5,4},{6,7},{7,6},{8,9},{9,8},{10,11... | collective-permute-start | bytes 393224 | tf_op jit(solution)/shard_map/ppermute | solution.py:457
  56.4 22.5 %all-to-all-start.2 = ((f32[64,8,128]{2,1,0:T(8,128)}), f32[64,8,128]{2,1,0:T(8,128)S(1)}, u32[]{:S(2)}, u32[]{:S(2)}) async-start(f32[64,8,128]{2,1,0:T(8,128)} %get-tuple-element.80), calls=%async_computation.2 | async-start | bytes 524288 | tf_op jit(solution)/shard_map/all_to_all | solution.py:454
  63.6 6.8 %collective-permute-start.5 = (f32[4,64,128]{2,1,0:T(8,128)S(1)}, f32[4,64,128]{2,1,0:T(8,128)S(1)}, u32[]{:S(2)}, u32[]{:S(2)}) collective-permute-start(f32[4,64,128]{2,1,0:T(8,128)S(1)} %get-tuple-element.75.outer_ref.here_ref), channel_id=1, source_target_pairs={{1,2},{3,4},{5,6},{7,8},{9,10},{11,12},{13,14},{2,1},{4,3},{6,5},{... | collective-permute-start | bytes 393224 | tf_op jit(solution)/shard_map/ppermute | solution.py:456
  65.5 5.4 %collective-permute-start.4 = (f32[4,64,128]{2,1,0:T(8,128)S(1)}, f32[4,64,128]{2,1,0:T(8,128)S(1)}, u32[]{:S(2)}, u32[]{:S(2)}) collective-permute-start(f32[4,64,128]{2,1,0:T(8,128)S(1)} %get-tuple-element.74.inner_ref.here_ref), channel_id=1, source_target_pairs={{0,1},{1,0},{2,3},{3,2},{4,5},{5,4},{6,7},{7,6},{8,9},{9,8},{10,11... | collective-permute-start | bytes 393224 | tf_op jit(solution)/shard_map/ppermute | solution.py:457

commit v4 on v3

--- a/solution.py
+++ b/solution.py
@@ -13,6 +13,7 @@
 FACES = 4
 SLOT = 2
 ROWS = FACES * V
+PIECES = 4
 
 relax_weight = 0.8
 
@@ -22,13 +23,14 @@
 PARAMS = pltpu.CompilerParams(vmem_limit_bytes=24 * 1024 * 1024)
 
 
-def call(kernel, out_shape, in_specs, args, scratch=(), flops=0, moved=512 * 1024):
-    single = not isinstance(out_shape, list)
+def call(
+    kernel, out_shape, in_specs, args, out_specs=None, scratch=(), flops=0, moved=512 * 1024
+):
     return pl.pallas_call(
         kernel,
         out_shape=out_shape,
         in_specs=in_specs,
-        out_specs=VMEM if single else [VMEM] * len(out_shape),
+        out_specs=out_specs or [VMEM] * len(out_shape),
         scratch_shapes=list(scratch),
         compiler_params=PARAMS,
         cost_estimate=pl.CostEstimate(flops=flops, bytes_accessed=moved, transcendentals=0),
@@ -51,8 +53,42 @@
     return (0, rows - 1)
 
 
+def face_halves(tiles):
+    upper = lax.broadcasted_iota(jnp.int32, tiles[0].shape, 0) < V
+    above, below = [], []
+    for tile in tiles:
+        other = pltpu.roll(tile, V, 0)
+        above += [tile, other]
+        below += [other, tile]
+    return upper, above, below
+
+
+def send_pieces(block, send_hbm, sems, fill):
+    pieces = sems.shape[0]
+    size = block.shape[0] // pieces
+    copies = []
+    for piece in range(pieces):
+        for group in range(piece * size, (piece + 1) * size):
+            block[group] = fill(group)
+        part = pl.ds(piece * size, size)
+        copies.append(pltpu.make_async_copy(block.at[part], send_hbm.at[part], sems.at[piece]))
+        copies[-1].start()
+    return copies
+
+
 def first_kernel(
-    faces_hbm, field_hbm, send_ref, strips_ref, inner_ref, outer_ref, faces, edges, scratch, sems
+    faces_hbm,
+    field_hbm,
+    send_hbm,
+    strips_ref,
+    inner_ref,
+    outer_ref,
+    faces,
+    edges,
+    choices,
+    block,
+    sems,
+    send_sems,
 ):
     rows = field_hbm.shape[2]
     tile = edges.shape[3]
@@ -73,29 +109,36 @@
     for plane in range(CX):
         for side, row in enumerate((0, tile - 1)):
             for var in range(V):
-                value = edges[side, var, plane, row : row + 1, :]
-                scratch[plane * 2 + side, var : var + 1, :] = value
                 to = side * V + var
-                strips_ref[plane, to : to + 1, :] = value
-    for group in range(send_ref.shape[0]):
-        for slot in range(SLOT):
-            send_ref[group, slot * V : (slot + 1) * V, :] = scratch[faces[slot, group]]
-    for copy in copies[3:]:
+                strips_ref[plane, to : to + 1, :] = edges[side, var, plane, row : row + 1, :]
+    upper, above, below = face_halves([strips_ref[plane] for plane in range(CX)])
+    for face in range(FACES):
+        for other in range(FACES):
+            choices[face * FACES + other] = jnp.where(upper, above[face], below[other])
+
+    def fill(group):
+        return choices[faces[0, group] * FACES + faces[1, group]]
+
+    for copy in send_pieces(block, send_hbm, send_sems, fill) + copies[3:]:
         copy.wait()
 
 
 def first_part(faces, field):
     groups, (rows, z) = faces.shape[1], field.shape[2:]
+    shape = (groups, SLOT * V, z)
     return call(
         first_kernel,
-        [f32(groups, SLOT * V, z), f32(CX, 2 * V, z), f32(V, rows, z), f32(V, rows, z)],
+        [f32(*shape), f32(CX, 2 * V, z), f32(V, rows, z), f32(V, rows, z)],
         [HBM, HBM],
         in_hbm(faces, field),
+        out_specs=[HBM, VMEM, VMEM, VMEM],
         scratch=[
             pltpu.SMEM(faces.shape, jnp.int32),
             pltpu.VMEM((2, V, CX, 8, z), jnp.float32),
-            pltpu.VMEM((FACES, V, z), jnp.float32),
+            pltpu.VMEM((FACES * FACES, SLOT * V, z), jnp.float32),
+            pltpu.VMEM(shape, jnp.float32),
             pltpu.SemaphoreType.DMA((5,)),
+            pltpu.SemaphoreType.DMA((PIECES,)),
         ],
     )
 
@@ -120,12 +163,12 @@
 
 
 def setup_kernel(
-    source_ref,
     live_ref,
-    target_ref,
-    stencil_ref,
-    weight_ref,
+    source_hbm,
     faces_hbm,
+    stencil_hbm,
+    target_hbm,
+    weight_hbm,
     right_hbm,
     conductivity_hbm,
     inverse_hbm,
@@ -136,17 +179,30 @@
     conductivity_ref,
     inverse_ref,
     edge_ref,
+    source_ref,
     faces_ref,
+    stencil_ref,
+    target_ref,
+    weight_ref,
     sems,
 ):
+    pairs = (
+        (source_hbm, source_ref),
+        (faces_hbm, faces_ref),
+        (stencil_hbm, stencil_ref),
+        (target_hbm, target_ref),
+        (weight_hbm, weight_ref),
+        (right_hbm, right_ref),
+        (conductivity_hbm, conductivity_ref),
+        (inverse_hbm, inverse_ref),
+    )
     copies = [
-        pltpu.make_async_copy(faces_hbm, faces_ref, sems.at[0]),
-        pltpu.make_async_copy(right_hbm, right_ref, sems.at[1]),
-        pltpu.make_async_copy(conductivity_hbm, conductivity_ref, sems.at[2]),
-        pltpu.make_async_copy(inverse_hbm, inverse_ref, sems.at[3]),
+        pltpu.make_async_copy(here, there, sems.at[at]) for at, (here, there) in enumerate(pairs)
     ]
     for copy in copies:
         copy.start()
+    for copy in copies[:5]:
+        copy.wait()
     entries = target_ref.shape[1]
     groups = mask_ref.shape[0]
     columns = matrix_ref.shape[1]
@@ -155,34 +211,30 @@
     chosen = (row_ids // V == target_ref[...]) & (entry_ids < live_ref[0, 0])
     place = lax.broadcasted_iota(jnp.int32, (entries, columns), 0) + SLOT * source_ref[0, 0]
     place = jnp.where(place >= SLOT * groups, place - SLOT * groups, place)
-    column_ids = lax.broadcasted_iota(jnp.int32, (entries, columns), 1)
-    matrix = jnp.zeros((V * ROWS, columns), jnp.float32)
+    shift = lax.broadcasted_iota(jnp.int32, (entries, columns), 1) - place * V
+    matrix = jnp.zeros(matrix_ref.shape, jnp.float32)
     for col in range(V):
         spread = jnp.concatenate(
             [jnp.where(chosen, weight_ref[var, col : col + 1, :], 0.0) for var in range(V)],
             axis=0,
         )
-        order = (column_ids == place * V + col).astype(jnp.float32)
+        high = spread.astype(jnp.bfloat16)
+        low = (spread - high.astype(jnp.float32)).astype(jnp.bfloat16)
+        order = (shift == col).astype(jnp.float32).astype(jnp.bfloat16)
         matrix = matrix + jnp.dot(
-            spread,
-            order,
-            precision=lax.Precision.HIGHEST,
-            preferred_element_type=jnp.float32,
+            jnp.concatenate([high, low], axis=0), order, preferred_element_type=jnp.float32
         )
-    high = matrix.astype(jnp.bfloat16)
-    matrix_ref[: V * ROWS, :] = high
-    matrix_ref[V * ROWS :, :] = (matrix - high.astype(jnp.float32)).astype(jnp.bfloat16)
+    matrix_ref[...] = matrix.astype(jnp.bfloat16)
     for direction in range(6):
         for var in range(V):
             for col in range(V):
                 coefs_ref[direction, var, col] = jnp.full(
                     coefs_ref.shape[3:], stencil_ref[var, col, direction], jnp.float32
                 )
-    copies[0].wait()
-    tile_rows = lax.broadcasted_iota(jnp.int32, mask_ref.shape[1:], 0)
+    upper = lax.broadcasted_iota(jnp.int32, mask_ref.shape[1:], 0) < V
     for group in range(groups):
-        mask_ref[group] = jnp.where(tile_rows < V, faces_ref[0, group], faces_ref[1, group])
-    for copy in copies[1:]:
+        mask_ref[group] = jnp.where(upper, faces_ref[0, group], faces_ref[1, group])
+    for copy in copies[5:]:
         copy.wait()
     for plane in range(CX):
         for side, row in enumerate(edge_rows(inverse_ref.shape[3])):
@@ -194,8 +246,10 @@
                     )
 
 
-def setup_part(source, live, target, stencil, weight, faces, right, cond, inverse):
+def setup_part(live, source, faces, stencil, target, weight, right, cond, inverse):
     groups, z = faces.shape[1], right.shape[-1]
+    scalars = [pltpu.SMEM(array.shape, array.dtype) for array in (source, faces, stencil)]
+    vectors = [pltpu.VMEM(array.shape, array.dtype) for array in (target, weight)]
     return call(
         setup_kernel,
         [
@@ -207,9 +261,9 @@
             f32(*inverse.shape),
             f32(V, CX, 2 * V, z),
         ],
-        [SMEM, SMEM, VMEM, SMEM, VMEM, HBM, HBM, HBM, HBM],
-        (source, live, target, stencil, weight, *in_hbm(faces, right, cond, inverse)),
-        scratch=[pltpu.SMEM(faces.shape, jnp.int32), pltpu.SemaphoreType.DMA((4,))],
+        [SMEM] + [HBM] * 8,
+        (live, *in_hbm(source, faces, stencil, target, weight, right, cond, inverse)),
+        scratch=[*scalars, *vectors, pltpu.SemaphoreType.DMA((8,))],
     )
 
 
@@ -362,21 +416,23 @@
 
 
 def strip_kernel(
-    matrix_ref, edge_ref, strips_ref, got_ref, mask_ref, send_ref, new_ref
+    matrix_ref, edge_ref, strips_ref, got_ref, mask_ref, send_hbm, new_ref, block, sems
 ):
     tiles = new_strips(matrix_ref, edge_ref, strips_ref, got_ref)
-    upper = lax.broadcasted_iota(jnp.int32, tiles[0].shape, 0) < V
-    faces = []
     for plane, tile in enumerate(tiles):
         new_ref[plane] = tile
-        other = pltpu.roll(tile, V, 0)
-        faces += [jnp.where(upper, tile, other), jnp.where(upper, other, tile)]
-    for group in range(send_ref.shape[0]):
+    upper, above, below = face_halves(tiles)
+    faces = [jnp.where(upper, above[face], below[face]) for face in range(FACES)]
+
+    def fill(group):
         mask = mask_ref[group]
         value = faces[FACES - 1]
         for face in range(FACES - 1):
             value = jnp.where(mask == face, faces[face], value)
-        send_ref[group] = value
+        return value
+
+    for copy in send_pieces(block, send_hbm, sems, fill):
+        copy.wait()
 
 
 def strip_part(matrix, edge, strips, got, mask):
@@ -385,32 +441,58 @@
         [f32(*got.shape), f32(*strips.shape)],
         [VMEM] * 5,
         (matrix, edge, strips, got, mask),
+        out_specs=[HBM, VMEM],
+        scratch=[pltpu.VMEM(got.shape, jnp.float32), pltpu.SemaphoreType.DMA((PIECES,))],
     )
 
 
 def last_kernel(
-    matrix_ref, edge_ref, strips_ref, got_ref, inner_ref, outer_ref, out_ref
+    matrix_ref, edge_ref, strips_ref, got_ref, inner_ref, outer_ref, out_hbm, edges, sems
 ):
     rows = inner_ref.shape[1]
+    tile = edges.shape[3]
     at = inner_plane()
+    middle = pl.ds(tile, rows - 2 * tile)
+    copies = [
+        pltpu.make_async_copy(
+            ref.at[:, middle], out_hbm.at[:, plane, middle], sems.at[number]
+        )
+        for number, (ref, plane) in enumerate(((inner_ref, at), (outer_ref, 1 - at)))
+    ]
+    for copy in copies:
+        copy.start()
+    starts = (0, rows - tile)
     for ref, plane in ((inner_ref, at), (outer_ref, 1 - at)):
-        for var in range(V):
-            out_ref[var, plane] = ref[var]
+        for side, start in enumerate(starts):
+            for var in range(V):
+                edges[side, var, plane] = ref[var, start : start + tile, :]
     tiles = new_strips(matrix_ref, edge_ref, strips_ref, got_ref)
-    for plane, tile in enumerate(tiles):
-        for side, row in enumerate(edge_rows(rows)):
+    for plane, value in enumerate(tiles):
+        for side, row in enumerate((0, tile - 1)):
             for var in range(V):
                 here = side * V + var
-                out_ref[var, plane, row : row + 1, :] = tile[here : here + 1]
+                edges[side, var, plane, row : row + 1, :] = value[here : here + 1]
+    for side, start in enumerate(starts):
+        copies.append(
+            pltpu.make_async_copy(
+                edges.at[side], out_hbm.at[:, :, pl.ds(start, tile)], sems.at[2 + side]
+            )
+        )
+        copies[-1].start()
+    for copy in copies:
+        copy.wait()
 
 
 def last_part(matrix, edge, strips, got, inner, outer):
+    rows, z = inner.shape[1:]
     return call(
         last_kernel,
-        f32(V, CX, *inner.shape[1:]),
+        [f32(V, CX, rows, z)],
         [VMEM] * 6,
         (matrix, edge, strips, got, inner, outer),
-    )
+        out_specs=[HBM],
+        scratch=[pltpu.VMEM((2, V, CX, 8, z), jnp.float32), pltpu.SemaphoreType.DMA((4,))],
+    )[0]
 
 
 def per_device(
@@ -440,12 +522,12 @@
 
     send, new, inner, outer = first_part(faces, field)
     matrix, mask, coefs, right, cond, inverse, edge = setup_part(
+        live_count,
         coupling_source[0],
-        live_count,
+        faces,
+        coefs,
         coupling_target[0],
-        coefs,
         weight,
-        faces,
         right,
         cond,
         inverse,

time: 80.3 us -> 78.8 us (0.981)
  starting transfers between devices: 51.7 us -> 50.4 us
  waiting for transfers between devices: 17.9 us -> 19.2 us
  Pallas kernels: 8.68 us -> 7.83 us
    all_to_all x3, waiting for transfers between devices: 17.1 us -> 18.4 us  [per_device(): got = lax.all_to_all(send, 'dom', 0, 0, tiled=True)]
    all_to_all x3, starting transfers between devices: 29.8 us -> 28.5 us  [per_device(): got = lax.all_to_all(send, 'dom', 0, 0, tiled=True)]
    pallas_call x17, Pallas kernels: 8.68 us -> 7.83 us  [call(): pl.pallas_call(kernel, out_shape=out_shape, in_specs=in_specs, out_specs=...]
  transfers between devices with their start and end apart: 9 -> 9, of which waited for: 5 -> 5; matrix products, arithmetic and copies ran while one was open for 0% -> 0% of each run, Pallas kernels for 5% -> 4%
where the time goes in v4:
time: 78.8 us; the launch traced here: 78.3 us
  starting transfers between devices  50.4 us (64%)
  waiting for transfers between devices  19.2 us (24%)
  Pallas kernels  7.83 us (10%)
  between operations  0.85 us (1%)
    all_to_all x3, starting transfers between devices, per_device(): got = lax.all_to_all(send, 'dom', 0, 0, tiled=True)  28.5 us
    all_to_all x3, waiting for transfers between devices, per_device(): got = lax.all_to_all(send, 'dom', 0, 0, tiled=True)  18.4 us
    ppermute x3, starting transfers between devices, per_device(): from_core = lax.ppermute(inner, 'within', core_swap)  16.2 us
    pallas_call x17, Pallas kernels, call(): pl.pallas_call(kernel, out_shape=out_shape, in_specs=in_specs, out_specs=...  7.83 us
    ppermute x3, starting transfers between devices, per_device(): from_chip = lax.ppermute(outer, 'within', chip_swap)  5.76 us
  transfers between devices with their start and end apart: 9, of which 5 were waited for; matrix products, arithmetic and copies ran while one was open for 0% of the time, Pallas kernels for 4%

profile of v4, /device:TPU:256, one launch (start us, length us, event | category | flops | bytes accessed | tf_op | source)
XLA Modules:
  0.0 78.3 jit_solution(7103239083512048681)
XLA Ops:
  0.0 1.6 %shard_map.101 = (f32[64,8,128]{2,1,0:T(8,128)}, f32[2,8,128]{2,1,0:T(8,128)S(1)}, f32[4,64,128]{2,1,0:T(8,128)S(1)}, f32[4,64,128]{2,1,0:T(8,128)S(1)}) custom-call(s32[2,64]{1,0:T(2,128)} %bitcast.22, f32[4,2,64,128]{3,2,1,0:T(8,128)} %bitcast.18), custom_call_target="tpu_custom_call" | custom-call | bytes 524288 | tf_op jit(solution)/shard_map/pallas_call | solution.py:29
  1.6 13.5 %all-to-all-start = ((f32[64,8,128]{2,1,0:T(8,128)}), f32[64,8,128]{2,1,0:T(8,128)S(1)}, u32[]{:S(2)}, u32[]{:S(2)}) async-start(f32[64,8,128]{2,1,0:T(8,128)} %get-tuple-element.59), calls=%async_computation | async-start | bytes 524288 | tf_op jit(solution)/shard_map/all_to_all | solution.py:536
  15.1 1.9 %collective-permute-start.1 = (f32[4,64,128]{2,1,0:T(8,128)S(1)}, f32[4,64,128]{2,1,0:T(8,128)S(1)}, u32[]{:S(2)}, u32[]{:S(2)}) collective-permute-start(f32[4,64,128]{2,1,0:T(8,128)S(1)} %get-tuple-element.51.outer_ref.here_ref), channel_id=1, source_target_pairs={{1,2},{3,4},{5,6},{7,8},{9,10},{11,12},{13,14},{2,1},{4,3},{6,5},{... | collective-permute-start | bytes 393224 | tf_op jit(solution)/shard_map/ppermute | solution.py:538
  17.1 5.3 %collective-permute-start = (f32[4,64,128]{2,1,0:T(8,128)S(1)}, f32[4,64,128]{2,1,0:T(8,128)S(1)}, u32[]{:S(2)}, u32[]{:S(2)}) collective-permute-start(f32[4,64,128]{2,1,0:T(8,128)S(1)} %get-tuple-element.50.inner_ref.here_ref), channel_id=1, source_target_pairs={{0,1},{1,0},{2,3},{3,2},{4,5},{5,4},{6,7},{7,6},{8,9},{9,8},{10,11... | collective-permute-start | bytes 393224 | tf_op jit(solution)/shard_map/ppermute | solution.py:539
  23.0 1.5 %shard_map.100 = (bf16[128,512]{1,0:T(8,128)(2,1)S(1)}, s32[64,8,128]{2,1,0:T(8,128)S(1)}, f32[6,4,4,8,128]{4,3,2,1,0:T(8,128)S(1)}, f32[4,2,64,128]{3,2,1,0:T(8...) custom-call(s32[1,1]{1,0:T(1,128)S(6)} %copy.11.live_ref, ...), custom_call_target="tpu_custom_call" | custom-call | bytes 524288 | tf_op jit(solution)/shard_map/pallas_call | solution.py:29
  24.5 0.4 shard_map.103
  24.9 0.0 collective-permute-done.1.outside_ref
  25.0 0.1 shard_map.104
  25.1 0.0 collective-permute-done.outside_ref
  25.1 0.1 shard_map.105
  25.2 4.9 %all-to-all-done.got_ref = f32[64,8,128]{2,1,0:T(8,128)S(1)} async-done(((f32[64,8,128]{2,1,0:T(8,128)}), f32[64,8,128]{2,1,0:T(8,128)S(1)}, u32[]{:S(2)}, u32[]{:S(2)}) %all-to-all-start) | async-done | bytes 262176 | tf_op jit(solution)/shard_map/all_to_all | solution.py:536
  30.1 0.9 %shard_map.106 = (f32[64,8,128]{2,1,0:T(8,128)}, f32[2,8,128]{2,1,0:T(8,128)S(1)}) custom-call(bf16[128,512]{1,0:T(8,128)(2,1)S(1)} %get-tuple-element.44.matrix_ref, f32[4,2,8,128]{3,2,1,0:T(8,128)S(1)} %get-tuple-element.45.edge_ref, f32[2,8,128]{2,1,0:T(8,128)S(1)} %get-tuple-element.58.strips_ref, f32[64,8,128]{2,1,0:T(8,128)S(1)} %all-to-all-done.got_ref, ...), custom_call_target="tpu_custom_call" | custom-call | bytes 524288 | tf_op jit(solution)/shard_map/pallas_call | solution.py:29
  31.0 7.8 %all-to-all-start.1 = ((f32[64,8,128]{2,1,0:T(8,128)}), f32[64,8,128]{2,1,0:T(8,128)S(1)}, u32[]{:S(2)}, u32[]{:S(2)}) async-start(f32[64,8,128]{2,1,0:T(8,128)} %get-tuple-element.70), calls=%async_computation.1 | async-start | bytes 524288 | tf_op jit(solution)/shard_map/all_to_all | solution.py:536
  38.9 1.9 %collective-permute-start.3 = (f32[4,64,128]{2,1,0:T(8,128)S(1)}, f32[4,64,128]{2,1,0:T(8,128)S(1)}, u32[]{:S(2)}, u32[]{:S(2)}) collective-permute-start(f32[4,64,128]{2,1,0:T(8,128)S(1)} %get-tuple-element.65.outer_ref.here_ref), channel_id=1, source_target_pairs={{1,2},{3,4},{5,6},{7,8},{9,10},{11,12},{13,14},{2,1},{4,3},{6,5},{... | collective-permute-start | bytes 393224 | tf_op jit(solution)/shard_map/ppermute | solution.py:538
  40.8 6.5 %collective-permute-start.2 = (f32[4,64,128]{2,1,0:T(8,128)S(1)}, f32[4,64,128]{2,1,0:T(8,128)S(1)}, u32[]{:S(2)}, u32[]{:S(2)}) collective-permute-start(f32[4,64,128]{2,1,0:T(8,128)S(1)} %get-tuple-element.64.inner_ref.here_ref), channel_id=1, source_target_pairs={{0,1},{1,0},{2,3},{3,2},{4,5},{5,4},{6,7},{7,6},{8,9},{9,8},{10,11... | collective-permute-start | bytes 393224 | tf_op jit(solution)/shard_map/ppermute | solution.py:539
  47.3 0.4 shard_map.108
  47.8 0.0 collective-permute-done.3.outside_ref
  47.8 0.1 shard_map.109
  47.9 0.4 collective-permute-done.2.outside_ref
  48.3 0.1 shard_map.110
  48.4 5.6 %all-to-all-done.1.got_ref = f32[64,8,128]{2,1,0:T(8,128)S(1)} async-done(((f32[64,8,128]{2,1,0:T(8,128)}), f32[64,8,128]{2,1,0:T(8,128)S(1)}, u32[]{:S(2)}, u32[]{:S(2)}) %all-to-all-start.1) | async-done | bytes 262176 | tf_op jit(solution)/shard_map/all_to_all | solution.py:536
  54.0 0.9 %shard_map.111 = (f32[64,8,128]{2,1,0:T(8,128)}, f32[2,8,128]{2,1,0:T(8,128)S(1)}) custom-call(bf16[128,512]{1,0:T(8,128)(2,1)S(1)} %get-tuple-element.44.matrix_ref, f32[4,2,8,128]{3,2,1,0:T(8,128)S(1)} %get-tuple-element.45.edge_ref, f32[2,8,128]{2,1,0:T(8,128)S(1)} %get-tuple-element.69.strips_ref, f32[64,8,128]{2,1,0:T(8,128)S(1)} %all-to-all-done.1.got_ref, ...), custom_call_target="tpu_custom_call" | custom-call | bytes 524288 | tf_op jit(solution)/shard_map/pallas_call | solution.py:29
  54.9 7.2 %all-to-all-start.2 = ((f32[64,8,128]{2,1,0:T(8,128)}), f32[64,8,128]{2,1,0:T(8,128)S(1)}, u32[]{:S(2)}, u32[]{:S(2)}) async-start(f32[64,8,128]{2,1,0:T(8,128)} %get-tuple-element.80), calls=%async_computation.2 | async-start | bytes 524288 | tf_op jit(solution)/shard_map/all_to_all | solution.py:536
  62.1 1.9 %collective-permute-start.5 = (f32[4,64,128]{2,1,0:T(8,128)S(1)}, f32[4,64,128]{2,1,0:T(8,128)S(1)}, u32[]{:S(2)}, u32[]{:S(2)}) collective-permute-start(f32[4,64,128]{2,1,0:T(8,128)S(1)} %get-tuple-element.75.outer_ref.here_ref), channel_id=1, source_target_pairs={{1,2},{3,4},{5,6},{7,8},{9,10},{11,12},{13,14},{2,1},{4,3},{6,5},{... | collective-permute-start | bytes 393224 | tf_op jit(solution)/shard_map/ppermute | solution.py:538
  64.1 4.4 %collective-permute-start.4 = (f32[4,64,128]{2,1,0:T(8,128)S(1)}, f32[4,64,128]{2,1,0:T(8,128)S(1)}, u32[]{:S(2)}, u32[]{:S(2)}) collective-permute-start(f32[4,64,128]{2,1,0:T(8,128)S(1)} %get-tuple-element.74.inner_ref.here_ref), channel_id=1, source_target_pairs={{0,1},{1,0},{2,3},{3,2},{4,5},{5,4},{6,7},{7,6},{8,9},{9,8},{10,11... | collective-permute-start | bytes 393224 | tf_op jit(solution)/shard_map/ppermute | solution.py:539
  68.5 0.4 shard_map.113
  68.9 0.0 collective-permute-done.5.outside_ref
  68.9 0.1 shard_map.114
  69.0 0.4 collective-permute-done.4.outside_ref
  69.4 0.1 shard_map.115
  69.5 7.9 %all-to-all-done.2.got_ref = f32[64,8,128]{2,1,0:T(8,128)S(1)} async-done(((f32[64,8,128]{2,1,0:T(8,128)}), f32[64,8,128]{2,1,0:T(8,128)S(1)}, u32[]{:S(2)}, u32[]{:S(2)}) %all-to-all-start.2) | async-done | bytes 262176 | tf_op jit(solution)/shard_map/all_to_all | solution.py:536
  77.4 0.9 %shard_map.116 = f32[4,2,64,128]{3,2,1,0:T(8,128)} custom-call(bf16[128,512]{1,0:T(8,128)(2,1)S(1)} %get-tuple-element.44.matrix_ref, f32[4,2,8,128]{3,2,1,0:T(8,128)S(1)} %get-tuple-element.45.edge_ref, f32[2,8,128]{2,1,0:T(8,128)S(1)} %get-tuple-element.79.strips_ref, f32[64,8,128]{2,1,0:T(8,128)S(1)} %all-to-all-done.2.got_ref, ...), custom_call_target="tpu_custom_call" | custom-call | bytes 524288 | tf_op jit(solution)/shard_map/pallas_call | solution.py:29
  (3 shorter events, 0.1 us)
Async XLA Ops:
  1.6 28.5 %all-to-all-start = ((f32[64,8,128]{2,1,0:T(8,128)}), f32[64,8,128]{2,1,0:T(8,128)S(1)}, u32[]{:S(2)}, u32[]{:S(2)}) async-start(f32[64,8,128]{2,1,0:T(8,128)} %get-tuple-element.59), calls=%async_computation | async-start | bytes 524288 | tf_op jit(solution)/shard_map/all_to_all | solution.py:536
  15.1 9.8 %collective-permute-start.1 = (f32[4,64,128]{2,1,0:T(8,128)S(1)}, f32[4,64,128]{2,1,0:T(8,128)S(1)}, u32[]{:S(2)}, u32[]{:S(2)}) collective-permute-start(f32[4,64,128]{2,1,0:T(8,128)S(1)} %get-tuple-element.51.outer_ref.here_ref), channel_id=1, source_target_pairs={{1,2},{3,4},{5,6},{7,8},{9,10},{11,12},{13,14},{2,1},{4,3},{6,5},{... | collective-permute-start | bytes 393224 | tf_op jit(solution)/shard_map/ppermute | solution.py:538
  17.1 8.0 %collective-permute-start = (f32[4,64,128]{2,1,0:T(8,128)S(1)}, f32[4,64,128]{2,1,0:T(8,128)S(1)}, u32[]{:S(2)}, u32[]{:S(2)}) collective-permute-start(f32[4,64,128]{2,1,0:T(8,128)S(1)} %get-tuple-element.50.inner_ref.here_ref), channel_id=1, source_target_pairs={{0,1},{1,0},{2,3},{3,2},{4,5},{5,4},{6,7},{7,6},{8,9},{9,8},{10,11... | collective-permute-start | bytes 393224 | tf_op jit(solution)/shard_map/ppermute | solution.py:539
  31.0 22.9 %all-to-all-start.1 = ((f32[64,8,128]{2,1,0:T(8,128)}), f32[64,8,128]{2,1,0:T(8,128)S(1)}, u32[]{:S(2)}, u32[]{:S(2)}) async-start(f32[64,8,128]{2,1,0:T(8,128)} %get-tuple-element.70), calls=%async_computation.1 | async-start | bytes 524288 | tf_op jit(solution)/shard_map/all_to_all | solution.py:536
  38.9 8.9 %collective-permute-start.3 = (f32[4,64,128]{2,1,0:T(8,128)S(1)}, f32[4,64,128]{2,1,0:T(8,128)S(1)}, u32[]{:S(2)}, u32[]{:S(2)}) collective-permute-start(f32[4,64,128]{2,1,0:T(8,128)S(1)} %get-tuple-element.65.outer_ref.here_ref), channel_id=1, source_target_pairs={{1,2},{3,4},{5,6},{7,8},{9,10},{11,12},{13,14},{2,1},{4,3},{6,5},{... | collective-permute-start | bytes 393224 | tf_op jit(solution)/shard_map/ppermute | solution.py:538
  40.8 7.5 %collective-permute-start.2 = (f32[4,64,128]{2,1,0:T(8,128)S(1)}, f32[4,64,128]{2,1,0:T(8,128)S(1)}, u32[]{:S(2)}, u32[]{:S(2)}) collective-permute-start(f32[4,64,128]{2,1,0:T(8,128)S(1)} %get-tuple-element.64.inner_ref.here_ref), channel_id=1, source_target_pairs={{0,1},{1,0},{2,3},{3,2},{4,5},{5,4},{6,7},{7,6},{8,9},{9,8},{10,11... | collective-permute-start | bytes 393224 | tf_op jit(solution)/shard_map/ppermute | solution.py:539
  54.9 22.5 %all-to-all-start.2 = ((f32[64,8,128]{2,1,0:T(8,128)}), f32[64,8,128]{2,1,0:T(8,128)S(1)}, u32[]{:S(2)}, u32[]{:S(2)}) async-start(f32[64,8,128]{2,1,0:T(8,128)} %get-tuple-element.80), calls=%async_computation.2 | async-start | bytes 524288 | tf_op jit(solution)/shard_map/all_to_all | solution.py:536
  62.1 6.8 %collective-permute-start.5 = (f32[4,64,128]{2,1,0:T(8,128)S(1)}, f32[4,64,128]{2,1,0:T(8,128)S(1)}, u32[]{:S(2)}, u32[]{:S(2)}) collective-permute-start(f32[4,64,128]{2,1,0:T(8,128)S(1)} %get-tuple-element.75.outer_ref.here_ref), channel_id=1, source_target_pairs={{1,2},{3,4},{5,6},{7,8},{9,10},{11,12},{13,14},{2,1},{4,3},{6,5},{... | collective-permute-start | bytes 393224 | tf_op jit(solution)/shard_map/ppermute | solution.py:538
  64.1 5.4 %collective-permute-start.4 = (f32[4,64,128]{2,1,0:T(8,128)S(1)}, f32[4,64,128]{2,1,0:T(8,128)S(1)}, u32[]{:S(2)}, u32[]{:S(2)}) collective-permute-start(f32[4,64,128]{2,1,0:T(8,128)S(1)} %get-tuple-element.74.inner_ref.here_ref), channel_id=1, source_target_pairs={{0,1},{1,0},{2,3},{3,2},{4,5},{5,4},{6,7},{7,6},{8,9},{9,8},{10,11... | collective-permute-start | bytes 393224 | tf_op jit(solution)/shard_map/ppermute | solution.py:539

commit v5 on v4

--- a/solution.py
+++ b/solution.py
@@ -68,8 +68,8 @@
     size = block.shape[0] // pieces
     copies = []
     for piece in range(pieces):
-        for group in range(piece * size, (piece + 1) * size):
-            block[group] = fill(group)
+        for place in range(piece * size, (piece + 1) * size):
+            block[place] = fill(block.shape[0] - 1 - place)
         part = pl.ds(piece * size, size)
         copies.append(pltpu.make_async_copy(block.at[part], send_hbm.at[part], sems.at[piece]))
         copies[-1].start()
@@ -211,6 +211,7 @@
     chosen = (row_ids // V == target_ref[...]) & (entry_ids < live_ref[0, 0])
     place = lax.broadcasted_iota(jnp.int32, (entries, columns), 0) + SLOT * source_ref[0, 0]
     place = jnp.where(place >= SLOT * groups, place - SLOT * groups, place)
+    place = SLOT * (groups - 1 - place // SLOT) + lax.rem(place, SLOT)
     shift = lax.broadcasted_iota(jnp.int32, (entries, columns), 1) - place * V
     matrix = jnp.zeros(matrix_ref.shape, jnp.float32)
     for col in range(V):
@@ -532,8 +533,9 @@
         cond,
         inverse,
     )
+    members = [list(reversed(range(lax.axis_size("dom"))))]
     for sweep in range(SWEEPS):
-        got = lax.all_to_all(send, "dom", 0, 0, tiled=True)
+        got = lax.all_to_all(send, "dom", 0, 0, tiled=True, axis_index_groups=members)
         inner, outer = patch_part(new, inner, outer)
         from_chip = lax.ppermute(outer, "within", chip_swap)
         from_core = lax.ppermute(inner, "within", core_swap)

time: 78.8 us -> 74.9 us (0.951)
  waiting for transfers between devices: 19.2 us -> 5.95 us
  starting transfers between devices: 50.4 us -> 59.8 us
    all_to_all x3, waiting for transfers between devices: 18.4 us -> 5.14 us  [per_device(): lax.all_to_all(send, 'dom', 0, 0, tiled=True, axis_index_groups=members)]
    all_to_all x3, starting transfers between devices: 28.5 us -> 37.8 us  [per_device(): lax.all_to_all(send, 'dom', 0, 0, tiled=True, axis_index_groups=members)]
  transfers between devices with their start and end apart: 9 -> 9, of which waited for: 5 -> 5; matrix products, arithmetic and copies ran while one was open for 0% -> 0% of each run, Pallas kernels for 4% -> 5%
where the time goes in v5:
time: 74.9 us; the launch traced here: 74.4 us
  starting transfers between devices  59.8 us (80%)
  Pallas kernels  7.83 us (10%)
  waiting for transfers between devices  5.95 us (8%)
  between operations  0.85 us (1%)
    all_to_all x3, starting transfers between devices, per_device(): lax.all_to_all(send, 'dom', 0, 0, tiled=True, axis_index_groups=members)  37.8 us
    ppermute x3, starting transfers between devices, per_device(): from_core = lax.ppermute(inner, 'within', core_swap)  16.2 us
    pallas_call x17, Pallas kernels, call(): pl.pallas_call(kernel, out_shape=out_shape, in_specs=in_specs, out_specs=...  7.83 us
    ppermute x3, starting transfers between devices, per_device(): from_chip = lax.ppermute(outer, 'within', chip_swap)  5.76 us
    all_to_all x3, waiting for transfers between devices, per_device(): lax.all_to_all(send, 'dom', 0, 0, tiled=True, axis_index_groups=members)  5.14 us
  transfers between devices with their start and end apart: 9, of which 5 were waited for; matrix products, arithmetic and copies ran while one was open for 0% of the time, Pallas kernels for 5%

profile of v5, /device:TPU:256, one launch (start us, length us, event | category | flops | bytes accessed | tf_op | source)
XLA Modules:
  0.0 74.4 jit_solution(13360406221560064127)
XLA Ops:
  0.0 1.6 %shard_map.101 = (f32[64,8,128]{2,1,0:T(8,128)}, f32[2,8,128]{2,1,0:T(8,128)S(1)}, f32[4,64,128]{2,1,0:T(8,128)S(1)}, f32[4,64,128]{2,1,0:T(8,128)S(1)}) custom-call(s32[2,64]{1,0:T(2,128)} %bitcast.22, f32[4,2,64,128]{3,2,1,0:T(8,128)} %bitcast.18), custom_call_target="tpu_custom_call" | custom-call | bytes 524288 | tf_op jit(solution)/shard_map/pallas_call | solution.py:29
  1.6 13.9 %all-to-all-start = ((f32[64,8,128]{2,1,0:T(8,128)}), f32[64,8,128]{2,1,0:T(8,128)S(1)}, u32[]{:S(2)}, u32[]{:S(2)}) async-start(f32[64,8,128]{2,1,0:T(8,128)} %get-tuple-element.59), calls=%async_computation | async-start | bytes 524288 | tf_op jit(solution)/shard_map/all_to_all | solution.py:538
  15.6 1.9 %collective-permute-start.1 = (f32[4,64,128]{2,1,0:T(8,128)S(1)}, f32[4,64,128]{2,1,0:T(8,128)S(1)}, u32[]{:S(2)}, u32[]{:S(2)}) collective-permute-start(f32[4,64,128]{2,1,0:T(8,128)S(1)} %get-tuple-element.51.outer_ref.here_ref), channel_id=1, source_target_pairs={{1,2},{3,4},{5,6},{7,8},{9,10},{11,12},{13,14},{2,1},{4,3},{6,5},{... | collective-permute-start | bytes 393224 | tf_op jit(solution)/shard_map/ppermute | solution.py:540
  17.5 5.3 %collective-permute-start = (f32[4,64,128]{2,1,0:T(8,128)S(1)}, f32[4,64,128]{2,1,0:T(8,128)S(1)}, u32[]{:S(2)}, u32[]{:S(2)}) collective-permute-start(f32[4,64,128]{2,1,0:T(8,128)S(1)} %get-tuple-element.50.inner_ref.here_ref), channel_id=1, source_target_pairs={{0,1},{1,0},{2,3},{3,2},{4,5},{5,4},{6,7},{7,6},{8,9},{9,8},{10,11... | collective-permute-start | bytes 393224 | tf_op jit(solution)/shard_map/ppermute | solution.py:541
  23.4 1.5 %shard_map.100 = (bf16[128,512]{1,0:T(8,128)(2,1)S(1)}, s32[64,8,128]{2,1,0:T(8,128)S(1)}, f32[6,4,4,8,128]{4,3,2,1,0:T(8,128)S(1)}, f32[4,2,64,128]{3,2,1,0:T(8...) custom-call(s32[1,1]{1,0:T(1,128)S(6)} %copy.11.live_ref, ...), custom_call_target="tpu_custom_call" | custom-call | bytes 524288 | tf_op jit(solution)/shard_map/pallas_call | solution.py:29
  24.9 0.4 shard_map.103
  25.4 0.0 collective-permute-done.1.outside_ref
  25.4 0.1 shard_map.104
  25.5 0.0 collective-permute-done.outside_ref
  25.5 0.1 shard_map.105
  25.6 0.4 all-to-all-done.got_ref
  26.0 0.9 %shard_map.106 = (f32[64,8,128]{2,1,0:T(8,128)}, f32[2,8,128]{2,1,0:T(8,128)S(1)}) custom-call(bf16[128,512]{1,0:T(8,128)(2,1)S(1)} %get-tuple-element.44.matrix_ref, f32[4,2,8,128]{3,2,1,0:T(8,128)S(1)} %get-tuple-element.45.edge_ref, f32[2,8,128]{2,1,0:T(8,128)S(1)} %get-tuple-element.58.strips_ref, f32[64,8,128]{2,1,0:T(8,128)S(1)} %all-to-all-done.got_ref, ...), custom_call_target="tpu_custom_call" | custom-call | bytes 524288 | tf_op jit(solution)/shard_map/pallas_call | solution.py:29
  27.0 12.3 %all-to-all-start.1 = ((f32[64,8,128]{2,1,0:T(8,128)}), f32[64,8,128]{2,1,0:T(8,128)S(1)}, u32[]{:S(2)}, u32[]{:S(2)}) async-start(f32[64,8,128]{2,1,0:T(8,128)} %get-tuple-element.70), calls=%async_computation.1 | async-start | bytes 524288 | tf_op jit(solution)/shard_map/all_to_all | solution.py:538
  39.3 1.9 %collective-permute-start.3 = (f32[4,64,128]{2,1,0:T(8,128)S(1)}, f32[4,64,128]{2,1,0:T(8,128)S(1)}, u32[]{:S(2)}, u32[]{:S(2)}) collective-permute-start(f32[4,64,128]{2,1,0:T(8,128)S(1)} %get-tuple-element.65.outer_ref.here_ref), channel_id=1, source_target_pairs={{1,2},{3,4},{5,6},{7,8},{9,10},{11,12},{13,14},{2,1},{4,3},{6,5},{... | collective-permute-start | bytes 393224 | tf_op jit(solution)/shard_map/ppermute | solution.py:540
  41.3 6.5 %collective-permute-start.2 = (f32[4,64,128]{2,1,0:T(8,128)S(1)}, f32[4,64,128]{2,1,0:T(8,128)S(1)}, u32[]{:S(2)}, u32[]{:S(2)}) collective-permute-start(f32[4,64,128]{2,1,0:T(8,128)S(1)} %get-tuple-element.64.inner_ref.here_ref), channel_id=1, source_target_pairs={{0,1},{1,0},{2,3},{3,2},{4,5},{5,4},{6,7},{7,6},{8,9},{9,8},{10,11... | collective-permute-start | bytes 393224 | tf_op jit(solution)/shard_map/ppermute | solution.py:541
  47.8 0.4 shard_map.108
  48.2 0.0 collective-permute-done.3.outside_ref
  48.2 0.1 shard_map.109
  48.3 0.4 collective-permute-done.2.outside_ref
  48.7 0.1 shard_map.110
  48.8 1.1 %all-to-all-done.1.got_ref = f32[64,8,128]{2,1,0:T(8,128)S(1)} async-done(((f32[64,8,128]{2,1,0:T(8,128)}), f32[64,8,128]{2,1,0:T(8,128)S(1)}, u32[]{:S(2)}, u32[]{:S(2)}) %all-to-all-start.1) | async-done | bytes 262176 | tf_op jit(solution)/shard_map/all_to_all | solution.py:538
  50.0 0.9 %shard_map.111 = (f32[64,8,128]{2,1,0:T(8,128)}, f32[2,8,128]{2,1,0:T(8,128)S(1)}) custom-call(bf16[128,512]{1,0:T(8,128)(2,1)S(1)} %get-tuple-element.44.matrix_ref, f32[4,2,8,128]{3,2,1,0:T(8,128)S(1)} %get-tuple-element.45.edge_ref, f32[2,8,128]{2,1,0:T(8,128)S(1)} %get-tuple-element.69.strips_ref, f32[64,8,128]{2,1,0:T(8,128)S(1)} %all-to-all-done.1.got_ref, ...), custom_call_target="tpu_custom_call" | custom-call | bytes 524288 | tf_op jit(solution)/shard_map/pallas_call | solution.py:29
  50.9 11.6 %all-to-all-start.2 = ((f32[64,8,128]{2,1,0:T(8,128)}), f32[64,8,128]{2,1,0:T(8,128)S(1)}, u32[]{:S(2)}, u32[]{:S(2)}) async-start(f32[64,8,128]{2,1,0:T(8,128)} %get-tuple-element.80), calls=%async_computation.2 | async-start | bytes 524288 | tf_op jit(solution)/shard_map/all_to_all | solution.py:538
  62.6 1.9 %collective-permute-start.5 = (f32[4,64,128]{2,1,0:T(8,128)S(1)}, f32[4,64,128]{2,1,0:T(8,128)S(1)}, u32[]{:S(2)}, u32[]{:S(2)}) collective-permute-start(f32[4,64,128]{2,1,0:T(8,128)S(1)} %get-tuple-element.75.outer_ref.here_ref), channel_id=1, source_target_pairs={{1,2},{3,4},{5,6},{7,8},{9,10},{11,12},{13,14},{2,1},{4,3},{6,5},{... | collective-permute-start | bytes 393224 | tf_op jit(solution)/shard_map/ppermute | solution.py:540
  64.5 4.4 %collective-permute-start.4 = (f32[4,64,128]{2,1,0:T(8,128)S(1)}, f32[4,64,128]{2,1,0:T(8,128)S(1)}, u32[]{:S(2)}, u32[]{:S(2)}) collective-permute-start(f32[4,64,128]{2,1,0:T(8,128)S(1)} %get-tuple-element.74.inner_ref.here_ref), channel_id=1, source_target_pairs={{0,1},{1,0},{2,3},{3,2},{4,5},{5,4},{6,7},{7,6},{8,9},{9,8},{10,11... | collective-permute-start | bytes 393224 | tf_op jit(solution)/shard_map/ppermute | solution.py:541
  68.9 0.4 shard_map.113
  69.3 0.0 collective-permute-done.5.outside_ref
  69.4 0.1 shard_map.114
  69.5 0.4 collective-permute-done.4.outside_ref
  69.9 0.1 shard_map.115
  70.0 3.6 %all-to-all-done.2.got_ref = f32[64,8,128]{2,1,0:T(8,128)S(1)} async-done(((f32[64,8,128]{2,1,0:T(8,128)}), f32[64,8,128]{2,1,0:T(8,128)S(1)}, u32[]{:S(2)}, u32[]{:S(2)}) %all-to-all-start.2) | async-done | bytes 262176 | tf_op jit(solution)/shard_map/all_to_all | solution.py:538
  73.5 0.9 %shard_map.116 = f32[4,2,64,128]{3,2,1,0:T(8,128)} custom-call(bf16[128,512]{1,0:T(8,128)(2,1)S(1)} %get-tuple-element.44.matrix_ref, f32[4,2,8,128]{3,2,1,0:T(8,128)S(1)} %get-tuple-element.45.edge_ref, f32[2,8,128]{2,1,0:T(8,128)S(1)} %get-tuple-element.79.strips_ref, f32[64,8,128]{2,1,0:T(8,128)S(1)} %all-to-all-done.2.got_ref, ...), custom_call_target="tpu_custom_call" | custom-call | bytes 524288 | tf_op jit(solution)/shard_map/pallas_call | solution.py:29
  (3 shorter events, 0.1 us)
Async XLA Ops:
  1.6 24.4 %all-to-all-start = ((f32[64,8,128]{2,1,0:T(8,128)}), f32[64,8,128]{2,1,0:T(8,128)S(1)}, u32[]{:S(2)}, u32[]{:S(2)}) async-start(f32[64,8,128]{2,1,0:T(8,128)} %get-tuple-element.59), calls=%async_computation | async-start | bytes 524288 | tf_op jit(solution)/shard_map/all_to_all | solution.py:538
  15.6 9.8 %collective-permute-start.1 = (f32[4,64,128]{2,1,0:T(8,128)S(1)}, f32[4,64,128]{2,1,0:T(8,128)S(1)}, u32[]{:S(2)}, u32[]{:S(2)}) collective-permute-start(f32[4,64,128]{2,1,0:T(8,128)S(1)} %get-tuple-element.51.outer_ref.here_ref), channel_id=1, source_target_pairs={{1,2},{3,4},{5,6},{7,8},{9,10},{11,12},{13,14},{2,1},{4,3},{6,5},{... | collective-permute-start | bytes 393224 | tf_op jit(solution)/shard_map/ppermute | solution.py:540
  17.5 8.0 %collective-permute-start = (f32[4,64,128]{2,1,0:T(8,128)S(1)}, f32[4,64,128]{2,1,0:T(8,128)S(1)}, u32[]{:S(2)}, u32[]{:S(2)}) collective-permute-start(f32[4,64,128]{2,1,0:T(8,128)S(1)} %get-tuple-element.50.inner_ref.here_ref), channel_id=1, source_target_pairs={{0,1},{1,0},{2,3},{3,2},{4,5},{5,4},{6,7},{7,6},{8,9},{9,8},{10,11... | collective-permute-start | bytes 393224 | tf_op jit(solution)/shard_map/ppermute | solution.py:541
  27.0 23.0 %all-to-all-start.1 = ((f32[64,8,128]{2,1,0:T(8,128)}), f32[64,8,128]{2,1,0:T(8,128)S(1)}, u32[]{:S(2)}, u32[]{:S(2)}) async-start(f32[64,8,128]{2,1,0:T(8,128)} %get-tuple-element.70), calls=%async_computation.1 | async-start | bytes 524288 | tf_op jit(solution)/shard_map/all_to_all | solution.py:538
  39.3 8.9 %collective-permute-start.3 = (f32[4,64,128]{2,1,0:T(8,128)S(1)}, f32[4,64,128]{2,1,0:T(8,128)S(1)}, u32[]{:S(2)}, u32[]{:S(2)}) collective-permute-start(f32[4,64,128]{2,1,0:T(8,128)S(1)} %get-tuple-element.65.outer_ref.here_ref), channel_id=1, source_target_pairs={{1,2},{3,4},{5,6},{7,8},{9,10},{11,12},{13,14},{2,1},{4,3},{6,5},{... | collective-permute-start | bytes 393224 | tf_op jit(solution)/shard_map/ppermute | solution.py:540
  41.3 7.5 %collective-permute-start.2 = (f32[4,64,128]{2,1,0:T(8,128)S(1)}, f32[4,64,128]{2,1,0:T(8,128)S(1)}, u32[]{:S(2)}, u32[]{:S(2)}) collective-permute-start(f32[4,64,128]{2,1,0:T(8,128)S(1)} %get-tuple-element.64.inner_ref.here_ref), channel_id=1, source_target_pairs={{0,1},{1,0},{2,3},{3,2},{4,5},{5,4},{6,7},{7,6},{8,9},{9,8},{10,11... | collective-permute-start | bytes 393224 | tf_op jit(solution)/shard_map/ppermute | solution.py:541
  50.9 22.6 %all-to-all-start.2 = ((f32[64,8,128]{2,1,0:T(8,128)}), f32[64,8,128]{2,1,0:T(8,128)S(1)}, u32[]{:S(2)}, u32[]{:S(2)}) async-start(f32[64,8,128]{2,1,0:T(8,128)} %get-tuple-element.80), calls=%async_computation.2 | async-start | bytes 524288 | tf_op jit(solution)/shard_map/all_to_all | solution.py:538
  62.6 6.8 %collective-permute-start.5 = (f32[4,64,128]{2,1,0:T(8,128)S(1)}, f32[4,64,128]{2,1,0:T(8,128)S(1)}, u32[]{:S(2)}, u32[]{:S(2)}) collective-permute-start(f32[4,64,128]{2,1,0:T(8,128)S(1)} %get-tuple-element.75.outer_ref.here_ref), channel_id=1, source_target_pairs={{1,2},{3,4},{5,6},{7,8},{9,10},{11,12},{13,14},{2,1},{4,3},{6,5},{... | collective-permute-start | bytes 393224 | tf_op jit(solution)/shard_map/ppermute | solution.py:540
  64.5 5.4 %collective-permute-start.4 = (f32[4,64,128]{2,1,0:T(8,128)S(1)}, f32[4,64,128]{2,1,0:T(8,128)S(1)}, u32[]{:S(2)}, u32[]{:S(2)}) collective-permute-start(f32[4,64,128]{2,1,0:T(8,128)S(1)} %get-tuple-element.74.inner_ref.here_ref), channel_id=1, source_target_pairs={{0,1},{1,0},{2,3},{3,2},{4,5},{5,4},{6,7},{7,6},{8,9},{9,8},{10,11... | collective-permute-start | bytes 393224 | tf_op jit(solution)/shard_map/ppermute | solution.py:541

commit v6 on v5

--- a/solution.py
+++ b/solution.py
@@ -14,6 +14,7 @@
 SLOT = 2
 ROWS = FACES * V
 PIECES = 4
+STAGED = 6
 
 relax_weight = 0.8
 
@@ -79,28 +80,28 @@
 def first_kernel(
     faces_hbm,
     field_hbm,
-    send_hbm,
-    strips_ref,
-    inner_ref,
-    outer_ref,
-    faces,
-    edges,
-    choices,
-    block,
-    sems,
-    send_sems,
-):
+    stencil_hbm,
+    *refs,
+):
+    staged_hbm, refs = refs[:STAGED], refs[STAGED:]
+    send_hbm, strips_ref, inner_ref, outer_ref, mask_ref, coefs_ref = refs[:6]
+    staged, refs = refs[6 : 6 + STAGED], refs[6 + STAGED :]
+    faces, stencil, edges, choices, block, sems, send_sems = refs
     rows = field_hbm.shape[2]
     tile = edges.shape[3]
     at = inner_plane()
+    pairs = [
+        (faces_hbm, faces),
+        (field_hbm.at[:, :, pl.ds(0, tile)], edges.at[0]),
+        (field_hbm.at[:, :, pl.ds(rows - tile, tile)], edges.at[1]),
+        (stencil_hbm, stencil),
+        (field_hbm.at[:, at], inner_ref),
+        (field_hbm.at[:, 1 - at], outer_ref),
+        *zip(staged_hbm, staged),
+    ]
     copies = [
-        pltpu.make_async_copy(faces_hbm, faces, sems.at[0]),
-        pltpu.make_async_copy(field_hbm.at[:, :, pl.ds(0, tile)], edges.at[0], sems.at[1]),
-        pltpu.make_async_copy(
-            field_hbm.at[:, :, pl.ds(rows - tile, tile)], edges.at[1], sems.at[2]
-        ),
-        pltpu.make_async_copy(field_hbm.at[:, at], inner_ref, sems.at[3]),
-        pltpu.make_async_copy(field_hbm.at[:, 1 - at], outer_ref, sems.at[4]),
+        pltpu.make_async_copy(here, there, sems.at[number])
+        for number, (here, there) in enumerate(pairs)
     ]
     for copy in copies:
         copy.start()
@@ -119,25 +120,44 @@
     def fill(group):
         return choices[faces[0, group] * FACES + faces[1, group]]
 
-    for copy in send_pieces(block, send_hbm, send_sems, fill) + copies[3:]:
+    sends = send_pieces(block, send_hbm, send_sems, fill)
+    for group in range(mask_ref.shape[0]):
+        mask_ref[group] = jnp.where(upper, faces[0, group], faces[1, group])
+    copies[3].wait()
+    for direction in range(6):
+        for var in range(V):
+            for col in range(V):
+                coefs_ref[direction, var, col] = jnp.full(
+                    coefs_ref.shape[3:], stencil[var, col, direction], jnp.float32
+                )
+    for copy in sends + copies[4:]:
         copy.wait()
 
 
-def first_part(faces, field):
+def first_part(faces, field, stencil, *staged):
     groups, (rows, z) = faces.shape[1], field.shape[2:]
     shape = (groups, SLOT * V, z)
     return call(
         first_kernel,
-        [f32(*shape), f32(CX, 2 * V, z), f32(V, rows, z), f32(V, rows, z)],
-        [HBM, HBM],
-        in_hbm(faces, field),
-        out_specs=[HBM, VMEM, VMEM, VMEM],
+        [
+            f32(*shape),
+            f32(CX, 2 * V, z),
+            f32(V, rows, z),
+            f32(V, rows, z),
+            jax.ShapeDtypeStruct(shape, jnp.int32),
+            f32(6, V, V, 8, z),
+            *(jax.ShapeDtypeStruct(array.shape, array.dtype) for array in staged),
+        ],
+        [HBM] * (3 + STAGED),
+        in_hbm(faces, field, stencil, *staged),
+        out_specs=[HBM] + [VMEM] * (5 + STAGED),
         scratch=[
             pltpu.SMEM(faces.shape, jnp.int32),
+            pltpu.SMEM(stencil.shape, jnp.float32),
             pltpu.VMEM((2, V, CX, 8, z), jnp.float32),
             pltpu.VMEM((FACES * FACES, SLOT * V, z), jnp.float32),
             pltpu.VMEM(shape, jnp.float32),
-            pltpu.SemaphoreType.DMA((5,)),
+            pltpu.SemaphoreType.DMA((6 + STAGED,)),
             pltpu.SemaphoreType.DMA((PIECES,)),
         ],
     )
@@ -163,56 +183,17 @@
 
 
 def setup_kernel(
-    live_ref,
-    source_hbm,
-    faces_hbm,
-    stencil_hbm,
-    target_hbm,
-    weight_hbm,
-    right_hbm,
-    conductivity_hbm,
-    inverse_hbm,
-    matrix_ref,
-    mask_ref,
-    coefs_ref,
-    right_ref,
-    conductivity_ref,
-    inverse_ref,
-    edge_ref,
-    source_ref,
-    faces_ref,
-    stencil_ref,
-    target_ref,
-    weight_ref,
-    sems,
-):
-    pairs = (
-        (source_hbm, source_ref),
-        (faces_hbm, faces_ref),
-        (stencil_hbm, stencil_ref),
-        (target_hbm, target_ref),
-        (weight_hbm, weight_ref),
-        (right_hbm, right_ref),
-        (conductivity_hbm, conductivity_ref),
-        (inverse_hbm, inverse_ref),
-    )
-    copies = [
-        pltpu.make_async_copy(here, there, sems.at[at]) for at, (here, there) in enumerate(pairs)
-    ]
-    for copy in copies:
-        copy.start()
-    for copy in copies[:5]:
-        copy.wait()
+    live_ref, source_ref, target_ref, weight_ref, inverse_ref, matrix_ref, edge_ref
+):
     entries = target_ref.shape[1]
-    groups = mask_ref.shape[0]
     columns = matrix_ref.shape[1]
+    groups = columns // (SLOT * V)
     row_ids = lax.broadcasted_iota(jnp.int32, (ROWS, entries), 0)
     entry_ids = lax.broadcasted_iota(jnp.int32, (ROWS, entries), 1)
     chosen = (row_ids // V == target_ref[...]) & (entry_ids < live_ref[0, 0])
-    place = lax.broadcasted_iota(jnp.int32, (entries, columns), 0) + SLOT * source_ref[0, 0]
-    place = jnp.where(place >= SLOT * groups, place - SLOT * groups, place)
-    place = SLOT * (groups - 1 - place // SLOT) + lax.rem(place, SLOT)
-    shift = lax.broadcasted_iota(jnp.int32, (entries, columns), 1) - place * V
+    slots = lax.rem(lax.broadcasted_iota(jnp.int32, (1, entries), 1), SLOT)
+    place = SLOT * (groups - 1 - source_ref[...]) + slots
+    shift = lax.broadcasted_iota(jnp.int32, (columns, entries), 0) - place * V
     matrix = jnp.zeros(matrix_ref.shape, jnp.float32)
     for col in range(V):
         spread = jnp.concatenate(
@@ -222,21 +203,13 @@
         high = spread.astype(jnp.bfloat16)
         low = (spread - high.astype(jnp.float32)).astype(jnp.bfloat16)
         order = (shift == col).astype(jnp.float32).astype(jnp.bfloat16)
-        matrix = matrix + jnp.dot(
-            jnp.concatenate([high, low], axis=0), order, preferred_element_type=jnp.float32
+        matrix = matrix + lax.dot_general(
+            jnp.concatenate([high, low], axis=0),
+            order,
+            (((1,), (1,)), ((), ())),
+            preferred_element_type=jnp.float32,
         )
     matrix_ref[...] = matrix.astype(jnp.bfloat16)
-    for direction in range(6):
-        for var in range(V):
-            for col in range(V):
-                coefs_ref[direction, var, col] = jnp.full(
-                    coefs_ref.shape[3:], stencil_ref[var, col, direction], jnp.float32
-                )
-    upper = lax.broadcasted_iota(jnp.int32, mask_ref.shape[1:], 0) < V
-    for group in range(groups):
-        mask_ref[group] = jnp.where(upper, faces_ref[0, group], faces_ref[1, group])
-    for copy in copies[5:]:
-        copy.wait()
     for plane in range(CX):
         for side, row in enumerate(edge_rows(inverse_ref.shape[3])):
             for var in range(V):
@@ -247,24 +220,15 @@
                     )
 
 
-def setup_part(live, source, faces, stencil, target, weight, right, cond, inverse):
-    groups, z = faces.shape[1], right.shape[-1]
-    scalars = [pltpu.SMEM(array.shape, array.dtype) for array in (source, faces, stencil)]
-    vectors = [pltpu.VMEM(array.shape, array.dtype) for array in (target, weight)]
+def setup_part(live, source, target, weight, inverse, groups):
     return call(
         setup_kernel,
         [
             jax.ShapeDtypeStruct((2 * V * ROWS, groups * SLOT * V), jnp.bfloat16),
-            jax.ShapeDtypeStruct((groups, SLOT * V, z), jnp.int32),
-            f32(6, V, V, 8, z),
-            f32(*right.shape),
-            f32(*cond.shape),
-            f32(*inverse.shape),
-            f32(V, CX, 2 * V, z),
+            f32(V, CX, 2 * V, inverse.shape[-1]),
         ],
-        [SMEM] + [HBM] * 8,
-        (live, *in_hbm(source, faces, stencil, target, weight, right, cond, inverse)),
-        scratch=[*scalars, *vectors, pltpu.SemaphoreType.DMA((8,))],
+        [SMEM] + [VMEM] * 4,
+        (live, source, target, weight, inverse),
     )
 
 
@@ -521,18 +485,19 @@
     chip_swap = [(i, i + 1) for i in range(1, count - 1, 2)]
     chip_swap += [(j, i) for i, j in chip_swap]
 
-    send, new, inner, outer = first_part(faces, field)
-    matrix, mask, coefs, right, cond, inverse, edge = setup_part(
-        live_count,
-        coupling_source[0],
+    send, new, inner, outer, mask, coefs, *staged = first_part(
         faces,
+        field,
         coefs,
-        coupling_target[0],
-        weight,
         right,
         cond,
         inverse,
-    )
+        coupling_source[0],
+        coupling_target[0],
+        weight,
+    )
+    right, cond, inverse, source, target, weight = staged
+    matrix, edge = setup_part(live_count, source, target, weight, inverse, faces.shape[1])
     members = [list(reversed(range(lax.axis_size("dom"))))]
     for sweep in range(SWEEPS):
         got = lax.all_to_all(send, "dom", 0, 0, tiled=True, axis_index_groups=members)

time: 74.9 us -> 73.8 us (0.985)
  starting transfers between devices: 59.8 us -> 58.6 us
  waiting for transfers between devices: 5.95 us -> 7.14 us
  Pallas kernels: 7.83 us -> 6.73 us
    all_to_all x3, waiting for transfers between devices: 5.14 us -> 6.32 us  [per_device(): lax.all_to_all(send, 'dom', 0, 0, tiled=True, axis_index_groups=members)]
    all_to_all x3, starting transfers between devices: 37.8 us -> 36.6 us  [per_device(): lax.all_to_all(send, 'dom', 0, 0, tiled=True, axis_index_groups=members)]
    pallas_call x17, Pallas kernels: 7.83 us -> 6.73 us  [call(): pl.pallas_call(kernel, out_shape=out_shape, in_specs=in_specs, out_specs=...]
  transfers between devices with their start and end apart: 9 -> 9, of which waited for: 5 -> 5; matrix products, arithmetic and copies ran while one was open for 0% -> 0% of each run, Pallas kernels for 5% -> 3%
where the time goes in v6:
time: 73.8 us; the launch traced here: 73.3 us
  starting transfers between devices  58.6 us (79%)
  waiting for transfers between devices  7.14 us (10%)
  Pallas kernels  6.73 us (9%)
  between operations  0.85 us (1%)
    all_to_all x3, starting transfers between devices, per_device(): lax.all_to_all(send, 'dom', 0, 0, tiled=True, axis_index_groups=members)  36.6 us
    ppermute x3, starting transfers between devices, per_device(): from_core = lax.ppermute(inner, 'within', core_swap)  16.2 us
    pallas_call x17, Pallas kernels, call(): pl.pallas_call(kernel, out_shape=out_shape, in_specs=in_specs, out_specs=...  6.73 us
    all_to_all x3, waiting for transfers between devices, per_device(): lax.all_to_all(send, 'dom', 0, 0, tiled=True, axis_index_groups=members)  6.32 us
    ppermute x3, starting transfers between devices, per_device(): from_chip = lax.ppermute(outer, 'within', chip_swap)  5.76 us
  transfers between devices with their start and end apart: 9, of which 5 were waited for; matrix products, arithmetic and copies ran while one was open for 0% of the time, Pallas kernels for 3%

profile of v6, /device:TPU:256, one launch (start us, length us, event | category | flops | bytes accessed | tf_op | source)
XLA Modules:
  0.0 73.3 jit_solution(4924745661202761341)
XLA Ops:
  0.0 1.7 %shard_map.100 = (f32[64,8,128]{2,1,0:T(8,128)}, f32[2,8,128]{2,1,0:T(8,128)S(1)}, f32[4,64,128]{2,1,0:T(8,128)S(1)}, f32[4,64,128]{2,1,0:T(8,128)S(1)}, s32[64,...) custom-call(s32[2,64]{1,0:T(2,128)} %bitcast.22, ...), custom_call_target="tpu_custom_call" | custom-call | bytes 524288 | tf_op jit(solution)/shard_map/pallas_call | solution.py:30
  1.7 13.9 %all-to-all-start = ((f32[64,8,128]{2,1,0:T(8,128)}), f32[64,8,128]{2,1,0:T(8,128)S(1)}, u32[]{:S(2)}, u32[]{:S(2)}) async-start(f32[64,8,128]{2,1,0:T(8,128)} %get-tuple-element.65), calls=%async_computation | async-start | bytes 524288 | tf_op jit(solution)/shard_map/all_to_all | solution.py:503
  15.6 1.9 %collective-permute-start.1 = (f32[4,64,128]{2,1,0:T(8,128)S(1)}, f32[4,64,128]{2,1,0:T(8,128)S(1)}, u32[]{:S(2)}, u32[]{:S(2)}) collective-permute-start(f32[4,64,128]{2,1,0:T(8,128)S(1)} %get-tuple-element.58.outer_ref.here_ref), channel_id=1, source_target_pairs={{1,2},{3,4},{5,6},{7,8},{9,10},{11,12},{13,14},{2,1},{4,3},{6,5},{... | collective-permute-start | bytes 393224 | tf_op jit(solution)/shard_map/ppermute | solution.py:505
  17.6 5.3 %collective-permute-start = (f32[4,64,128]{2,1,0:T(8,128)S(1)}, f32[4,64,128]{2,1,0:T(8,128)S(1)}, u32[]{:S(2)}, u32[]{:S(2)}) collective-permute-start(f32[4,64,128]{2,1,0:T(8,128)S(1)} %get-tuple-element.57.inner_ref.here_ref), channel_id=1, source_target_pairs={{0,1},{1,0},{2,3},{3,2},{4,5},{5,4},{6,7},{7,6},{8,9},{9,8},{10,11... | collective-permute-start | bytes 393224 | tf_op jit(solution)/shard_map/ppermute | solution.py:506
  23.5 0.3 shard_map.101
  23.8 0.4 shard_map.103
  24.3 0.0 collective-permute-done.1.outside_ref
  24.3 0.1 shard_map.104
  24.4 0.0 collective-permute-done.outside_ref
  24.4 0.1 shard_map.105
  24.5 1.6 %all-to-all-done.got_ref = f32[64,8,128]{2,1,0:T(8,128)S(1)} async-done(((f32[64,8,128]{2,1,0:T(8,128)}), f32[64,8,128]{2,1,0:T(8,128)S(1)}, u32[]{:S(2)}, u32[]{:S(2)}) %all-to-all-start) | async-done | bytes 262176 | tf_op jit(solution)/shard_map/all_to_all | solution.py:503
  26.1 0.9 %shard_map.106 = (f32[64,8,128]{2,1,0:T(8,128)}, f32[2,8,128]{2,1,0:T(8,128)S(1)}) custom-call(bf16[128,512]{1,0:T(8,128)(2,1)S(1)} %get-tuple-element.51.matrix_ref, f32[4,2,8,128]{3,2,1,0:T(8,128)S(1)} %get-tuple-element.52.edge_ref, f32[2,8,128]{2,1,0:T(8,128)S(1)} %get-tuple-element.64.strips_ref, f32[64,8,128]{2,1,0:T(8,128)S(1)} %all-to-all-done.got_ref, ...), custom_call_target="tpu_custom_call" | custom-call | bytes 524288 | tf_op jit(solution)/shard_map/pallas_call | solution.py:30
  27.1 11.1 %all-to-all-start.1 = ((f32[64,8,128]{2,1,0:T(8,128)}), f32[64,8,128]{2,1,0:T(8,128)S(1)}, u32[]{:S(2)}, u32[]{:S(2)}) async-start(f32[64,8,128]{2,1,0:T(8,128)} %get-tuple-element.76), calls=%async_computation.1 | async-start | bytes 524288 | tf_op jit(solution)/shard_map/all_to_all | solution.py:503
  38.2 1.9 %collective-permute-start.3 = (f32[4,64,128]{2,1,0:T(8,128)S(1)}, f32[4,64,128]{2,1,0:T(8,128)S(1)}, u32[]{:S(2)}, u32[]{:S(2)}) collective-permute-start(f32[4,64,128]{2,1,0:T(8,128)S(1)} %get-tuple-element.71.outer_ref.here_ref), channel_id=1, source_target_pairs={{1,2},{3,4},{5,6},{7,8},{9,10},{11,12},{13,14},{2,1},{4,3},{6,5},{... | collective-permute-start | bytes 393224 | tf_op jit(solution)/shard_map/ppermute | solution.py:505
  40.2 6.5 %collective-permute-start.2 = (f32[4,64,128]{2,1,0:T(8,128)S(1)}, f32[4,64,128]{2,1,0:T(8,128)S(1)}, u32[]{:S(2)}, u32[]{:S(2)}) collective-permute-start(f32[4,64,128]{2,1,0:T(8,128)S(1)} %get-tuple-element.70.inner_ref.here_ref), channel_id=1, source_target_pairs={{0,1},{1,0},{2,3},{3,2},{4,5},{5,4},{6,7},{7,6},{8,9},{9,8},{10,11... | collective-permute-start | bytes 393224 | tf_op jit(solution)/shard_map/ppermute | solution.py:506
  46.7 0.4 shard_map.108
  47.1 0.0 collective-permute-done.3.outside_ref
  47.1 0.1 shard_map.109
  47.2 0.4 collective-permute-done.2.outside_ref
  47.6 0.1 shard_map.110
  47.7 1.2 %all-to-all-done.1.got_ref = f32[64,8,128]{2,1,0:T(8,128)S(1)} async-done(((f32[64,8,128]{2,1,0:T(8,128)}), f32[64,8,128]{2,1,0:T(8,128)S(1)}, u32[]{:S(2)}, u32[]{:S(2)}) %all-to-all-start.1) | async-done | bytes 262176 | tf_op jit(solution)/shard_map/all_to_all | solution.py:503
  48.9 0.9 %shard_map.111 = (f32[64,8,128]{2,1,0:T(8,128)}, f32[2,8,128]{2,1,0:T(8,128)S(1)}) custom-call(bf16[128,512]{1,0:T(8,128)(2,1)S(1)} %get-tuple-element.51.matrix_ref, f32[4,2,8,128]{3,2,1,0:T(8,128)S(1)} %get-tuple-element.52.edge_ref, f32[2,8,128]{2,1,0:T(8,128)S(1)} %get-tuple-element.75.strips_ref, f32[64,8,128]{2,1,0:T(8,128)S(1)} %all-to-all-done.1.got_ref, ...), custom_call_target="tpu_custom_call" | custom-call | bytes 524288 | tf_op jit(solution)/shard_map/pallas_call | solution.py:30
  49.8 11.6 %all-to-all-start.2 = ((f32[64,8,128]{2,1,0:T(8,128)}), f32[64,8,128]{2,1,0:T(8,128)S(1)}, u32[]{:S(2)}, u32[]{:S(2)}) async-start(f32[64,8,128]{2,1,0:T(8,128)} %get-tuple-element.86), calls=%async_computation.2 | async-start | bytes 524288 | tf_op jit(solution)/shard_map/all_to_all | solution.py:503
  61.5 1.9 %collective-permute-start.5 = (f32[4,64,128]{2,1,0:T(8,128)S(1)}, f32[4,64,128]{2,1,0:T(8,128)S(1)}, u32[]{:S(2)}, u32[]{:S(2)}) collective-permute-start(f32[4,64,128]{2,1,0:T(8,128)S(1)} %get-tuple-element.81.outer_ref.here_ref), channel_id=1, source_target_pairs={{1,2},{3,4},{5,6},{7,8},{9,10},{11,12},{13,14},{2,1},{4,3},{6,5},{... | collective-permute-start | bytes 393224 | tf_op jit(solution)/shard_map/ppermute | solution.py:505
  63.4 4.4 %collective-permute-start.4 = (f32[4,64,128]{2,1,0:T(8,128)S(1)}, f32[4,64,128]{2,1,0:T(8,128)S(1)}, u32[]{:S(2)}, u32[]{:S(2)}) collective-permute-start(f32[4,64,128]{2,1,0:T(8,128)S(1)} %get-tuple-element.80.inner_ref.here_ref), channel_id=1, source_target_pairs={{0,1},{1,0},{2,3},{3,2},{4,5},{5,4},{6,7},{7,6},{8,9},{9,8},{10,11... | collective-permute-start | bytes 393224 | tf_op jit(solution)/shard_map/ppermute | solution.py:506
  67.8 0.4 shard_map.113
  68.3 0.0 collective-permute-done.5.outside_ref
  68.3 0.1 shard_map.114
  68.4 0.4 collective-permute-done.4.outside_ref
  68.8 0.1 shard_map.115
  68.9 3.6 %all-to-all-done.2.got_ref = f32[64,8,128]{2,1,0:T(8,128)S(1)} async-done(((f32[64,8,128]{2,1,0:T(8,128)}), f32[64,8,128]{2,1,0:T(8,128)S(1)}, u32[]{:S(2)}, u32[]{:S(2)}) %all-to-all-start.2) | async-done | bytes 262176 | tf_op jit(solution)/shard_map/all_to_all | solution.py:503
  72.5 0.9 %shard_map.116 = f32[4,2,64,128]{3,2,1,0:T(8,128)} custom-call(bf16[128,512]{1,0:T(8,128)(2,1)S(1)} %get-tuple-element.51.matrix_ref, f32[4,2,8,128]{3,2,1,0:T(8,128)S(1)} %get-tuple-element.52.edge_ref, f32[2,8,128]{2,1,0:T(8,128)S(1)} %get-tuple-element.85.strips_ref, f32[64,8,128]{2,1,0:T(8,128)S(1)} %all-to-all-done.2.got_ref, ...), custom_call_target="tpu_custom_call" | custom-call | bytes 524288 | tf_op jit(solution)/shard_map/pallas_call | solution.py:30
  (3 shorter events, 0.1 us)
Async XLA Ops:
  1.7 24.4 %all-to-all-start = ((f32[64,8,128]{2,1,0:T(8,128)}), f32[64,8,128]{2,1,0:T(8,128)S(1)}, u32[]{:S(2)}, u32[]{:S(2)}) async-start(f32[64,8,128]{2,1,0:T(8,128)} %get-tuple-element.65), calls=%async_computation | async-start | bytes 524288 | tf_op jit(solution)/shard_map/all_to_all | solution.py:503
  15.6 8.7 %collective-permute-start.1 = (f32[4,64,128]{2,1,0:T(8,128)S(1)}, f32[4,64,128]{2,1,0:T(8,128)S(1)}, u32[]{:S(2)}, u32[]{:S(2)}) collective-permute-start(f32[4,64,128]{2,1,0:T(8,128)S(1)} %get-tuple-element.58.outer_ref.here_ref), channel_id=1, source_target_pairs={{1,2},{3,4},{5,6},{7,8},{9,10},{11,12},{13,14},{2,1},{4,3},{6,5},{... | collective-permute-start | bytes 393224 | tf_op jit(solution)/shard_map/ppermute | solution.py:505
  17.6 6.8 %collective-permute-start = (f32[4,64,128]{2,1,0:T(8,128)S(1)}, f32[4,64,128]{2,1,0:T(8,128)S(1)}, u32[]{:S(2)}, u32[]{:S(2)}) collective-permute-start(f32[4,64,128]{2,1,0:T(8,128)S(1)} %get-tuple-element.57.inner_ref.here_ref), channel_id=1, source_target_pairs={{0,1},{1,0},{2,3},{3,2},{4,5},{5,4},{6,7},{7,6},{8,9},{9,8},{10,11... | collective-permute-start | bytes 393224 | tf_op jit(solution)/shard_map/ppermute | solution.py:506
  27.1 21.8 %all-to-all-start.1 = ((f32[64,8,128]{2,1,0:T(8,128)}), f32[64,8,128]{2,1,0:T(8,128)S(1)}, u32[]{:S(2)}, u32[]{:S(2)}) async-start(f32[64,8,128]{2,1,0:T(8,128)} %get-tuple-element.76), calls=%async_computation.1 | async-start | bytes 524288 | tf_op jit(solution)/shard_map/all_to_all | solution.py:503
  38.2 8.9 %collective-permute-start.3 = (f32[4,64,128]{2,1,0:T(8,128)S(1)}, f32[4,64,128]{2,1,0:T(8,128)S(1)}, u32[]{:S(2)}, u32[]{:S(2)}) collective-permute-start(f32[4,64,128]{2,1,0:T(8,128)S(1)} %get-tuple-element.71.outer_ref.here_ref), channel_id=1, source_target_pairs={{1,2},{3,4},{5,6},{7,8},{9,10},{11,12},{13,14},{2,1},{4,3},{6,5},{... | collective-permute-start | bytes 393224 | tf_op jit(solution)/shard_map/ppermute | solution.py:505
  40.2 7.5 %collective-permute-start.2 = (f32[4,64,128]{2,1,0:T(8,128)S(1)}, f32[4,64,128]{2,1,0:T(8,128)S(1)}, u32[]{:S(2)}, u32[]{:S(2)}) collective-permute-start(f32[4,64,128]{2,1,0:T(8,128)S(1)} %get-tuple-element.70.inner_ref.here_ref), channel_id=1, source_target_pairs={{0,1},{1,0},{2,3},{3,2},{4,5},{5,4},{6,7},{7,6},{8,9},{9,8},{10,11... | collective-permute-start | bytes 393224 | tf_op jit(solution)/shard_map/ppermute | solution.py:506
  49.8 22.6 %all-to-all-start.2 = ((f32[64,8,128]{2,1,0:T(8,128)}), f32[64,8,128]{2,1,0:T(8,128)S(1)}, u32[]{:S(2)}, u32[]{:S(2)}) async-start(f32[64,8,128]{2,1,0:T(8,128)} %get-tuple-element.86), calls=%async_computation.2 | async-start | bytes 524288 | tf_op jit(solution)/shard_map/all_to_all | solution.py:503
  61.5 6.8 %collective-permute-start.5 = (f32[4,64,128]{2,1,0:T(8,128)S(1)}, f32[4,64,128]{2,1,0:T(8,128)S(1)}, u32[]{:S(2)}, u32[]{:S(2)}) collective-permute-start(f32[4,64,128]{2,1,0:T(8,128)S(1)} %get-tuple-element.81.outer_ref.here_ref), channel_id=1, source_target_pairs={{1,2},{3,4},{5,6},{7,8},{9,10},{11,12},{13,14},{2,1},{4,3},{6,5},{... | collective-permute-start | bytes 393224 | tf_op jit(solution)/shard_map/ppermute | solution.py:505
  63.4 5.4 %collective-permute-start.4 = (f32[4,64,128]{2,1,0:T(8,128)S(1)}, f32[4,64,128]{2,1,0:T(8,128)S(1)}, u32[]{:S(2)}, u32[]{:S(2)}) collective-permute-start(f32[4,64,128]{2,1,0:T(8,128)S(1)} %get-tuple-element.80.inner_ref.here_ref), channel_id=1, source_target_pairs={{0,1},{1,0},{2,3},{3,2},{4,5},{5,4},{6,7},{7,6},{8,9},{9,8},{10,11... | collective-permute-start | bytes 393224 | tf_op jit(solution)/shard_map/ppermute | solution.py:506

commit v7 on v6

--- a/solution.py
+++ b/solution.py
@@ -78,6 +78,7 @@
 
 
 def first_kernel(
+    live_ref,
     faces_hbm,
     field_hbm,
     stencil_hbm,
@@ -85,7 +86,8 @@
 ):
     staged_hbm, refs = refs[:STAGED], refs[STAGED:]
     send_hbm, strips_ref, inner_ref, outer_ref, mask_ref, coefs_ref = refs[:6]
-    staged, refs = refs[6 : 6 + STAGED], refs[6 + STAGED :]
+    matrix_ref, edge_ref = refs[6:8]
+    staged, refs = refs[8 : 8 + STAGED], refs[8 + STAGED :]
     faces, stencil, edges, choices, block, sems, send_sems = refs
     rows = field_hbm.shape[2]
     tile = edges.shape[3]
@@ -130,11 +132,15 @@
                 coefs_ref[direction, var, col] = jnp.full(
                     coefs_ref.shape[3:], stencil[var, col, direction], jnp.float32
                 )
-    for copy in sends + copies[4:]:
+    for copy in copies[4:]:
         copy.wait()
-
-
-def first_part(faces, field, stencil, *staged):
+    _, _, inverse_ref, source_ref, target_ref, weight_ref = staged
+    setup(live_ref, source_ref, target_ref, weight_ref, inverse_ref, matrix_ref, edge_ref)
+    for copy in sends:
+        copy.wait()
+
+
+def first_part(live, faces, field, stencil, *staged):
     groups, (rows, z) = faces.shape[1], field.shape[2:]
     shape = (groups, SLOT * V, z)
     return call(
@@ -146,11 +152,13 @@
             f32(V, rows, z),
             jax.ShapeDtypeStruct(shape, jnp.int32),
             f32(6, V, V, 8, z),
+            jax.ShapeDtypeStruct((2 * V * ROWS, groups * SLOT * V), jnp.bfloat16),
+            f32(V, CX, 2 * V, z),
             *(jax.ShapeDtypeStruct(array.shape, array.dtype) for array in staged),
         ],
-        [HBM] * (3 + STAGED),
-        in_hbm(faces, field, stencil, *staged),
-        out_specs=[HBM] + [VMEM] * (5 + STAGED),
+        [SMEM] + [HBM] * (3 + STAGED),
+        (live, *in_hbm(faces, field, stencil, *staged)),
+        out_specs=[HBM] + [VMEM] * (7 + STAGED),
         scratch=[
             pltpu.SMEM(faces.shape, jnp.int32),
             pltpu.SMEM(stencil.shape, jnp.float32),
@@ -182,7 +190,7 @@
     return call(patch_kernel, [shape, shape], [VMEM] * 3, (strips, inner, outer))
 
 
-def setup_kernel(
+def setup(
     live_ref, source_ref, target_ref, weight_ref, inverse_ref, matrix_ref, edge_ref
 ):
     entries = target_ref.shape[1]
@@ -220,18 +228,6 @@
                     )
 
 
-def setup_part(live, source, target, weight, inverse, groups):
-    return call(
-        setup_kernel,
-        [
-            jax.ShapeDtypeStruct((2 * V * ROWS, groups * SLOT * V), jnp.bfloat16),
-            f32(V, CX, 2 * V, inverse.shape[-1]),
-        ],
-        [SMEM] + [VMEM] * 4,
-        (live, source, target, weight, inverse),
-    )
-
-
 def times(coef, value):
     rows, lanes = value.shape
     return (value.reshape(rows // 8, 8, lanes) * coef).reshape(rows, lanes)
@@ -485,7 +481,8 @@
     chip_swap = [(i, i + 1) for i in range(1, count - 1, 2)]
     chip_swap += [(j, i) for i, j in chip_swap]
 
-    send, new, inner, outer, mask, coefs, *staged = first_part(
+    send, new, inner, outer, mask, coefs, matrix, edge, *staged = first_part(
+        live_count,
         faces,
         field,
         coefs,
@@ -496,8 +493,7 @@
         coupling_target[0],
         weight,
     )
-    right, cond, inverse, source, target, weight = staged
-    matrix, edge = setup_part(live_count, source, target, weight, inverse, faces.shape[1])
+    right, cond, inverse = staged[:3]
     members = [list(reversed(range(lax.axis_size("dom"))))]
     for sweep in range(SWEEPS):
         got = lax.all_to_all(send, "dom", 0, 0, tiled=True, axis_index_groups=members)

time: 73.8 us -> 74.8 us (1.014)
  waiting for transfers between devices: 7.14 us -> 8.17 us
    all_to_all x3, starting transfers between devices: 36.6 us -> 35.7 us  [per_device(): lax.all_to_all(send, 'dom', 0, 0, tiled=True, axis_index_groups=members)]
    pallas_call x17 -> x16, Pallas kernels: 6.73 us -> 7.35 us  [call(): pl.pallas_call(kernel, out_shape=out_shape, in_specs=in_specs, out_specs=...]
  transfers between devices with their start and end apart: 9 -> 9, of which waited for: 5 -> 6; matrix products, arithmetic and copies ran while one was open for 0% -> 0% of each run, Pallas kernels for 3% -> 3%
where the time goes in v7:
time: 74.8 us; the launch traced here: 74.3 us
  starting transfers between devices  58 us (78%)
  waiting for transfers between devices  8.17 us (11%)
  Pallas kernels  7.35 us (10%)
  between operations  0.84 us (1%)
    all_to_all x3, starting transfers between devices, per_device(): lax.all_to_all(send, 'dom', 0, 0, tiled=True, axis_index_groups=members)  35.7 us
    ppermute x3, starting transfers between devices, per_device(): from_core = lax.ppermute(inner, 'within', core_swap)  16.5 us
    pallas_call x16, Pallas kernels, call(): pl.pallas_call(kernel, out_shape=out_shape, in_specs=in_specs, out_specs=...  7.35 us
    all_to_all x3, waiting for transfers between devices, per_device(): lax.all_to_all(send, 'dom', 0, 0, tiled=True, axis_index_groups=members)  6.95 us
    ppermute x3, starting transfers between devices, per_device(): from_chip = lax.ppermute(outer, 'within', chip_swap)  5.76 us
  transfers between devices with their start and end apart: 9, of which 6 were waited for; matrix products, arithmetic and copies ran while one was open for 0% of the time, Pallas kernels for 3%

profile of v7, /device:TPU:256, one launch (start us, length us, event | category | flops | bytes accessed | tf_op | source)
XLA Modules:
  0.0 74.3 jit_solution(14394851759505649781)
XLA Ops:
  0.7 2.6 %shard_map.100 = (f32[64,8,128]{2,1,0:T(8,128)}, f32[2,8,128]{2,1,0:T(8,128)S(1)}, f32[4,64,128]{2,1,0:T(8,128)S(1)}, f32[4,64,128]{2,1,0:T(8,128)S(1)}, s32[64,...) custom-call(s32[1,1]{1,0:T(1,128)S(6)} %copy.11.live_ref, ...), custom_call_target="tpu_custom_call" | custom-call | bytes 524288 | tf_op jit(solution)/shard_map/pallas_call | solution.py:30
  3.3 13.9 %all-to-all-start = ((f32[64,8,128]{2,1,0:T(8,128)}), f32[64,8,128]{2,1,0:T(8,128)S(1)}, u32[]{:S(2)}, u32[]{:S(2)}) async-start(f32[64,8,128]{2,1,0:T(8,128)} %get-tuple-element.59), calls=%async_computation | async-start | bytes 524288 | tf_op jit(solution)/shard_map/all_to_all | solution.py:499
  17.2 1.9 %collective-permute-start.1 = (f32[4,64,128]{2,1,0:T(8,128)S(1)}, f32[4,64,128]{2,1,0:T(8,128)S(1)}, u32[]{:S(2)}, u32[]{:S(2)}) collective-permute-start(f32[4,64,128]{2,1,0:T(8,128)S(1)} %get-tuple-element.51.outer_ref.here_ref), channel_id=1, source_target_pairs={{1,2},{3,4},{5,6},{7,8},{9,10},{11,12},{13,14},{2,1},{4,3},{6,5},{... | collective-permute-start | bytes 393224 | tf_op jit(solution)/shard_map/ppermute | solution.py:501
  19.2 5.3 %collective-permute-start = (f32[4,64,128]{2,1,0:T(8,128)S(1)}, f32[4,64,128]{2,1,0:T(8,128)S(1)}, u32[]{:S(2)}, u32[]{:S(2)}) collective-permute-start(f32[4,64,128]{2,1,0:T(8,128)S(1)} %get-tuple-element.50.inner_ref.here_ref), channel_id=1, source_target_pairs={{0,1},{1,0},{2,3},{3,2},{4,5},{5,4},{6,7},{7,6},{8,9},{9,8},{10,11... | collective-permute-start | bytes 393224 | tf_op jit(solution)/shard_map/ppermute | solution.py:502
  24.5 0.4 shard_map.102
  24.9 0.0 collective-permute-done.1.outside_ref
  24.9 0.1 shard_map.103
  25.0 0.4 collective-permute-done.outside_ref
  25.4 0.1 shard_map.104
  25.5 2.2 %all-to-all-done.got_ref = f32[64,8,128]{2,1,0:T(8,128)S(1)} async-done(((f32[64,8,128]{2,1,0:T(8,128)}), f32[64,8,128]{2,1,0:T(8,128)S(1)}, u32[]{:S(2)}, u32[]{:S(2)}) %all-to-all-start) | async-done | bytes 262176 | tf_op jit(solution)/shard_map/all_to_all | solution.py:499
  27.7 0.9 %shard_map.105 = (f32[64,8,128]{2,1,0:T(8,128)}, f32[2,8,128]{2,1,0:T(8,128)S(1)}) custom-call(bf16[128,512]{1,0:T(8,128)(2,1)S(1)} %get-tuple-element.44.matrix_ref, f32[4,2,8,128]{3,2,1,0:T(8,128)S(1)} %get-tuple-element.45.edge_ref, f32[2,8,128]{2,1,0:T(8,128)S(1)} %get-tuple-element.58.strips_ref, f32[64,8,128]{2,1,0:T(8,128)S(1)} %all-to-all-done.got_ref, ...), custom_call_target="tpu_custom_call" | custom-call | bytes 524288 | tf_op jit(solution)/shard_map/pallas_call | solution.py:30
  28.7 10.6 %all-to-all-start.1 = ((f32[64,8,128]{2,1,0:T(8,128)}), f32[64,8,128]{2,1,0:T(8,128)S(1)}, u32[]{:S(2)}, u32[]{:S(2)}) async-start(f32[64,8,128]{2,1,0:T(8,128)} %get-tuple-element.70), calls=%async_computation.1 | async-start | bytes 524288 | tf_op jit(solution)/shard_map/all_to_all | solution.py:499
  39.3 1.9 %collective-permute-start.3 = (f32[4,64,128]{2,1,0:T(8,128)S(1)}, f32[4,64,128]{2,1,0:T(8,128)S(1)}, u32[]{:S(2)}, u32[]{:S(2)}) collective-permute-start(f32[4,64,128]{2,1,0:T(8,128)S(1)} %get-tuple-element.65.outer_ref.here_ref), channel_id=1, source_target_pairs={{1,2},{3,4},{5,6},{7,8},{9,10},{11,12},{13,14},{2,1},{4,3},{6,5},{... | collective-permute-start | bytes 393224 | tf_op jit(solution)/shard_map/ppermute | solution.py:501
  41.2 6.5 %collective-permute-start.2 = (f32[4,64,128]{2,1,0:T(8,128)S(1)}, f32[4,64,128]{2,1,0:T(8,128)S(1)}, u32[]{:S(2)}, u32[]{:S(2)}) collective-permute-start(f32[4,64,128]{2,1,0:T(8,128)S(1)} %get-tuple-element.64.inner_ref.here_ref), channel_id=1, source_target_pairs={{0,1},{1,0},{2,3},{3,2},{4,5},{5,4},{6,7},{7,6},{8,9},{9,8},{10,11... | collective-permute-start | bytes 393224 | tf_op jit(solution)/shard_map/ppermute | solution.py:502
  47.7 0.4 shard_map.107
  48.1 0.0 collective-permute-done.3.outside_ref
  48.2 0.1 shard_map.108
  48.3 0.4 collective-permute-done.2.outside_ref
  48.7 0.1 shard_map.109
  48.8 1.5 %all-to-all-done.1.got_ref = f32[64,8,128]{2,1,0:T(8,128)S(1)} async-done(((f32[64,8,128]{2,1,0:T(8,128)}), f32[64,8,128]{2,1,0:T(8,128)S(1)}, u32[]{:S(2)}, u32[]{:S(2)}) %all-to-all-start.1) | async-done | bytes 262176 | tf_op jit(solution)/shard_map/all_to_all | solution.py:499
  50.2 0.9 %shard_map.110 = (f32[64,8,128]{2,1,0:T(8,128)}, f32[2,8,128]{2,1,0:T(8,128)S(1)}) custom-call(bf16[128,512]{1,0:T(8,128)(2,1)S(1)} %get-tuple-element.44.matrix_ref, f32[4,2,8,128]{3,2,1,0:T(8,128)S(1)} %get-tuple-element.45.edge_ref, f32[2,8,128]{2,1,0:T(8,128)S(1)} %get-tuple-element.69.strips_ref, f32[64,8,128]{2,1,0:T(8,128)S(1)} %all-to-all-done.1.got_ref, ...), custom_call_target="tpu_custom_call" | custom-call | bytes 524288 | tf_op jit(solution)/shard_map/pallas_call | solution.py:30
  51.2 11.3 %all-to-all-start.2 = ((f32[64,8,128]{2,1,0:T(8,128)}), f32[64,8,128]{2,1,0:T(8,128)S(1)}, u32[]{:S(2)}, u32[]{:S(2)}) async-start(f32[64,8,128]{2,1,0:T(8,128)} %get-tuple-element.80), calls=%async_computation.2 | async-start | bytes 524288 | tf_op jit(solution)/shard_map/all_to_all | solution.py:499
  62.5 1.9 %collective-permute-start.5 = (f32[4,64,128]{2,1,0:T(8,128)S(1)}, f32[4,64,128]{2,1,0:T(8,128)S(1)}, u32[]{:S(2)}, u32[]{:S(2)}) collective-permute-start(f32[4,64,128]{2,1,0:T(8,128)S(1)} %get-tuple-element.75.outer_ref.here_ref), channel_id=1, source_target_pairs={{1,2},{3,4},{5,6},{7,8},{9,10},{11,12},{13,14},{2,1},{4,3},{6,5},{... | collective-permute-start | bytes 393224 | tf_op jit(solution)/shard_map/ppermute | solution.py:501
  64.4 4.7 %collective-permute-start.4 = (f32[4,64,128]{2,1,0:T(8,128)S(1)}, f32[4,64,128]{2,1,0:T(8,128)S(1)}, u32[]{:S(2)}, u32[]{:S(2)}) collective-permute-start(f32[4,64,128]{2,1,0:T(8,128)S(1)} %get-tuple-element.74.inner_ref.here_ref), channel_id=1, source_target_pairs={{0,1},{1,0},{2,3},{3,2},{4,5},{5,4},{6,7},{7,6},{8,9},{9,8},{10,11... | collective-permute-start | bytes 393224 | tf_op jit(solution)/shard_map/ppermute | solution.py:502
  69.1 0.4 shard_map.112
  69.6 0.0 collective-permute-done.5.outside_ref
  69.6 0.1 shard_map.113
  69.7 0.4 collective-permute-done.4.outside_ref
  70.1 0.1 shard_map.114
  70.2 3.3 %all-to-all-done.2.got_ref = f32[64,8,128]{2,1,0:T(8,128)S(1)} async-done(((f32[64,8,128]{2,1,0:T(8,128)}), f32[64,8,128]{2,1,0:T(8,128)S(1)}, u32[]{:S(2)}, u32[]{:S(2)}) %all-to-all-start.2) | async-done | bytes 262176 | tf_op jit(solution)/shard_map/all_to_all | solution.py:499
  73.5 0.9 %shard_map.115 = f32[4,2,64,128]{3,2,1,0:T(8,128)} custom-call(bf16[128,512]{1,0:T(8,128)(2,1)S(1)} %get-tuple-element.44.matrix_ref, f32[4,2,8,128]{3,2,1,0:T(8,128)S(1)} %get-tuple-element.45.edge_ref, f32[2,8,128]{2,1,0:T(8,128)S(1)} %get-tuple-element.79.strips_ref, f32[64,8,128]{2,1,0:T(8,128)S(1)} %all-to-all-done.2.got_ref, ...), custom_call_target="tpu_custom_call" | custom-call | bytes 524288 | tf_op jit(solution)/shard_map/pallas_call | solution.py:30
  (3 shorter events, 0.1 us)
Async XLA Ops:
  3.3 24.4 %all-to-all-start = ((f32[64,8,128]{2,1,0:T(8,128)}), f32[64,8,128]{2,1,0:T(8,128)S(1)}, u32[]{:S(2)}, u32[]{:S(2)}) async-start(f32[64,8,128]{2,1,0:T(8,128)} %get-tuple-element.59), calls=%async_computation | async-start | bytes 524288 | tf_op jit(solution)/shard_map/all_to_all | solution.py:499
  17.2 7.7 %collective-permute-start.1 = (f32[4,64,128]{2,1,0:T(8,128)S(1)}, f32[4,64,128]{2,1,0:T(8,128)S(1)}, u32[]{:S(2)}, u32[]{:S(2)}) collective-permute-start(f32[4,64,128]{2,1,0:T(8,128)S(1)} %get-tuple-element.51.outer_ref.here_ref), channel_id=1, source_target_pairs={{1,2},{3,4},{5,6},{7,8},{9,10},{11,12},{13,14},{2,1},{4,3},{6,5},{... | collective-permute-start | bytes 393224 | tf_op jit(solution)/shard_map/ppermute | solution.py:501
  19.2 6.3 %collective-permute-start = (f32[4,64,128]{2,1,0:T(8,128)S(1)}, f32[4,64,128]{2,1,0:T(8,128)S(1)}, u32[]{:S(2)}, u32[]{:S(2)}) collective-permute-start(f32[4,64,128]{2,1,0:T(8,128)S(1)} %get-tuple-element.50.inner_ref.here_ref), channel_id=1, source_target_pairs={{0,1},{1,0},{2,3},{3,2},{4,5},{5,4},{6,7},{7,6},{8,9},{9,8},{10,11... | collective-permute-start | bytes 393224 | tf_op jit(solution)/shard_map/ppermute | solution.py:502
  28.7 21.6 %all-to-all-start.1 = ((f32[64,8,128]{2,1,0:T(8,128)}), f32[64,8,128]{2,1,0:T(8,128)S(1)}, u32[]{:S(2)}, u32[]{:S(2)}) async-start(f32[64,8,128]{2,1,0:T(8,128)} %get-tuple-element.70), calls=%async_computation.1 | async-start | bytes 524288 | tf_op jit(solution)/shard_map/all_to_all | solution.py:499
  39.3 8.9 %collective-permute-start.3 = (f32[4,64,128]{2,1,0:T(8,128)S(1)}, f32[4,64,128]{2,1,0:T(8,128)S(1)}, u32[]{:S(2)}, u32[]{:S(2)}) collective-permute-start(f32[4,64,128]{2,1,0:T(8,128)S(1)} %get-tuple-element.65.outer_ref.here_ref), channel_id=1, source_target_pairs={{1,2},{3,4},{5,6},{7,8},{9,10},{11,12},{13,14},{2,1},{4,3},{6,5},{... | collective-permute-start | bytes 393224 | tf_op jit(solution)/shard_map/ppermute | solution.py:501
  41.2 7.5 %collective-permute-start.2 = (f32[4,64,128]{2,1,0:T(8,128)S(1)}, f32[4,64,128]{2,1,0:T(8,128)S(1)}, u32[]{:S(2)}, u32[]{:S(2)}) collective-permute-start(f32[4,64,128]{2,1,0:T(8,128)S(1)} %get-tuple-element.64.inner_ref.here_ref), channel_id=1, source_target_pairs={{0,1},{1,0},{2,3},{3,2},{4,5},{5,4},{6,7},{7,6},{8,9},{9,8},{10,11... | collective-permute-start | bytes 393224 | tf_op jit(solution)/shard_map/ppermute | solution.py:502
  51.2 22.3 %all-to-all-start.2 = ((f32[64,8,128]{2,1,0:T(8,128)}), f32[64,8,128]{2,1,0:T(8,128)S(1)}, u32[]{:S(2)}, u32[]{:S(2)}) async-start(f32[64,8,128]{2,1,0:T(8,128)} %get-tuple-element.80), calls=%async_computation.2 | async-start | bytes 524288 | tf_op jit(solution)/shard_map/all_to_all | solution.py:499
  62.5 7.1 %collective-permute-start.5 = (f32[4,64,128]{2,1,0:T(8,128)S(1)}, f32[4,64,128]{2,1,0:T(8,128)S(1)}, u32[]{:S(2)}, u32[]{:S(2)}) collective-permute-start(f32[4,64,128]{2,1,0:T(8,128)S(1)} %get-tuple-element.75.outer_ref.here_ref), channel_id=1, source_target_pairs={{1,2},{3,4},{5,6},{7,8},{9,10},{11,12},{13,14},{2,1},{4,3},{6,5},{... | collective-permute-start | bytes 393224 | tf_op jit(solution)/shard_map/ppermute | solution.py:501
  64.4 5.7 %collective-permute-start.4 = (f32[4,64,128]{2,1,0:T(8,128)S(1)}, f32[4,64,128]{2,1,0:T(8,128)S(1)}, u32[]{:S(2)}, u32[]{:S(2)}) collective-permute-start(f32[4,64,128]{2,1,0:T(8,128)S(1)} %get-tuple-element.74.inner_ref.here_ref), channel_id=1, source_target_pairs={{0,1},{1,0},{2,3},{3,2},{4,5},{5,4},{6,7},{7,6},{8,9},{9,8},{10,11... | collective-permute-start | bytes 393224 | tf_op jit(solution)/shard_map/ppermute | solution.py:502
